TPU v7x, 32 devices: a whole 2x2x4 slice. The times are simulated.
32 devices in a mesh: segment: 2 (over core), dp: 16 (over z, y, x).
Axes of the slice: x: 2, y: 2, z: 4, core: 2. Of those that a mesh axis runs over, the one named last changes fastest.
Arguments:
- inputs: bfloat16 [2, 96, 197, 384], P(None, 'dp'), may hold values from -6 to 6
- image_count: int32 [2, 16], P(None, 'dp'), may hold values from 1 to 6, as said below
- cotangent: bfloat16 [2, 96, 197, 384], P(None, 'dp'), may hold values from -6 to 6
- ln1_gain: float32 [2, 384], P('segment'), may hold values from 0.1 to 1.9
- ln1_bias: float32 [2, 384], P('segment'), may hold values from -3 to 3
- w_qkv: bfloat16 [2, 384, 1152], P('segment'), may hold values from -0.4375 to 0.4375
- bias_qv: float32 [2, 768], P('segment'), may hold values from -3 to 3
- w_out: bfloat16 [2, 384, 384], P('segment'), may hold values from -0.625 to 0.625
- b_out: float32 [2, 384], P('segment'), may hold values from -3 to 3
- ln2_gain: float32 [2, 384], P('segment'), may hold values from 0.1 to 1.9
- ln2_bias: float32 [2, 384], P('segment'), may hold values from -3 to 3
- w_up: bfloat16 [2, 384, 1536], P('segment'), may hold values from -0.3125 to 0.3125
- b_up: float32 [2, 1536], P('segment'), may hold values from -4 to 4
- w_down: bfloat16 [2, 1536, 384], P('segment'), may hold values from -0.21875 to 0.21875
- b_down: float32 [2, 384], P('segment'), may hold values from -3 to 3
Outputs:
- activations: bfloat16 [2, 2, 96, 197, 384], P('segment', None, 'dp')
- input_grads: bfloat16 [2, 2, 96, 197, 384], P('segment', None, 'dp')
- ln1_gain_grad: float32 [2, 384], P('segment', 'dp')
- ln1_bias_grad: float32 [2, 384], P('segment', 'dp')
- w_qkv_grad: float32 [2, 384, 1152], P('segment', 'dp')
- bias_qv_grad: float32 [2, 768], P('segment', 'dp')
- w_out_grad: float32 [2, 384, 384], P('segment', 'dp')
- b_out_grad: float32 [2, 384], P('segment', 'dp')
- ln2_gain_grad: float32 [2, 384], P('segment', 'dp')
- ln2_bias_grad: float32 [2, 384], P('segment', 'dp')
- w_up_grad: float32 [2, 384, 1536], P('segment', 'dp')
- b_up_grad: float32 [2, 1536], P('segment', 'dp')
- w_down_grad: float32 [2, 1536, 384], P('segment', 'dp')
- b_down_grad: float32 [2, 384], P('segment', 'dp')
Inputs may be any that keep to these rules, and one draw needn't show every extreme that they name: Images of micro-batch m held by data rank r fill its slots below image_count[m, r]; higher slots hold no image. In each micro-batch some rank holds 6.
All inputs are finite; a program needn't handle non-finite values.
Results may differ from a plain program's by a relative error of at most 0.02.
The roundings to bfloat16 on the way count: a program that leaves them out, or rounds other values in their place, can miss the bound.
Values may be sent and summed in bfloat16 or wider, within the bound.
No kernel may reach another device: no remote copies, remote signals or barrier semaphores. Data moves between devices by JAX's collectives and lax.ppermute only.
A program may use at most 192 MiB of HBM per device.

v0:
```python
import jax
import jax.numpy as jnp
from jax import lax
from jax.sharding import PartitionSpec as P

HEAD = 64


epsilon = 1e-06


def from_behind(block, axis, distance):
    devices = range(lax.axis_size(axis))
    route = [(i - distance, i) for i in devices if i - distance in devices]
    return lax.ppermute(block, axis, route)


def norm_rows(rows, gain, shift):
    centered = rows - jnp.mean(rows, axis=-1, keepdims=True)
    spread = jnp.mean(centered * centered, axis=-1, keepdims=True)
    return centered * lax.rsqrt(spread + epsilon) * gain + shift


def gelu_exact(values):
    return jax.nn.gelu(values, approximate=False)


def split_heads(joined, head_size):
    images, tokens, columns = joined.shape
    return joined.reshape(images, tokens, 3, columns // (3 * head_size), head_size)


def forward(params, hidden, head_size):
    (
        ln1_gain,
        ln1_bias,
        w_qkv,
        bias_qv,
        w_out,
        b_out,
        ln2_gain,
        ln2_bias,
        w_up,
        b_up,
        w_down,
        b_down,
    ) = params
    images, tokens, features = hidden.shape
    normed = norm_rows(hidden, ln1_gain, ln1_bias).astype(jnp.bfloat16)
    bias_full = jnp.concatenate(
        [bias_qv[:features], jnp.zeros((features,), jnp.float32), bias_qv[features:]]
    )
    joined = (
        jnp.einsum("nsd,de->nse", normed, w_qkv, preferred_element_type=jnp.float32) + bias_full
    )
    joined = joined.astype(jnp.bfloat16)
    parts = split_heads(joined, head_size)
    scores = jnp.einsum(
        "nqhc,nkhc->nhqk", parts[:, :, 0], parts[:, :, 1], preferred_element_type=jnp.float32
    ) * head_size ** (-0.5)
    highest_score = jnp.max(scores, axis=-1, keepdims=True)
    log_total = highest_score + jnp.log(
        jnp.sum(jnp.exp(scores - highest_score), axis=-1, keepdims=True)
    )
    probs = jnp.exp(scores - log_total).astype(jnp.bfloat16)
    attended = jnp.einsum(
        "nhqk,nkhc->nqhc", probs, parts[:, :, 2], preferred_element_type=jnp.float32
    )
    attended = attended.reshape(images, tokens, features).astype(jnp.bfloat16)
    middle = (
        hidden
        + jnp.einsum("nsd,de->nse", attended, w_out, preferred_element_type=jnp.float32)
        + b_out
    )
    second_norm = norm_rows(middle, ln2_gain, ln2_bias).astype(jnp.bfloat16)
    before = jnp.einsum("nsd,df->nsf", second_norm, w_up, preferred_element_type=jnp.float32) + b_up
    active = gelu_exact(before).astype(jnp.bfloat16)
    output = (
        middle
        + jnp.einsum("nsf,fd->nsd", active, w_down, preferred_element_type=jnp.float32)
        + b_down
    )
    return (
        output,
        (hidden, normed, joined, log_total, attended, middle, second_norm, before, active),
    )


def backward(params, saved, grad_out, head_size):
    (
        ln1_gain,
        ln1_bias,
        w_qkv,
        bias_qv,
        w_out,
        b_out,
        ln2_gain,
        ln2_bias,
        w_up,
        b_up,
        w_down,
        b_down,
    ) = params
    hidden, normed, joined, log_total, attended, middle, second_norm, before, active = saved
    images, tokens, features = hidden.shape
    scale = head_size ** (-0.5)
    down_in = grad_out.astype(jnp.bfloat16)
    g_down = jnp.einsum("nsf,nsd->fd", active, down_in, preferred_element_type=jnp.float32)
    g_bdown = jnp.sum(down_in.astype(jnp.float32), axis=(0, 1))
    grad_active = jnp.einsum("nsd,fd->nsf", down_in, w_down, preferred_element_type=jnp.float32)
    grad_before = jax.vjp(gelu_exact, before)[1](grad_active)[0].astype(jnp.bfloat16)
    g_up = jnp.einsum("nsd,nsf->df", second_norm, grad_before, preferred_element_type=jnp.float32)
    g_bup = jnp.sum(grad_before.astype(jnp.float32), axis=(0, 1))
    grad_norm_two = jnp.einsum("nsf,df->nsd", grad_before, w_up, preferred_element_type=jnp.float32)
    grad_middle, g_gain_two, g_bias_two = jax.vjp(norm_rows, middle, ln2_gain, ln2_bias)[1](
        grad_norm_two
    )
    grad_middle = grad_out + grad_middle
    out_in = grad_middle.astype(jnp.bfloat16)
    g_out = jnp.einsum("nsd,nse->de", attended, out_in, preferred_element_type=jnp.float32)
    g_bout = jnp.sum(out_in.astype(jnp.float32), axis=(0, 1))
    grad_attended = jnp.einsum("nse,de->nsd", out_in, w_out, preferred_element_type=jnp.float32)
    grad_attended = grad_attended.astype(jnp.bfloat16).reshape(
        images, tokens, features // head_size, head_size
    )
    parts = split_heads(joined, head_size)
    scores = (
        jnp.einsum(
            "nqhc,nkhc->nhqk", parts[:, :, 0], parts[:, :, 1], preferred_element_type=jnp.float32
        )
        * scale
    )
    probs = jnp.exp(scores - log_total)
    grad_value = jnp.einsum(
        "nhqk,nqhc->nkhc",
        probs.astype(jnp.bfloat16),
        grad_attended,
        preferred_element_type=jnp.float32,
    )
    grad_probs = jnp.einsum(
        "nqhc,nkhc->nhqk", grad_attended, parts[:, :, 2], preferred_element_type=jnp.float32
    )
    grad_scores = probs * (grad_probs - jnp.sum(probs * grad_probs, axis=-1, keepdims=True))
    grad_scores = grad_scores.astype(jnp.bfloat16)
    grad_query = (
        jnp.einsum(
            "nhqk,nkhc->nqhc", grad_scores, parts[:, :, 1], preferred_element_type=jnp.float32
        )
        * scale
    )
    grad_key = (
        jnp.einsum(
            "nhqk,nqhc->nkhc", grad_scores, parts[:, :, 0], preferred_element_type=jnp.float32
        )
        * scale
    )
    grad_joined = jnp.stack([grad_query, grad_key, grad_value], axis=2).reshape(
        images, tokens, 3 * features
    )
    grad_joined = grad_joined.astype(jnp.bfloat16)
    g_qkv = jnp.einsum("nsd,nse->de", normed, grad_joined, preferred_element_type=jnp.float32)
    joined_sums = jnp.sum(grad_joined.astype(jnp.float32), axis=(0, 1))
    g_bqv = jnp.concatenate([joined_sums[:features], joined_sums[2 * features :]])
    grad_normed = jnp.einsum("nse,de->nsd", grad_joined, w_qkv, preferred_element_type=jnp.float32)
    grad_hidden, g_gain_one, g_bias_one = jax.vjp(norm_rows, hidden, ln1_gain, ln1_bias)[1](
        grad_normed
    )
    grad_hidden = grad_middle + grad_hidden
    grads = (
        g_gain_one,
        g_bias_one,
        g_qkv,
        g_bqv,
        g_out,
        g_bout,
        g_gain_two,
        g_bias_two,
        g_up,
        g_bup,
        g_down,
        g_bdown,
    )
    return (grad_hidden, grads)


def on_device(
    inputs,
    image_count,
    cotangent,
    ln1_gain,
    ln1_bias,
    w_qkv,
    bias_qv,
    w_out,
    b_out,
    ln2_gain,
    ln2_bias,
    w_up,
    b_up,
    w_down,
    b_down,
):
    micro = inputs.shape[0]
    slots = inputs.shape[1]
    slot_ids = jnp.arange(slots, dtype=jnp.int32)
    masks = (slot_ids[None, :] < image_count).astype(jnp.float32)[:, :, None, None]
    params = tuple(
        (
            arg[0]
            for arg in (
                ln1_gain,
                ln1_bias,
                w_qkv,
                bias_qv,
                w_out,
                b_out,
                ln2_gain,
                ln2_bias,
                w_up,
                b_up,
                w_down,
                b_down,
            )
        )
    )
    first = lax.axis_index("segment") == 0

    def batch_mask(which):
        return lax.dynamic_index_in_dim(
            masks, jnp.clip(which, 0, micro - 1).astype(jnp.int32), 0, keepdims=False
        )

    received = jnp.zeros(inputs.shape[1:], jnp.bfloat16)
    outputs = []
    stored = []
    for tick in range(micro + 1):
        source = jnp.where(first, inputs[min(tick, micro - 1)], received).astype(jnp.float32)
        mask = batch_mask(jnp.where(first, tick, tick - 1))
        result, saved = forward(params, source, HEAD)
        sent = (result * mask).astype(jnp.bfloat16)
        outputs.append(sent)
        stored.append(saved)
        if tick < micro:
            received = from_behind(sent, "segment", 1)
    returned = jnp.zeros(inputs.shape[1:], jnp.bfloat16)
    totals = None
    in_grads = []
    for tick in range(micro + 1):
        lower = stored[max(tick - 1, 0)]
        upper = stored[min(tick + 1, micro)]
        picked = jax.tree.map(lambda former, latter: jnp.where(first, former, latter), lower, upper)
        active_flag = jnp.where(first, tick >= 1, tick < micro).astype(jnp.float32)
        mask = batch_mask(jnp.where(first, tick - 1, tick)) * active_flag
        incoming = (
            jnp.where(first, returned, cotangent[min(tick, micro - 1)]).astype(jnp.float32) * mask
        )
        grad_hidden, grads = backward(params, picked, incoming, HEAD)
        going = grad_hidden.astype(jnp.bfloat16)
        in_grads.append(going)
        if tick < micro:
            returned = from_behind(going, "segment", -1)
        if totals is None:
            totals = grads
        else:
            totals = tuple((former + latter for former, latter in zip(totals, grads)))
    totals = lax.psum_scatter(totals, "dp", scatter_dimension=0, tiled=True)
    activations = jnp.stack(
        [jnp.where(first, outputs[batch], outputs[batch + 1]) for batch in range(micro)]
    )[None]
    input_grads = jnp.stack(
        [jnp.where(first, in_grads[batch + 1], in_grads[batch]) for batch in range(micro)]
    )[None]
    shards = tuple((total[None] for total in totals))
    return (activations, input_grads) + shards


def solution(mesh):
    in_specs = (
        P(None, "dp", None, None),
        P(None, "dp"),
        P(None, "dp", None, None),
        P("segment", None),
        P("segment", None),
        P("segment", None, None),
        P("segment", None),
        P("segment", None, None),
        P("segment", None),
        P("segment", None),
        P("segment", None),
        P("segment", None, None),
        P("segment", None),
        P("segment", None, None),
        P("segment", None),
    )
    out_specs = (
        P("segment", None, "dp", None, None),
        P("segment", None, "dp", None, None),
        P("segment", "dp"),
        P("segment", "dp"),
        P("segment", "dp", None),
        P("segment", "dp"),
        P("segment", "dp", None),
        P("segment", "dp"),
        P("segment", "dp"),
        P("segment", "dp"),
        P("segment", "dp", None),
        P("segment", "dp"),
        P("segment", "dp", None),
        P("segment", "dp"),
    )
    return jax.shard_map(
        on_device, mesh=mesh, in_specs=in_specs, out_specs=out_specs, check_vma=False
    )
```

profile of v0, /device:TPU:0, one launch (start us, length us, event | category | flops | bytes accessed | tf_op | source)
XLA Modules:
  0.0 878.3 jit_solution(6661280061818050668)
XLA Ops:
  7.3 6.5 fusion.291
  18.3 5.6 copy.138
  42.3 17.1 %fusion.2 = bf16[6,197,1536]{2,1,0:T(8,128)(2,1)S(1)} fusion(f32[6,197,1536]{2,1,0:T(8,128)S(1)} %get-tuple-element.178, f32[1536]{0:T(1024)S(1)} %reduce.11, u8[197,1536]{1,0:T(8,128)(4,1)S(1)} %get-tuple-element.61, u8[197,1536]{1,0:T(8,128)(4,1)S(1)} %get-tuple-element.60), kind=kLoop, calls=%fused_computation.8 | loop fusion | flops 128904192 | bytes 11504640 | tf_op jit(solution)/shard_map/convert_element_type | solution.py:77
  72.0 4.2 broadcast_select_fusion.2
  76.2 5.5 copy.145
  91.5 4.8 fusion.152
  96.9 21.4 %convert_reduce_fusion.2 = (f32[1536]{0:T(1024)}, bf16[6,197,1536]{2,1,0:T(8,128)(2,1)S(1)}) fusion(bf16[1,1536,384]{2,1,0:T(8,128)(2,1)S(1)} %copy-done.147, bf16[1,6,197,384]{3,2,1,0:T(8,128)(2,1)S(1)} %copy-done.55, f32[6]{0:T(128)S(1)} %get-tuple-element.170, f32[6,197,1536]{2,1,0:T(8,128)S(1)} %get-tuple-element.183, ...), kind=kOutput, calls=%fused_computation.45 | convolution fusion | flops 1535501568 | bytes 20255256 | tf_op jit(solution)/shard_map/nsd,fd->nsf/dot_general | solution.py:110
  129.6 5.5 copy.158
  148.7 16.8 %fusion.5 = bf16[6,197,1536]{2,1,0:T(8,128)(2,1)S(1)} fusion(f32[6,197,1536]{2,1,0:T(8,128)S(1)} %bitcast.532, f32[1536]{0:T(1024)S(1)} %reduce.11, u8[197,1536]{1,0:T(8,128)(4,1)S(1)} %copy-done.94, u8[197,1536]{1,0:T(8,128)(4,1)S(1)} %copy-done.93), kind=kLoop, calls=%fused_computation.11 | loop fusion | flops 128904192 | bytes 11504640 | tf_op jit(solution)/shard_map/convert_element_type | solution.py:77
  179.7 4.3 broadcast_select_fusion
  184.0 5.5 copy.151
  194.5 4.9 broadcast_select_fusion.4
  208.5 5.6 copy.169
  214.2 5.8 fusion.204
  220.0 5.5 copy.179
  225.4 5.9 fusion.205
  231.9 4.8 fusion.153
  239.7 21.2 %convert_reduce_fusion.1 = (f32[1536]{0:T(1024)}, bf16[6,197,1536]{2,1,0:T(8,128)(2,1)S(1)}) fusion(bf16[1,1536,384]{2,1,0:T(8,128)(2,1)S(1)} %copy-done.149, bf16[6,197,384]{2,1,0:T(8,128)(2,1)S(1)} %get-tuple-element.102, f32[6]{0:T(128)S(1)} %copy-done.109, f32[6,197,1536]{2,1,0:T(8,128)S(1)} %get-tuple-element.194, f32[6,197,1536]{2,1,0:T(8,128)S(1)} %bitcast.538, ...), kind=kOutput, calls=%fused_computation.44 | convolution fusion | flops 1535501568 | bytes 20255256 | tf_op jit(solution)/shard_map/nsd,fd->nsf/dot_general | solution.py:110
  272.9 6.0 multiply_reduce_fusion.1
  298.9 3.9 fusion.112
  304.0 20.6 %convert_reduce_fusion = (f32[1536]{0:T(1024)S(1)}, bf16[6,197,1536]{2,1,0:T(8,128)(2,1)S(1)}) fusion(bf16[1,1536,384]{2,1,0:T(8,128)(2,1)S(1)} %copy-done.150, bf16[6,197,384]{2,1,0:T(8,128)(2,1)S(1)} %get-tuple-element.106, f32[6]{0:T(128)S(1)} %copy-done.122, f32[6,197,1536]{2,1,0:T(8,128)S(1)} %bitcast.540, f32[6,197,1536]{2,1,0:T(8,128)S(1)} %bitcast.534, ...), kind=kOutput, calls=%fused_computation.43 | convolution fusion | flops 1535501568 | bytes 20255256 | tf_op jit(solution)/shard_map/nsd,fd->nsf/dot_general | solution.py:110
  333.2 8.8 %multiply_reduce_fusion = (f32[6,6,197]{2,1,0:T(8,128)S(1)}, f32[6,6,197,197]{2,3,1,0:T(8,128)}) fusion(f32[6,6,197,197]{2,3,1,0:T(8,128)} %fusion.205, f32[6,6,197]{2,1,0:T(8,128)S(1)} %copy-done.90, bf16[6,197,6,64]{1,3,2,0:T(8,128)(2,1)} %bitcast.527, bf16[6,197,3,6,64]{1,4,3,2,0:T(8,128)(2,1)} %bitcast.506), kind=kOutput, calls=%fused_computation.47 | convolution fusion | flops 184413264 | bytes 15377328 | tf_op jit(solution)/shard_map/nqhc,nkhc->nhqk/dot_general | solution.py:140
  342.1 5.7 fusion.166
  350.2 6.7 multiply_convert_fusion
  362.9 3.9 fusion.111
  367.0 18.4 %fusion.8 = bf16[6,197,1536]{2,1,0:T(8,128)(2,1)S(1)} fusion(f32[6,197,1536]{2,1,0:T(8,128)} %copy-done.60, f32[1536]{0:T(1024)S(1)} %reduce.11, u8[197,1536]{1,0:T(8,128)(4,1)} %get-tuple-element.57, u8[197,1536]{1,0:T(8,128)(4,1)S(1)} %copy-done.92), kind=kLoop, calls=%fused_computation.14 | loop fusion | flops 128904192 | bytes 11504640 | tf_op jit(solution)/shard_map/convert_element_type | solution.py:77
  399.4 5.5 fusion.173
  415.8 5.1 multiply_reduce_fusion.13
  427.5 78.0 %all-reduce.10 = (f32[384]{0:T(512)S(1)}, f32[384]{0:T(512)S(1)}, f32[768]{0:T(1024)S(1)}, f32[384]{0:T(512)S(1)}, f32[384]{0:T(512)S(1)}, /*index=5*/f32[384]{0:T(512)S(1)}, f32[1536]{0:T(1024)S(1)}, f32[384]{0:T(512)S(1)}) all-reduce(f32[384]{0:T(512)S(1)} %add_add_fusion.14, ...), channel_id=2, replica_groups=mesh['segment'=2,'dp'=16] {'dp'}, use_global_device_ids=true, to_apply=%region_48.49.clone | all-reduce | flops 4608 | bytes 36864
  510.2 96.4 %reduce-scatter.13.cloned.1.call-done = f32[24,1152]{1,0:T(8,128)} async-done(((f32[384,1152]{1,0:T(8,128)}), f32[24,1152]{1,0:T(8,128)}) %reduce-scatter.13.cloned.1.call-update) | async-done | bytes 110608
  606.6 132.8 %reduce-scatter.11.cloned.1.call-done = f32[96,384]{1,0:T(8,128)} async-done(((f32[1536,384]{1,0:T(8,128)}), f32[96,384]{1,0:T(8,128)}) %reduce-scatter.11.cloned.1.call-update) | async-done | bytes 147472 | tf_op jit(solution)/shard_map/reduce_scatter | solution.py:266
  739.4 132.1 %reduce-scatter.9.cloned.1.call-done = f32[24,1536]{1,0:T(8,128)} async-done(((f32[384,1536]{1,0:T(8,128)}), f32[24,1536]{1,0:T(8,128)}) %reduce-scatter.9.cloned.1.call-update) | async-done | bytes 147472 | tf_op jit(solution)/shard_map/reduce_scatter | solution.py:266
  (528 shorter events, 185.2 us)
Async XLA Ops:
  7.2 31.2 %copy-start = (bf16[1,384,1536]{2,1,0:T(8,128)(2,1)S(1)}, bf16[1,384,1536]{2,1,0:T(8,128)(2,1)}, u32[]{:S(2)}) copy-start(bf16[1,384,1536]{2,1,0:T(8,128)(2,1)} %param.26) | copy-start | bytes 3538948
  7.2 503.0 %reduce-scatter.15.cloned.1.call-start = ((), (), s32[]{:S(2)}) async-start(), calls=%async_computation.7 | async-start | bytes 626688
  14.8 157.7 %copy-start.130 = (f32[384]{0:T(512)}, f32[384]{0:T(512)S(1)}, u32[]{:S(2)}) copy-start(f32[384]{0:T(512)S(1)} %reduce.5) | copy-start | bytes 4612
  14.9 57.0 %copy-start.110 = (f32[1152]{0:T(1024)}, f32[1152]{0:T(1024)S(1)}, u32[]{:S(2)}) copy-start(f32[1152]{0:T(1024)S(1)} %pad_maximum_fusion) | copy-start | bytes 13828
  28.3 57.7 %copy-start.88 = (f32[6,6,197]{2,1,0:T(8,128)}, f32[6,6,197]{2,1,0:T(8,128)S(1)}, u32[]{:S(2)}) copy-start(f32[6,6,197]{2,1,0:T(8,128)S(1)} %log_add_fusion.2) | copy-start | bytes 85108
  36.4 129.1 %copy-start.128 = (f32[384]{0:T(512)}, f32[384]{0:T(512)S(1)}, u32[]{:S(2)}) copy-start(f32[384]{0:T(512)S(1)} %reduce.12) | copy-start | bytes 4612
  42.3 17.1 %copy-start.59 = (f32[6,197,1536]{2,1,0:T(8,128)}, f32[6,197,1536]{2,1,0:T(8,128)S(1)}, u32[]{:S(2)}) copy-start(f32[6,197,1536]{2,1,0:T(8,128)S(1)} %get-tuple-element.178) | copy-start | bytes 21786628
  42.3 17.7 %copy-start.2 = (f32[6,197,384]{2,1,0:T(8,128)S(1)}, f32[6,197,384]{2,1,0:T(8,128)}, u32[]{:S(2)}) copy-start(f32[6,197,384]{2,1,0:T(8,128)} %copy-done.1) | copy-start | bytes 5446660
  42.3 17.7 %copy-start.146 = (bf16[1,1536,384]{2,1,0:T(8,128)(2,1)S(1)}, bf16[1,1536,384]{2,1,0:T(8,128)(2,1)}, u32[]{:S(2)}) copy-start(bf16[1,1536,384]{2,1,0:T(8,128)(2,1)} %param.28) | copy-start | bytes 3538948
  60.0 62.3 %copy-start.123 = (f32[6]{0:T(128)}, f32[6]{0:T(128)S(1)}, u32[]{:S(2)}) copy-start(f32[6]{0:T(128)S(1)} %get-tuple-element.170) | copy-start | bytes 76
  62.2 8.4 collective-permute-start
  71.0 101.5 %copy-start.101 = (f32[6,197]{1,0:T(8,128)}, f32[6,197]{1,0:T(8,128)S(1)}, u32[]{:S(2)}) copy-start(f32[6,197]{1,0:T(8,128)S(1)} %broadcast_multiply_fusion.9) | copy-start | bytes 14188
  72.0 100.5 %copy-start.115 = (f32[6,197]{1,0:T(8,128)}, f32[6,197]{1,0:T(8,128)S(1)}, u32[]{:S(2)}) copy-start(f32[6,197]{1,0:T(8,128)S(1)} %add_rsqrt_fusion.3) | copy-start | bytes 14188
  96.3 21.9 %copy-start.58 = (f32[6,197,1536]{2,1,0:T(8,128)}, f32[6,197,1536]{2,1,0:T(8,128)S(1)}, u32[]{:S(2)}) copy-start(f32[6,197,1536]{2,1,0:T(8,128)S(1)} %get-tuple-element.183) | copy-start | bytes 21786628
  148.7 16.9 %copy-start.10 = (f32[6,197,384]{2,1,0:T(8,128)S(1)}, f32[6,197,384]{2,1,0:T(8,128)}, u32[]{:S(2)}) copy-start(f32[6,197,384]{2,1,0:T(8,128)} %copy-done.9) | copy-start | bytes 5446660
  148.7 16.9 %copy-start.148 = (bf16[1,1536,384]{2,1,0:T(8,128)(2,1)S(1)}, bf16[1,1536,384]{2,1,0:T(8,128)(2,1)}, u32[]{:S(2)}) copy-start(bf16[1,1536,384]{2,1,0:T(8,128)(2,1)} %param.28) | copy-start | bytes 3538948
  167.7 8.6 collective-permute-start.1
  201.5 35.2 %collective-permute-start.2 = (bf16[6,197,384]{2,1,0:T(8,128)(2,1)}, bf16[6,197,384]{2,1,0:T(8,128)(2,1)}, u32[]{:S(2)}, u32[]{:S(2)}) collective-permute-start(bf16[6,197,384]{2,1,0:T(8,128)(2,1)} %add_convert_fusion.5), channel_id=1, source_target_pairs={{16,0},{17,1},{18,2},{19,3},{20,4},{21,5},{22,6},{23,7},{24,8},{25... | collective-permute-start | bytes 2723336 | tf_op jit(solution)/shard_map/ppermute | solution.py:15
  220.0 11.4 %copy-start.95 = (f32[6,197]{1,0:T(8,128)}, f32[6,197]{1,0:T(8,128)S(1)}, u32[]{:S(2)}) copy-start(f32[6,197]{1,0:T(8,128)S(1)} %broadcast_multiply_fusion.1) | copy-start | bytes 14188
  225.4 14.3 %slice-start.8 = ((s8[7372800]{0:T(1024)(128)(4,1)}), s8[4194304]{0:T(1024)(128)(4,1)S(1)}, s32[]{:S(2)}) async-start(s8[7372800]{0:T(1024)(128)(4,1)} %bitcast.537), calls=%async_computation.16 | async-start | bytes 8388608
  236.7 24.2 %copy-start.60 = (f32[6,197,1536]{2,1,0:T(8,128)}, f32[6,197,1536]{2,1,0:T(8,128)S(1)}, u32[]{:S(2)}) copy-start(f32[6,197,1536]{2,1,0:T(8,128)S(1)} %get-tuple-element.194) | copy-start | bytes 21786628
  239.7 25.9 %copy-start.50 = (bf16[6,197,384]{2,1,0:T(8,128)(2,1)}, bf16[6,197,384]{2,1,0:T(8,128)(2,1)S(1)}, u32[]{:S(2)}) copy-start(bf16[6,197,384]{2,1,0:T(8,128)(2,1)S(1)} %get-tuple-element.102) | copy-start | bytes 2723332
  239.7 21.2 %copy-start.23 = (f32[6,197,384]{2,1,0:T(8,128)S(1)}, f32[6,197,384]{2,1,0:T(8,128)}, u32[]{:S(2)}) copy-start(f32[6,197,384]{2,1,0:T(8,128)} %copy-done.22) | copy-start | bytes 5446660
  295.5 7.4 collective-permute-start.3
  303.9 24.5 %copy-start.47 = (bf16[6,197,384]{2,1,0:T(8,128)(2,1)}, bf16[6,197,384]{2,1,0:T(8,128)(2,1)S(1)}, u32[]{:S(2)}) copy-start(bf16[6,197,384]{2,1,0:T(8,128)(2,1)S(1)} %get-tuple-element.106) | copy-start | bytes 2723332
  304.0 20.7 %copy-start.19 = (f32[6,197,384]{2,1,0:T(8,128)S(1)}, f32[6,197,384]{2,1,0:T(8,128)}, u32[]{:S(2)}) copy-start(f32[6,197,384]{2,1,0:T(8,128)} %get-tuple-element.126) | copy-start | bytes 5446660
  304.0 20.7 %copy-start.96 = (f32[6,197]{1,0:T(8,128)S(1)}, f32[6,197]{1,0:T(8,128)}, u32[]{:S(2)}) copy-start(f32[6,197]{1,0:T(8,128)} %copy-done.95) | copy-start | bytes 14188
  350.2 256.4 %reduce-scatter.13.cloned.1.call-start = ((), (), s32[]{:S(2)}) async-start(), calls=%async_computation.6 | async-start | bytes 1880064
  366.9 372.6 %reduce-scatter.11.cloned.1.call-start = ((), (), s32[]{:S(2)}) async-start(), calls=%async_computation.5 | async-start | bytes 2506752 | tf_op jit(solution)/shard_map/reduce_scatter | solution.py:266
  366.9 18.4 %copy-start.52 = (bf16[6,197,384]{2,1,0:T(8,128)(2,1)S(1)}, bf16[6,197,384]{2,1,0:T(8,128)(2,1)}, u32[]{:S(2)}) copy-start(bf16[6,197,384]{2,1,0:T(8,128)(2,1)} %copy-done.50) | copy-start | bytes 2723332
  366.9 18.4 %copy-start.71 = (bf16[6,197,1536]{2,1,0:T(8,128)(2,1)S(1)}, bf16[6,197,1536]{2,1,0:T(8,128)(2,1)}, u32[]{:S(2)}) copy-start(bf16[6,197,1536]{2,1,0:T(8,128)(2,1)} %copy-done.70) | copy-start | bytes 10893316
  395.2 476.3 %reduce-scatter.9.cloned.1.call-start = ((), (), s32[]{:S(2)}) async-start(), calls=%async_computation.4 | async-start | bytes 2506752 | tf_op jit(solution)/shard_map/reduce_scatter | solution.py:266
  (147 other events, 563.7 us)
Sparse Core Ops, SparseCore 0:
  350.3 125.2 reduce-scatter.14
  481.8 124.8 reduce-scatter.12
  612.9 126.5 reduce-scatter.10
  744.8 126.6 reduce-scatter.8
where the time goes:
time: 885 us; the launch traced here: 878 us
  waiting for transfers between devices  361 us (41%)
  matrix products  225 us (25%)
  other arithmetic  110 us (12%)
  local copies, waits for them, and re-layouts  78.7 us (9%)
  blocking collectives  78 us (9%)
  between operations  18.4 us (2%)
    reduce_scatter x2, waiting for transfers between devices, on_device(): totals = lax.psum_scatter(totals, 'dp', scatter_dimension=0, tiled=True)  265 us
    unnamed x6, waiting for transfers between devices  96.5 us
    unnamed x1, blocking collectives  78 us
    dot_general x3, matrix products, backward(): jnp.einsum('nsd,fd->nsf', down_in, w_down, preferred_element_type=jnp.flo...  63.2 us
    convert_element_type x3, other arithmetic, forward(): active = gelu_exact(before).astype(jnp.bfloat16)  52.3 us
    unnamed x345, local copies, waits for them, and re-layouts  23.2 us
  transfers between devices with their start and end apart: 8, of which 3 were waited for; matrix products, arithmetic and copies ran while one was open for 14% of the time, Pallas kernels for 0%

commit v1 on v0

v1 whole, which is shorter than its diff:
```python
import jax
import jax.numpy as jnp
from jax import lax
from jax.experimental import pallas as pl
from jax.experimental.pallas import tpu as pltpu
from jax.sharding import PartitionSpec as P

HEAD = 64
EPSILON = 1e-06
BF16 = jnp.bfloat16
F32 = jnp.float32
GROUP = 2
VMEM_LIMIT = 58 * 1024 * 1024


def dot(a, b):
    return lax.dot_general(a, b, (((1,), (0,)), ((), ())), preferred_element_type=F32)


def dot_nt(a, b):
    return lax.dot_general(a, b, (((1,), (1,)), ((), ())), preferred_element_type=F32)


def dot_tn(a, b):
    return lax.dot_general(a, b, (((0,), (0,)), ((), ())), preferred_element_type=F32)


def normalized(rows):
    centered = rows - jnp.mean(rows, axis=-1, keepdims=True)
    spread = jnp.mean(centered * centered, axis=-1, keepdims=True)
    inverse = lax.rsqrt(spread + EPSILON)
    return centered * inverse, inverse


def norm_backward(rows, grad, gain):
    hat, inverse = normalized(rows)
    scaled = grad * gain
    inner = jnp.mean(scaled * hat, axis=-1, keepdims=True)
    dx = inverse * (scaled - jnp.mean(scaled, axis=-1, keepdims=True) - hat * inner)
    return dx, grad * hat


def gelu_and_slope(x):
    bell = jnp.exp(x * x * -0.5)
    t = 1.0 / (1.0 + jnp.abs(x) * (0.3275911 * 0.7071067811865476))
    poly = t * (
        0.5 * 0.254829592
        + t
        * (
            0.5 * -0.284496736
            + t * (0.5 * 1.421413741 + t * (0.5 * -1.453152027 + t * (0.5 * 1.061405429)))
        )
    )
    tail = poly * bell
    cdf = jnp.where(x >= 0.0, 1.0 - tail, tail)
    return x * cdf, cdf + x * (bell * 0.3989422804014327)


def fold(rows):
    total = rows[0:8]
    for at in range(8, rows.shape[0], 8):
        total = total + rows[at : at + 8]
    return total


def row_chunks(total, size=32):
    return [(at, min(size, total - at)) for at in range(0, total, size)]


def forward_kernel(
    padded,
    keys,
    meta,
    h_ref,
    gain1,
    bias1,
    w_qkv,
    b_qkv,
    w_out,
    b_out,
    gain2,
    bias2,
    w_up,
    b_up,
    w_down,
    b_down,
    act_ref,
    normed_ref,
    joined_ref,
    p_ref,
    attended_ref,
    middle_ref,
    second_ref,
    active_ref,
    slope_ref,
    hidden,
    before,
):
    step = pl.program_id(0)
    count = meta[0]
    tokens, features = h_ref.shape[2:]
    heads = features // HEAD
    rows = GROUP * padded
    hidden_units = w_up.shape[1]

    @pl.when(step * GROUP >= count)
    def _():
        act_ref[...] = jnp.zeros_like(act_ref)

    @pl.when(step * GROUP < count)
    def _():
        for j in range(GROUP):
            hidden[j * padded + padded - 16 : (j + 1) * padded] = jnp.zeros((16, features), F32)
            hidden[j * padded : j * padded + tokens] = h_ref[0, j].astype(F32)
        for at, size in row_chunks(rows):
            hat, _ = normalized(hidden[at : at + size])
            normed_ref[at : at + size] = (hat * gain1[...] + bias1[...]).astype(BF16)
        for j in range(GROUP):
            lines = normed_ref[j * padded : (j + 1) * padded]
            for part in range(3):
                columns = slice(part * features, (part + 1) * features)
                value = (dot(lines, w_qkv[:, columns]) + b_qkv[:, columns]).astype(BF16)
                if part == 0:
                    value = value * jnp.asarray(HEAD**-0.5, BF16)
                joined_ref[j * keys : j * keys + padded, columns] = value
            joined_ref[j * keys + padded : (j + 1) * keys] = jnp.zeros(
                (keys - padded, 3 * features), BF16
            )
        lane = lax.broadcasted_iota(jnp.int32, (padded, 2 * HEAD), 1)
        real = lax.broadcasted_iota(jnp.int32, (padded, keys), 1) < tokens
        for j in range(GROUP):
            for pair in range(heads // 2):
                at = pair * 2 * HEAD
                q = joined_ref[j * keys : j * keys + padded, at : at + 2 * HEAD]
                k = joined_ref[j * keys : (j + 1) * keys, features + at : features + at + 2 * HEAD]
                v = joined_ref[
                    j * keys : (j + 1) * keys, 2 * features + at : 2 * features + at + 2 * HEAD
                ]
                parts = []
                for half in range(2):
                    mine = (lane < HEAD) if half == 0 else (lane >= HEAD)
                    s = dot_nt(jnp.where(mine, q, jnp.zeros_like(q)), k)
                    s = jnp.where(real, s, -1e30)
                    e = jnp.exp(s - jnp.max(s, axis=-1, keepdims=True))
                    p = (e * (1.0 / jnp.sum(e, axis=-1, keepdims=True))).astype(BF16)
                    p_ref[j, 2 * pair + half] = p
                    parts.append(dot(p, v))
                attended_ref[j * padded : (j + 1) * padded, at : at + 2 * HEAD] = jnp.where(
                    lane < HEAD, parts[0], parts[1]
                ).astype(BF16)
        middle_ref[...] = dot(attended_ref[...], w_out[...])
        for at, size in row_chunks(rows):
            middle = middle_ref[at : at + size] + hidden[at : at + size] + b_out[...]
            middle_ref[at : at + size] = middle
            hat, _ = normalized(middle)
            second_ref[at : at + size] = (hat * gain2[...] + bias2[...]).astype(BF16)
        width = features
        for j in range(GROUP):
            lines = slice(j * padded, (j + 1) * padded)
            for c in range(hidden_units // width):
                columns = slice(c * width, (c + 1) * width)
                before[lines, columns] = dot(second_ref[lines], w_up[:, columns])
                for at, size in row_chunks(padded, 16):
                    piece = slice(j * padded + at, j * padded + at + size)
                    active, slope = gelu_and_slope(before[piece, columns] + b_up[:, columns])
                    active_ref[piece, columns] = active.astype(BF16)
                    slope_ref[piece, columns] = slope.astype(BF16)
            hidden[lines] = dot(active_ref[lines], w_down[...])
        for j in range(GROUP):
            keep = jnp.where(step * GROUP + j < count, 1.0, 0.0)
            lines = slice(j * padded, (j + 1) * padded)
            result = (hidden[lines] + middle_ref[lines] + b_down[...]) * keep
            act_ref[0, j] = result[:tokens].astype(BF16)


def mlp_backward_kernel(
    padded,
    meta,
    grad_ref,
    active_ref,
    slope_ref,
    second_ref,
    middle_ref,
    gain2,
    w_up,
    w_down,
    grad_middle_ref,
    up_ref,
    down_ref,
    vec_ref,
    grad_out,
    down_in,
    grad_before,
    grad_norm,
    sum_up,
    sum_down,
    vec_one,
    vec_up,
):
    step = pl.program_id(0)
    count = meta[0]
    tokens, features = grad_ref.shape[2:]
    rows = GROUP * padded
    hidden_units = w_up.shape[1]

    @pl.when(step == 0)
    def _():
        for ref in (sum_up, sum_down, vec_one, vec_up):
            ref[...] = jnp.zeros_like(ref)

    @pl.when(step * GROUP < count)
    def _():
        for j in range(GROUP):
            keep = jnp.where(step * GROUP + j < count, 1.0, 0.0)
            value = grad_ref[0, j].astype(F32) * keep
            grad_out[j * padded + padded - 16 : (j + 1) * padded] = jnp.zeros((16, features), F32)
            grad_out[j * padded : j * padded + tokens] = value
        for at, size in row_chunks(rows):
            value = grad_out[at : at + size]
            down_in[at : at + size] = value.astype(BF16)
            vec_one[0:8] += fold(value)
        width = features
        sum_down[...] += dot_tn(down_in[...], active_ref[...])
        for j in range(GROUP):
            lines = slice(j * padded, (j + 1) * padded)
            for c in range(hidden_units // width):
                columns = slice(c * width, (c + 1) * width)
                piece = dot_nt(down_in[lines], w_down[columns, :])
                piece = (piece * slope_ref[lines, columns].astype(F32)).astype(BF16)
                grad_before[lines, columns] = piece
                vec_up[:, columns] += fold(piece.astype(F32))
            grad_norm[lines] = dot_nt(grad_before[lines], w_up[...])
        sum_up[...] += dot_tn(second_ref[...], grad_before[...])
        for at, size in row_chunks(rows):
            grad = grad_norm[at : at + size]
            dx, by_hat = norm_backward(middle_ref[at : at + size], grad, gain2[...])
            vec_one[8:16] += fold(by_hat)
            vec_one[16:24] += fold(grad)
            grad_middle_ref[at : at + size] = grad_out[at : at + size] + dx

    @pl.when(step == pl.num_programs(0) - 1)
    def _():
        for c in range(hidden_units // features):
            columns = slice(c * features, (c + 1) * features)
            up_ref[c] = sum_up[:, columns].astype(BF16)
            down_ref[columns, :] = sum_down[:, columns].T.astype(BF16)
        vec_ref[...] = jnp.zeros_like(vec_ref)
        vec_ref[0:1, :hidden_units] = jnp.sum(vec_up[...], axis=0, keepdims=True)
        for n in range(3):
            vec_ref[n + 1 : n + 2, :features] = jnp.sum(
                vec_one[8 * n : 8 * n + 8], axis=0, keepdims=True
            )


def attention_backward_kernel(
    padded,
    keys,
    meta,
    grad_middle_ref,
    h_ref,
    normed_ref,
    joined_ref,
    p_ref,
    attended_ref,
    gain1,
    w_qkv,
    w_out,
    grad_ref,
    big_ref,
    vec_ref,
    hidden,
    out_in,
    grad_attended,
    grad_joined,
    grad_norm,
    sums,
    vec_one,
    vec_qkv,
):
    step = pl.program_id(0)
    count = meta[0]
    tokens, features = h_ref.shape[2:]
    heads = features // HEAD
    rows = GROUP * padded

    @pl.when(step == 0)
    def _():
        for ref in (sums, vec_one, vec_qkv):
            ref[...] = jnp.zeros_like(ref)

    @pl.when(step * GROUP >= count)
    def _():
        grad_ref[...] = jnp.zeros_like(grad_ref)

    @pl.when(step * GROUP < count)
    def _():
        for j in range(GROUP):
            hidden[j * padded + padded - 16 : (j + 1) * padded] = jnp.zeros((16, features), F32)
            hidden[j * padded : j * padded + tokens] = h_ref[0, j].astype(F32)
        for at, size in row_chunks(rows):
            value = grad_middle_ref[at : at + size].astype(BF16)
            out_in[at : at + size] = value
            vec_one[0:8] += fold(value.astype(F32))
        sums[:, 3 * features :] += dot_tn(attended_ref[...], out_in[...])
        grad_attended[...] = dot_nt(out_in[...], w_out[...]).astype(BF16)
        lane = lax.broadcasted_iota(jnp.int32, (padded, 2 * HEAD), 1)
        for j in range(GROUP):
            lines = slice(j * padded, (j + 1) * padded)
            for pair in range(heads // 2):
                at = pair * 2 * HEAD
                q = joined_ref[j * keys : j * keys + padded, at : at + 2 * HEAD]
                k = joined_ref[j * keys : (j + 1) * keys, features + at : features + at + 2 * HEAD]
                v = joined_ref[
                    j * keys : (j + 1) * keys, 2 * features + at : 2 * features + at + 2 * HEAD
                ]
                ga = grad_attended[lines, at : at + 2 * HEAD]
                gq, gk, gv = [], [], []
                for half in range(2):
                    mine = (lane < HEAD) if half == 0 else (lane >= HEAD)
                    gp = dot_nt(jnp.where(mine, ga, jnp.zeros_like(ga)), v)
                    p = p_ref[j, 2 * pair + half]
                    wide = p.astype(F32)
                    by = wide * gp
                    gs = (by - wide * jnp.sum(by, axis=-1, keepdims=True)).astype(BF16)
                    gq.append(dot(gs, k))
                    gk.append(dot_tn(gs, q)[:padded])
                    gv.append(dot_tn(p, ga)[:padded])
                left = lane < HEAD
                parts = (
                    jnp.where(left, gq[0], gq[1]) * HEAD**-0.5,
                    jnp.where(left, gk[0], gk[1]),
                    jnp.where(left, gv[0], gv[1]),
                )
                for n, part in enumerate(parts):
                    column = n * features + at
                    part = part.astype(BF16)
                    grad_joined[lines, column : column + 2 * HEAD] = part
                    vec_qkv[:, column : column + 2 * HEAD] += fold(part.astype(F32))
        sums[:, : 3 * features] += dot_tn(normed_ref[...], grad_joined[...])
        grad_norm[...] = dot_nt(grad_joined[...], w_qkv[...])
        for at, size in row_chunks(rows):
            grad = grad_norm[at : at + size]
            dx, by_hat = norm_backward(hidden[at : at + size], grad, gain1[...])
            vec_one[8:16] += fold(by_hat)
            vec_one[16:24] += fold(grad)
            hidden[at : at + size] = grad_middle_ref[at : at + size] + dx
        for j in range(GROUP):
            grad_ref[0, j] = hidden[j * padded : j * padded + tokens].astype(BF16)

    @pl.when(step == pl.num_programs(0) - 1)
    def _():
        big_ref[...] = sums[...].astype(BF16)
        vec_ref[...] = jnp.zeros_like(vec_ref)
        vec_ref[0:1, : 3 * features] = jnp.sum(vec_qkv[...], axis=0, keepdims=True)
        for n in range(3):
            vec_ref[n + 1 : n + 2, :features] = jnp.sum(
                vec_one[8 * n : 8 * n + 8], axis=0, keepdims=True
            )


def whole(shape):
    return pl.BlockSpec(shape, lambda i, meta: (0,) * len(shape))


def lines_of(shape):
    return pl.BlockSpec(shape, lambda i, meta: (i,) + (0,) * (len(shape) - 1))


def images_of(micro_shape):
    tokens, features = micro_shape[2:]
    return pl.BlockSpec((1, GROUP, tokens, features), lambda i, meta: (meta[1], i, 0, 0))


def call(body, meta, args, arg_specs, outs, out_specs, scratch, flops):
    return pl.pallas_call(
        body,
        grid_spec=pltpu.PrefetchScalarGridSpec(
            num_scalar_prefetch=1,
            grid=(args[0][1],),
            in_specs=arg_specs,
            out_specs=out_specs,
            scratch_shapes=scratch,
        ),
        out_shape=outs,
        compiler_params=pltpu.CompilerParams(
            vmem_limit_bytes=VMEM_LIMIT, dimension_semantics=("arbitrary",)
        ),
        cost_estimate=pl.CostEstimate(flops=flops, bytes_accessed=20_000_000, transcendentals=0),
    )(meta, *args[1:])


def struct(shape, kind):
    return jax.ShapeDtypeStruct(shape, kind)


def sizes(images):
    slots, tokens, features = images.shape[1:]
    padded = -(-tokens // 16) * 16
    keys = -(-tokens // 128) * 128
    return slots, tokens, features, padded, keys


def forward(meta, images, params):
    slots, tokens, features, padded, keys = sizes(images)
    heads = features // HEAD
    steps = slots // GROUP
    rows = slots * padded
    units = params[8].shape[1]
    outs = [
        (struct((1, slots, tokens, features), BF16), None),
        (struct((rows, features), BF16), (GROUP * padded, features)),
        (struct((slots * keys, 3 * features), BF16), (GROUP * keys, 3 * features)),
        (struct((slots, heads, padded, keys), BF16), (GROUP, heads, padded, keys)),
        (struct((rows, features), BF16), (GROUP * padded, features)),
        (struct((rows, features), F32), (GROUP * padded, features)),
        (struct((rows, features), BF16), (GROUP * padded, features)),
        (struct((rows, units), BF16), (GROUP * padded, units)),
        (struct((rows, units), BF16), (GROUP * padded, units)),
    ]
    act_spec = pl.BlockSpec((1, GROUP, tokens, features), lambda i, meta: (0, i, 0, 0))
    return call(
        lambda *refs: forward_kernel(padded, keys, *refs),
        meta,
        ((None, steps), images, *params),
        [images_of(images.shape)] + [whole(p.shape) for p in params],
        [o[0] for o in outs],
        [act_spec] + [lines_of(o[1]) for o in outs[1:]],
        [
            pltpu.VMEM((GROUP * padded, features), F32),
            pltpu.VMEM((GROUP * padded, units), F32),
        ],
        flops=steps * GROUP * padded * features * (features * 8 + units * 4),
    )


def mlp_backward(meta, grad, saved, params):
    slots, tokens, features, padded, keys = sizes(grad)
    steps = slots // GROUP
    units = params[1].shape[1]
    block = GROUP * padded
    active, slope, second, middle = saved
    return call(
        lambda *refs: mlp_backward_kernel(padded, *refs),
        meta,
        ((None, steps), grad, active, slope, second, middle, *params),
        [images_of(grad.shape)]
        + [lines_of((block, units))] * 2
        + [lines_of((block, features))] * 2
        + [whole(p.shape) for p in params],
        [
            struct((slots * padded, features), F32),
            struct((units // features, features, features), BF16),
            struct((units, features), BF16),
            struct((8, units), F32),
        ],
        [
            lines_of((block, features)),
            whole((units // features, features, features)),
            whole((units, features)),
            whole((8, units)),
        ],
        [
            pltpu.VMEM((block, features), F32),
            pltpu.VMEM((block, features), BF16),
            pltpu.VMEM((block, units), BF16),
            pltpu.VMEM((block, features), F32),
            pltpu.VMEM((features, units), F32),
            pltpu.VMEM((features, units), F32),
            pltpu.VMEM((24, features), F32),
            pltpu.VMEM((8, units), F32),
        ],
        flops=steps * block * features * units * 8,
    )


def attention_backward(meta, grad_middle, images, saved, params):
    slots, tokens, features, padded, keys = sizes(images)
    steps = slots // GROUP
    heads = features // HEAD
    block = GROUP * padded
    normed, joined, p, attended = saved
    return call(
        lambda *refs: attention_backward_kernel(padded, keys, *refs),
        meta,
        ((None, steps), grad_middle, images, normed, joined, p, attended, *params),
        [
            lines_of((block, features)),
            images_of(images.shape),
            lines_of((block, features)),
            lines_of((GROUP * keys, 3 * features)),
            lines_of((GROUP, heads, padded, keys)),
            lines_of((block, features)),
        ]
        + [whole(q.shape) for q in params],
        [
            struct((1, slots, tokens, features), BF16),
            struct((features, 4 * features), BF16),
            struct((8, 3 * features), F32),
        ],
        [
            pl.BlockSpec((1, GROUP, tokens, features), lambda i, meta: (0, i, 0, 0)),
            whole((features, 4 * features)),
            whole((8, 3 * features)),
        ],
        [
            pltpu.VMEM((block, features), F32),
            pltpu.VMEM((block, features), BF16),
            pltpu.VMEM((block, features), BF16),
            pltpu.VMEM((block, 3 * features), BF16),
            pltpu.VMEM((block, features), F32),
            pltpu.VMEM((features, 4 * features), F32),
            pltpu.VMEM((24, features), F32),
            pltpu.VMEM((8, 3 * features), F32),
        ],
        flops=steps * block * features * features * 24,
    )


def swap_cores(block):
    return lax.ppermute(block, "segment", [(0, 1), (1, 0)])


def halve(block, bit):
    dp = lax.axis_size("dp")
    mine = (lax.axis_index("dp") >> bit) & 1
    keep = lax.dynamic_index_in_dim(block, mine, 1, keepdims=False)
    send = lax.dynamic_index_in_dim(block, 1 - mine, 1, keepdims=False)
    got = lax.ppermute(send, "dp", [(i, i ^ (1 << bit)) for i in range(dp)])
    return (keep.astype(F32) + got.astype(F32)).astype(block.dtype)


def reduce_shards(block, order):
    dp = lax.axis_size("dp")
    rest = block.shape[1:]
    bits = dp.bit_length() - 1
    held = list(range(bits))
    for bit in order:
        below = held.index(bit)
        block = block.reshape((-1, 2, 1 << below) + rest)
        block = halve(block, bit)
        held.remove(bit)
        block = block.reshape((-1,) + rest)
    top = 1 << len(held)
    low = bits - len(held)
    me = lax.axis_index("dp") >> low
    total = lax.dynamic_index_in_dim(block, me, 0, keepdims=False).astype(F32)
    for other in range(1, top):
        route = [(i, i ^ (other << low)) for i in range(dp)]
        send = lax.dynamic_index_in_dim(block, me ^ other, 0, keepdims=False)
        total = total + lax.ppermute(send, "dp", route).astype(F32)
    return total


def reduce_both_ways(block, axis):
    dp = lax.axis_size("dp")
    low = list(range(max(dp.bit_length() - 3, 0)))
    first, second = jnp.split(block, 2, axis=axis)
    parts = [reduce_shards(first, low), reduce_shards(second, low[:2][::-1] + low[2:])]
    return jnp.concatenate(parts, axis=axis - 1)


def meet(keep, send):
    return (keep.astype(F32) + swap_cores(send).astype(F32)).astype(BF16)


def reduce_mlp(up, down, first):
    dp = lax.axis_size("dp")
    blocks, rows, features = up.shape
    up = up.reshape(blocks, dp, rows // dp, features).swapaxes(0, 1)
    up = up.reshape(dp, blocks * rows // dp, features)
    down = down.reshape(up.shape)
    return reduce_both_ways(meet(jnp.where(first, up, down), jnp.where(first, down, up)), 1)


def reduce_attention(block, first):
    dp = lax.axis_size("dp")
    low, high = jnp.split(block.reshape(dp, block.shape[0] // dp, -1), 2, axis=2)
    return reduce_both_ways(meet(jnp.where(first, low, high), jnp.where(first, high, low)), 2)


def on_device(inputs, image_count, cotangent, *params):
    dp = lax.axis_size("dp")
    core = lax.axis_index("segment")
    first = core == 0
    slots, tokens, features = inputs.shape[1:]
    own = [p[0] for p in params]
    received = [swap_cores(p) for p in own]
    layers = []
    for layer in range(2):
        mine = core == layer
        named = [jnp.where(mine, a, b) for a, b in zip(own, received)]
        g1, b1, wq, bqv, wo, bo, g2, b2, wu, bu, wd, bd = named
        bq = jnp.concatenate([bqv[:features], jnp.zeros((features,), F32), bqv[features:]])
        rows = [v[None] for v in (g1, b1, bq, bo, g2, b2, bu, bd)]
        g1, b1, bq, bo, g2, b2, bu, bd = rows
        layers.append((g1, b1, wq, bq, wo, bo, g2, b2, wu, bu, wd, bd))
    count = lax.dynamic_index_in_dim(image_count[:, 0], core, 0, keepdims=False)
    outer = jnp.stack([count, core.astype(jnp.int32)])
    inner = jnp.stack([count, jnp.zeros((), jnp.int32)])

    saved = []
    acts = []
    images = inputs
    for layer in range(2):
        act, *kept = forward(outer if layer == 0 else inner, images, layers[layer])
        saved.append((images, kept))
        acts.append(act)
        images = act
    grad = cotangent
    grads = [None, None]
    bigs = [None, None]
    vecs = [None, None]
    for layer in (1, 0):
        g1, b1, wq, bq, wo, bo, g2, b2, wu, bu, wd, bd = layers[layer]
        images, (normed, joined, p, attended, middle, second, active, slope) = saved[layer]
        grad_middle, up, down, vec_mlp = mlp_backward(
            outer if layer == 1 else inner, grad, (active, slope, second, middle), (g2, wu, wd)
        )
        grad, big_att, vec_att = attention_backward(
            outer if layer == 0 else inner,
            grad_middle,
            images,
            (normed, joined, p, attended),
            (g1, wq, wo),
        )
        grads[layer] = grad
        bigs[layer] = (reduce_mlp(up, down, first), reduce_attention(big_att, first))
        vecs[layer] = (vec_mlp, vec_att)

    def both(values):
        low, high = values
        from_high = lax.ppermute(low, "segment", [(1, 0)])
        from_low = lax.ppermute(high, "segment", [(0, 1)])
        return jnp.where(
            first,
            jnp.concatenate([low, from_high], 0),
            jnp.concatenate([from_low, high], 0),
        )[None]

    activations = both(acts)
    input_grads = both(grads)

    share = features // dp
    units = params[8].shape[2]

    def exchange(low, high):
        mine = jnp.where(first, low, high)
        other = swap_cores(jnp.where(first, high, low))
        return jnp.where(first, mine, other), jnp.where(first, other, mine)

    g_up, g_down = exchange(bigs[0][0], bigs[1][0])
    attention = jnp.concatenate(exchange(bigs[0][1], bigs[1][1]), axis=1)
    g_up = g_up.reshape(units // features, share, features).swapaxes(0, 1).reshape(share, units)
    g_qkv = attention[:, : 3 * features]
    g_out = attention[:, 3 * features :]

    def vector_shards(layer):
        vec_mlp, vec_att = vecs[layer]
        qv = jnp.concatenate([vec_att[0, :features], vec_att[0, 2 * features : 3 * features]])
        named = [
            vec_att[2, :features],
            vec_att[3, :features],
            qv,
            vec_att[1, :features],
            vec_mlp[2, :features],
            vec_mlp[3, :features],
            vec_mlp[0],
            vec_mlp[1, :features],
        ]
        return jnp.concatenate([v.reshape(dp, -1) for v in named], axis=1)

    vec = [vector_shards(layer) for layer in range(2)]
    vec = jnp.where(first, vec[0], vec[1]) + swap_cores(jnp.where(first, vec[1], vec[0]))
    bits = dp.bit_length() - 1
    vec = reduce_shards(vec, list(range(max(bits - 2, 0))))
    at = 0
    parts = []
    for n in (1, 1, 2, 1, 1, 1, units // features, 1):
        parts.append(vec[at : at + n * share])
        at += n * share
    ln1_gain, ln1_bias, b_qv, b_out, ln2_gain, ln2_bias, b_up, b_down = parts
    outs = (
        ln1_gain,
        ln1_bias,
        g_qkv,
        b_qv,
        g_out,
        b_out,
        ln2_gain,
        ln2_bias,
        g_up,
        b_up,
        g_down,
        b_down,
    )
    return (activations, input_grads) + tuple(o[None] for o in outs)


def solution(mesh):
    in_specs = (
        P(None, "dp", None, None),
        P(None, "dp"),
        P(None, "dp", None, None),
        P("segment", None),
        P("segment", None),
        P("segment", None, None),
        P("segment", None),
        P("segment", None, None),
        P("segment", None),
        P("segment", None),
        P("segment", None),
        P("segment", None, None),
        P("segment", None),
        P("segment", None, None),
        P("segment", None),
    )
    out_specs = (
        P("segment", None, "dp", None, None),
        P("segment", None, "dp", None, None),
        P("segment", "dp"),
        P("segment", "dp"),
        P("segment", "dp", None),
        P("segment", "dp"),
        P("segment", "dp", None),
        P("segment", "dp"),
        P("segment", "dp"),
        P("segment", "dp"),
        P("segment", "dp", None),
        P("segment", "dp"),
        P("segment", "dp", None),
        P("segment", "dp"),
    )
    return jax.shard_map(
        on_device, mesh=mesh, in_specs=in_specs, out_specs=out_specs, check_vma=False
    )
```

time: 885 us -> 320 us (0.36)
  waiting for transfers between devices: 361 us -> 44.3 us
  matrix products: 225 us -> 0 us
  Pallas kernels: 0 us -> 131 us
  other arithmetic: 110 us -> 31.5 us
  blocking collectives: 78 us -> 0 us
  starting transfers between devices: 7.63 us -> 72.6 us
  local copies, waits for them, and re-layouts: 78.7 us -> 34.6 us
  between operations: 18.4 us -> 1.92 us
    reduce_scatter x2 -> x0, waiting for transfers between devices: 265 us -> none  [on_device(): totals = lax.psum_scatter(totals, 'dp', scatter_dimension=0, tiled=True)]
    dot_general x57 -> x0, matrix products: 225 us -> none  [the longest x3 63.2 us: backward(): jnp.einsum('nsd,fd->nsf', down_in, w_down, preferred_element_type=jnp.flo...]
    pallas_call x0 -> x6, Pallas kernels: none -> 131 us  [call(): pl.pallas_call(body, grid_spec=pltpu.PrefetchScalarGridSpec(num_scalar_pr...]
    unnamed x6 -> x0, waiting for transfers between devices: 96.5 us -> none
    unnamed x1 -> x0, blocking collectives: 78 us -> none
    ppermute x4 -> x68, starting transfers between devices: 7.3 us -> 72.6 us  [the longest x27 34.7 us: reduce_shards(): total = total + lax.ppermute(send, 'dp', route).astype(F32)]
    convert_element_type x9 -> x20, other arithmetic: 66.6 us -> 2.48 us  [the longest x4 1.65 us: meet(): return (keep.astype(F32) + swap_cores(send).astype(F32)).astype(BF16)]
    ppermute x4 -> x68, waiting for transfers between devices: 0.01 us -> 44.3 us  [the longest x18 22.3 us: halve(): got = lax.ppermute(send, 'dp', [(i, i ^ 1 << bit) for i in range(dp)])]
  transfers between devices with their start and end apart: 8 -> 68, of which waited for: 3 -> 27; matrix products, arithmetic and copies ran while one was open for 14% -> 18% of each run, Pallas kernels for 0% -> 8%
where the time goes in v1:
time: 320 us; the launch traced here: 316 us
  Pallas kernels  131 us (41%)
  starting transfers between devices  72.6 us (23%)
  waiting for transfers between devices  44.3 us (14%)
  local copies, waits for them, and re-layouts  34.6 us (11%)
  other arithmetic  31.5 us (10%)
    pallas_call x6, Pallas kernels, call(): pl.pallas_call(body, grid_spec=pltpu.PrefetchScalarGridSpec(num_scalar_pr...  131 us
    ppermute x27, starting transfers between devices, reduce_shards(): total = total + lax.ppermute(send, 'dp', route).astype(F32)  34.7 us
    ppermute x18, starting transfers between devices, halve(): got = lax.ppermute(send, 'dp', [(i, i ^ 1 << bit) for i in range(dp)])  26.8 us
    ppermute x18, waiting for transfers between devices, halve(): got = lax.ppermute(send, 'dp', [(i, i ^ 1 << bit) for i in range(dp)])  22.3 us
    ppermute x27, waiting for transfers between devices, reduce_shards(): total = total + lax.ppermute(send, 'dp', route).astype(F32)  21.2 us
    select_n x12, other arithmetic, on_device(): named = [jnp.where(mine, a, b) for a, b in zip(own, received)]  11.1 us
    unnamed x46, local copies, waits for them, and re-layouts  10.5 us
    unnamed x8, other arithmetic  9.06 us
  transfers between devices with their start and end apart: 68, of which 27 were waited for; matrix products, arithmetic and copies ran while one was open for 18% of the time, Pallas kernels for 8%

profile of v1, /device:TPU:0, one launch (start us, length us, event | category | flops | bytes accessed | tf_op | source)
XLA Modules:
  0.0 316.1 jit_solution(348334969116487014)
XLA Ops:
  13.2 3.1 copy.53.refs_1_.refs_2_
  39.7 24.6 %shard_map.254 = (bf16[1,6,197,384]{3,2,1,0:T(8,128)(2,1)}, bf16[1248,384]{1,0:T(8,128)(2,1)}, bf16[1536,1152]{1,0:T(8,128)(2,1)}, bf16[6,6,208,256]{3,2,1,0:T(8...) custom-call(s32[2]{0:T(128)} %get-tuple-element.212.refs_0_, ...), custom_call_target="tpu_custom_call" | custom-call | flops 4416602112 | bytes 20000000 | tf_op jit(solution)/shard_map/pallas_call | solution.py:375
  64.3 24.5 %shard_map.255 = (bf16[1,6,197,384]{3,2,1,0:T(8,128)(2,1)}, bf16[1248,384]{1,0:T(8,128)(2,1)}, bf16[1536,1152]{1,0:T(8,128)(2,1)}, bf16[6,6,208,256]{3,2,1,0:T(8...) custom-call(s32[2]{0:T(128)} %get-tuple-element.213.refs_0_, ...), custom_call_target="tpu_custom_call" | custom-call | flops 4416602112 | bytes 20000000 | tf_op jit(solution)/shard_map/pallas_call | solution.py:375
  88.8 16.6 %shard_map.256 = (f32[1248,384]{1,0:T(8,128)}, bf16[4,384,384]{2,1,0:T(8,128)(2,1)}, bf16[1536,384]{1,0:T(8,128)(2,1)}, f32[8,1536]{1,0:T(8,128)}) custom-call(s32[2]{0:T(128)} %get-tuple-element.212.refs_0_, bf16[2,6,197,384]{3,2,1,0:T(8,128)(2,1)} %copy.54.refs_1_, bf16[1248,1536]{1,0:T(8,128)(2,1)} %get-tuple-element.48.refs_2_, ...), custom_call_target="tpu_custom_call" | custom-call | flops 5888802816 | bytes 20000000 | tf_op jit(solution)/shard_map/pallas_call | solution.py:375
  105.4 24.4 %shard_map.257 = (bf16[1,6,197,384]{3,2,1,0:T(8,128)(2,1)}, bf16[384,1536]{1,0:T(8,128)(2,1)}, f32[8,1152]{1,0:T(8,128)}) custom-call(s32[2]{0:T(128)} %get-tuple-element.213.refs_0_, f32[1248,384]{1,0:T(8,128)} %get-tuple-element.52.refs_1_, bf16[1,6,197,384]{3,2,1,0:T(8,128)(2,1)} %get-tuple-element.46.refs_1_.refs_2_, ...), custom_call_target="tpu_custom_call" | custom-call | flops 4416602112 | bytes 20000000 | tf_op jit(solution)/shard_map/pallas_call | solution.py:375
  129.8 16.2 %shard_map.258 = (f32[1248,384]{1,0:T(8,128)}, bf16[4,384,384]{2,1,0:T(8,128)(2,1)}, bf16[1536,384]{1,0:T(8,128)(2,1)}, f32[8,1536]{1,0:T(8,128)}) custom-call(s32[2]{0:T(128)} %get-tuple-element.213.refs_0_, bf16[1,6,197,384]{3,2,1,0:T(8,128)(2,1)} %get-tuple-element.57.refs_1_, bf16[1248,1536]{1,0:T(8,128)(2,1)} %get-tuple-element.58.refs_2_, ...), custom_call_target="tpu_custom_call" | custom-call | flops 5888802816 | bytes 20000000 | tf_op jit(solution)/shard_map/pallas_call | solution.py:375
  149.4 2.2 collective-permute-start.15
  154.3 24.7 %shard_map.259 = (bf16[1,6,197,384]{3,2,1,0:T(8,128)(2,1)}, bf16[384,1536]{1,0:T(8,128)(2,1)}, f32[8,1152]{1,0:T(8,128)}) custom-call(s32[2]{0:T(128)} %get-tuple-element.212.refs_0_, f32[1248,384]{1,0:T(8,128)} %get-tuple-element.62.refs_1_, bf16[2,6,197,384]{3,2,1,0:T(8,128)(2,1)} %copy.53.refs_1_.refs_2_, bf16[1248,384]{1,0:T(8,128)(2,1)} %get-tuple-element.63.refs_3_, ...), custom_call_target="tpu_custom_call" | custom-call | flops 4416602112 | bytes 20000000 | tf_op jit(solution)/shard_map/pallas_call | solution.py:375
  187.6 5.7 %collective-permute-start.17 = (f32[8,1,288]{2,1,0:T(1,128)S(1)}, f32[8,1,288]{2,1,0:T(1,128)S(1)}, u32[]{:S(2)}, u32[]{:S(2)}) collective-permute-start(f32[8,1,288]{2,1,0:T(1,128)S(1)} %fusion.51), channel_id=1, source_target_pairs={{0,1},{1,0},{2,3},{3,2},{4,5},{5,4},{6,7},{7,6},{8,9},{9,8},{10,11... | collective-permute-start | bytes 27656 | tf_op jit(solution)/shard_map/ppermute | solution.py:528
  195.0 2.1 collective-permute-start.18
  199.9 2.6 collective-permute-start.20
  204.4 3.5 %collective-permute-done.21 = f32[288]{0:T(512)S(1)} collective-permute-done((f32[288]{0:T(512)S(1)}, f32[288]{0:T(512)S(1)}, u32[]{:S(2)}, u32[]{:S(2)}) %collective-permute-start.21) | collective-permute-done | bytes 1184 | tf_op jit(solution)/shard_map/ppermute | solution.py:550
  209.4 2.1 collective-permute-start.23
  211.5 2.1 collective-permute-start.28
  214.0 2.2 collective-permute-done.23
  222.2 2.5 collective-permute-start.40
  227.2 2.2 collective-permute-start.27
  232.9 2.2 collective-permute-start.32
  235.2 2.2 collective-permute-start.37
  238.5 2.3 collective-permute-start.38
  240.9 2.1 collective-permute-start.42
  244.1 2.3 collective-permute-start.43
  252.5 2.5 collective-permute-start.13
  256.9 2.6 copy.68
  260.3 1.9 collective-permute-start.46
  264.2 6.1 %collective-permute-done.46 = bf16[8,1,48,384]{3,2,0,1:T(8,128)(2,1)S(1)} collective-permute-done((bf16[8,1,48,384]{3,2,0,1:T(8,128)(2,1)S(1)}, bf16[8,1,48,384]{3,2,0,1:T(8,128)(2,1)S(1)}, u32[]{:S(2)}, u32[]{:S(2)}) %collective-permute-start.46) | collective-permute-done | bytes 294944 | tf_op jit(solution)/shard_map/ppermute | solution.py:528
  272.6 2.3 collective-permute-done.57
  279.2 2.0 collective-permute-done.47
  294.9 2.0 collective-permute-start.60
  299.7 3.0 collective-permute-start.65
  305.4 4.4 %collective-permute-done.66 = bf16[48,384]{1,0:T(8,128)(2,1)S(1)} collective-permute-done((bf16[48,384]{1,0:T(8,128)(2,1)S(1)}, bf16[48,384]{1,0:T(8,128)(2,1)S(1)}, u32[]{:S(2)}, u32[]{:S(2)}) %collective-permute-start.66) | collective-permute-done | bytes 36896 | tf_op jit(solution)/shard_map/ppermute | solution.py:550
  311.8 2.6 copy.67
  (309 shorter events, 112.2 us)
Async XLA Ops:
  1.4 28.8 %collective-permute-start.3 = (f32[768]{0:T(1024)S(1)}, f32[768]{0:T(1024)}, u32[]{:S(2)}, u32[]{:S(2)}) collective-permute-start(f32[768]{0:T(1024)S(1)} %reduce.2), channel_id=1, source_target_pairs={{0,16},{16,0},{1,17},{17,1},{2,18},{18,2},{3,19},{19,3},{4,20},{20... | collective-permute-start | bytes 9224 | tf_op jit(solution)/shard_map/ppermute | solution.py:520
  3.2 14.6 %collective-permute-start = (f32[384]{0:T(512)}, f32[384]{0:T(512)}, u32[]{:S(2)}, u32[]{:S(2)}) collective-permute-start(f32[384]{0:T(512)} %reduce), channel_id=1, source_target_pairs={{0,16},{16,0},{1,17},{17,1},{2,18},{18,2},{3,19},{19,3},{4,20},{20... | collective-permute-start | bytes 4616 | tf_op jit(solution)/shard_map/ppermute | solution.py:520
  4.5 14.2 %collective-permute-start.6 = (f32[384]{0:T(512)}, f32[384]{0:T(512)}, u32[]{:S(2)}, u32[]{:S(2)}) collective-permute-start(f32[384]{0:T(512)} %reduce.4), channel_id=1, source_target_pairs={{0,16},{16,0},{1,17},{17,1},{2,18},{18,2},{3,19},{19,3},{4,20},{20... | collective-permute-start | bytes 4616 | tf_op jit(solution)/shard_map/ppermute | solution.py:520
  5.7 26.7 %collective-permute-start.9 = (f32[1536]{0:T(1024)S(1)}, f32[1536]{0:T(1024)}, u32[]{:S(2)}, u32[]{:S(2)}) collective-permute-start(f32[1536]{0:T(1024)S(1)} %reduce.6), channel_id=1, source_target_pairs={{0,16},{16,0},{1,17},{17,1},{2,18},{18,2},{3,19},{19,3},{4,20},{20... | collective-permute-start | bytes 18440 | tf_op jit(solution)/shard_map/ppermute | solution.py:520
  7.1 12.6 %collective-permute-start.1 = (f32[384]{0:T(512)}, f32[384]{0:T(512)}, u32[]{:S(2)}, u32[]{:S(2)}) collective-permute-start(f32[384]{0:T(512)} %reduce.1), channel_id=1, source_target_pairs={{0,16},{16,0},{1,17},{17,1},{2,18},{18,2},{3,19},{19,3},{4,20},{20... | collective-permute-start | bytes 4616 | tf_op jit(solution)/shard_map/ppermute | solution.py:520
  20.6 15.9 %collective-permute-start.10 = (bf16[1536,384]{1,0:T(8,128)(2,1)S(1)}, bf16[1536,384]{1,0:T(8,128)(2,1)S(1)}, u32[]{:S(2)}, u32[]{:S(2)}) collective-permute-start(bf16[1536,384]{1,0:T(8,128)(2,1)S(1)} %bitcast.264), channel_id=1, source_target_pairs={{0,16},{16,0},{1,17},{17,1},{2,18},{18,2},{3,19},{19,3},{4,20},{20... | collective-permute-start | bytes 3538952 | tf_op jit(solution)/shard_map/ppermute | solution.py:520
  21.6 16.5 %collective-permute-start.8 = (bf16[384,1536]{1,0:T(8,128)(2,1)S(1)}, bf16[384,1536]{1,0:T(8,128)(2,1)S(1)}, u32[]{:S(2)}, u32[]{:S(2)}) collective-permute-start(bf16[384,1536]{1,0:T(8,128)(2,1)S(1)} %bitcast.265), channel_id=1, source_target_pairs={{0,16},{16,0},{1,17},{17,1},{2,18},{18,2},{3,19},{19,3},{4,20},{20... | collective-permute-start | bytes 3538952 | tf_op jit(solution)/shard_map/ppermute | solution.py:520
  22.6 12.5 %collective-permute-start.2 = (bf16[384,1152]{1,0:T(8,128)(2,1)S(1)}, bf16[384,1152]{1,0:T(8,128)(2,1)S(1)}, u32[]{:S(2)}, u32[]{:S(2)}) collective-permute-start(bf16[384,1152]{1,0:T(8,128)(2,1)S(1)} %bitcast.284), channel_id=1, source_target_pairs={{0,16},{16,0},{1,17},{17,1},{2,18},{18,2},{3,19},{19,3},{4,20},{20... | collective-permute-start | bytes 2654216 | tf_op jit(solution)/shard_map/ppermute | solution.py:520
  149.4 105.6 %collective-permute-start.15 = (bf16[1,6,197,384]{3,2,1,0:T(8,128)(2,1)}, bf16[1,6,197,384]{3,2,1,0:T(8,128)(2,1)}, u32[]{:S(2)}, u32[]{:S(2)}) collective-permute-start(bf16[1,6,197,384]{3,2,1,0:T(8,128)(2,1)} %get-tuple-element.57.refs_1_), channel_id=1, source_target_pairs={{0,16},{1,17},{2,18},{3,19},{4,20},{5,21},{6,22},{7,23},{8,24},{9,... | collective-permute-start | bytes 2723336 | tf_op jit(solution)/shard_map/ppermute | solution.py:633
  151.6 158.3 %collective-permute-start.12 = (bf16[1,6,197,384]{3,2,1,0:T(8,128)(2,1)}, bf16[1,6,197,384]{3,2,1,0:T(8,128)(2,1)}, u32[]{:S(2)}, u32[]{:S(2)}) collective-permute-start(bf16[1,6,197,384]{3,2,1,0:T(8,128)(2,1)} %get-tuple-element.46.refs_1_.refs_2_), channel_id=1, source_target_pairs={{16,0},{17,1},{18,2},{19,3},{20,4},{21,5},{22,6},{23,7},{24,8},{25... | collective-permute-start | bytes 2723336 | tf_op jit(solution)/shard_map/ppermute | solution.py:632
  187.6 7.4 %collective-permute-start.17 = (f32[8,1,288]{2,1,0:T(1,128)S(1)}, f32[8,1,288]{2,1,0:T(1,128)S(1)}, u32[]{:S(2)}, u32[]{:S(2)}) collective-permute-start(f32[8,1,288]{2,1,0:T(1,128)S(1)} %fusion.51), channel_id=1, source_target_pairs={{0,1},{1,0},{2,3},{3,2},{4,5},{5,4},{6,7},{7,6},{8,9},{9,8},{10,11... | collective-permute-start | bytes 27656 | tf_op jit(solution)/shard_map/ppermute | solution.py:528
  203.3 5.8 %collective-permute-start.22 = (bf16[16,24,768]{2,1,0:T(8,128)(2,1)S(1)}, bf16[16,24,768]{2,1,0:T(8,128)(2,1)S(1)}, u32[]{:S(2)}, u32[]{:S(2)}) collective-permute-start(bf16[16,24,768]{2,1,0:T(8,128)(2,1)S(1)} %broadcast_select_fusion.7), channel_id=1, source_target_pairs={{0,16},{16,0},{1,17},{17,1},{2,18},{18,2},{3,19},{19,3},{4,20},{20... | collective-permute-start | bytes 1769480 | tf_op jit(solution)/shard_map/ppermute | solution.py:520
  204.4 9.2 %collective-permute-start.33 = (bf16[16,24,768]{2,1,0:T(8,128)(2,1)S(1)}, bf16[16,24,768]{2,1,0:T(8,128)(2,1)S(1)}, u32[]{:S(2)}, u32[]{:S(2)}) collective-permute-start(bf16[16,24,768]{2,1,0:T(8,128)(2,1)S(1)} %broadcast_select_fusion.6), channel_id=1, source_target_pairs={{0,16},{16,0},{1,17},{17,1},{2,18},{18,2},{3,19},{19,3},{4,20},{20... | collective-permute-start | bytes 1769480 | tf_op jit(solution)/shard_map/ppermute | solution.py:520
  209.4 6.8 %collective-permute-start.23 = (bf16[8,1,24,384]{3,2,0,1:T(8,128)(2,1)S(1)}, bf16[8,1,24,384]{3,2,0,1:T(8,128)(2,1)S(1)}, u32[]{:S(2)}, u32[]{:S(2)}) collective-permute-start(bf16[8,1,24,384]{3,2,0,1:T(8,128)(2,1)S(1)} %dynamic-slice_bitcast_fusion.9), channel_id=1, source_target_pairs={{0,1},{1,0},{2,3},{3,2},{4,5},{5,4},{6,7},{7,6},{8,9},{9,8},{10,11... | collective-permute-start | bytes 442376 | tf_op jit(solution)/shard_map/ppermute | solution.py:528
  211.5 6.1 %collective-permute-start.28 = (bf16[4,2,24,384]{3,2,1,0:T(8,128)(2,1)S(1)}, bf16[4,2,24,384]{3,2,1,0:T(8,128)(2,1)S(1)}, u32[]{:S(2)}, u32[]{:S(2)}) collective-permute-start(bf16[4,2,24,384]{3,2,1,0:T(8,128)(2,1)S(1)} %dynamic-slice_bitcast_fusion.8), channel_id=1, source_target_pairs={{0,2},{1,3},{2,0},{3,1},{4,6},{5,7},{6,4},{7,5},{8,10},{9,11},{10,... | collective-permute-start | bytes 442376 | tf_op jit(solution)/shard_map/ppermute | solution.py:528
  246.4 13.1 %collective-permute-start.45 = (bf16[16,96,384]{2,1,0:T(8,128)(2,1)S(1)}, bf16[16,96,384]{2,1,0:T(8,128)(2,1)S(1)}, u32[]{:S(2)}, u32[]{:S(2)}) collective-permute-start(bf16[16,96,384]{2,1,0:T(8,128)(2,1)S(1)} %copy-done.11), channel_id=1, source_target_pairs={{0,16},{16,0},{1,17},{17,1},{2,18},{18,2},{3,19},{19,3},{4,20},{20... | collective-permute-start | bytes 3538952 | tf_op jit(solution)/shard_map/ppermute | solution.py:520
  246.5 5.9 %collective-permute-start.14 = (bf16[1,6,197,384]{3,2,1,0:T(8,128)(2,1)S(1)}, bf16[1,6,197,384]{3,2,1,0:T(8,128)(2,1)S(1)}, u32[]{:S(2)}, u32[]{:S(2)}) collective-permute-start(bf16[1,6,197,384]{3,2,1,0:T(8,128)(2,1)S(1)} %copy-done.13), channel_id=1, source_target_pairs={{16,0},{17,1},{18,2},{19,3},{20,4},{21,5},{22,6},{23,7},{24,8},{25... | collective-permute-start | bytes 2723336 | tf_op jit(solution)/shard_map/ppermute | solution.py:632
  251.0 11.8 %collective-permute-start.56 = (bf16[16,96,384]{2,1,0:T(8,128)(2,1)S(1)}, bf16[16,96,384]{2,1,0:T(8,128)(2,1)S(1)}, u32[]{:S(2)}, u32[]{:S(2)}) collective-permute-start(bf16[16,96,384]{2,1,0:T(8,128)(2,1)S(1)} %bitcast_select_fusion), channel_id=1, source_target_pairs={{0,16},{16,0},{1,17},{17,1},{2,18},{18,2},{3,19},{19,3},{4,20},{20... | collective-permute-start | bytes 3538952 | tf_op jit(solution)/shard_map/ppermute | solution.py:520
  252.5 57.5 %collective-permute-start.13 = (bf16[1,6,197,384]{3,2,1,0:T(8,128)(2,1)S(1)}, bf16[1,6,197,384]{3,2,1,0:T(8,128)(2,1)S(1)}, u32[]{:S(2)}, u32[]{:S(2)}) collective-permute-start(bf16[1,6,197,384]{3,2,1,0:T(8,128)(2,1)S(1)} %copy-done.12), channel_id=1, source_target_pairs={{0,16},{1,17},{2,18},{3,19},{4,20},{5,21},{6,22},{7,23},{8,24},{9,... | collective-permute-start | bytes 2723336 | tf_op jit(solution)/shard_map/ppermute | solution.py:633
  260.3 10.0 %collective-permute-start.46 = (bf16[8,1,48,384]{3,2,0,1:T(8,128)(2,1)S(1)}, bf16[8,1,48,384]{3,2,0,1:T(8,128)(2,1)S(1)}, u32[]{:S(2)}, u32[]{:S(2)}) collective-permute-start(bf16[8,1,48,384]{3,2,0,1:T(8,128)(2,1)S(1)} %dynamic-slice_bitcast_fusion.3), channel_id=1, source_target_pairs={{0,1},{1,0},{2,3},{3,2},{4,5},{5,4},{6,7},{7,6},{8,9},{9,8},{10,11... | collective-permute-start | bytes 884744 | tf_op jit(solution)/shard_map/ppermute | solution.py:528
  262.2 9.0 %collective-permute-start.51 = (bf16[4,2,48,384]{3,2,1,0:T(8,128)(2,1)S(1)}, bf16[4,2,48,384]{3,2,1,0:T(8,128)(2,1)S(1)}, u32[]{:S(2)}, u32[]{:S(2)}) collective-permute-start(bf16[4,2,48,384]{3,2,1,0:T(8,128)(2,1)S(1)} %dynamic-slice_bitcast_fusion.2), channel_id=1, source_target_pairs={{0,2},{1,3},{2,0},{3,1},{4,6},{5,7},{6,4},{7,5},{8,10},{9,11},{10,... | collective-permute-start | bytes 884744 | tf_op jit(solution)/shard_map/ppermute | solution.py:528
  263.7 11.2 %collective-permute-start.57 = (bf16[8,1,48,384]{3,2,0,1:T(8,128)(2,1)S(1)}, bf16[8,1,48,384]{3,2,0,1:T(8,128)(2,1)S(1)}, u32[]{:S(2)}, u32[]{:S(2)}) collective-permute-start(bf16[8,1,48,384]{3,2,0,1:T(8,128)(2,1)S(1)} %dynamic-slice_bitcast_fusion.1), channel_id=1, source_target_pairs={{0,1},{1,0},{2,3},{3,2},{4,5},{5,4},{6,7},{7,6},{8,9},{9,8},{10,11... | collective-permute-start | bytes 884744 | tf_op jit(solution)/shard_map/ppermute | solution.py:528
  270.3 8.2 %collective-permute-start.62 = (bf16[4,2,48,384]{3,2,1,0:T(8,128)(2,1)S(1)}, bf16[4,2,48,384]{3,2,1,0:T(8,128)(2,1)S(1)}, u32[]{:S(2)}, u32[]{:S(2)}) collective-permute-start(bf16[4,2,48,384]{3,2,1,0:T(8,128)(2,1)S(1)} %dynamic-slice_bitcast_fusion), channel_id=1, source_target_pairs={{0,2},{1,3},{2,0},{3,1},{4,6},{5,7},{6,4},{7,5},{8,10},{9,11},{10,... | collective-permute-start | bytes 884744 | tf_op jit(solution)/shard_map/ppermute | solution.py:528
  271.2 10.1 %collective-permute-start.47 = (bf16[4,1,48,384]{3,2,0,1:T(8,128)(2,1)S(1)}, bf16[4,1,48,384]{3,2,0,1:T(8,128)(2,1)S(1)}, u32[]{:S(2)}, u32[]{:S(2)}) collective-permute-start(bf16[4,1,48,384]{3,2,0,1:T(8,128)(2,1)S(1)} %dynamic-slice_bitcast_fusion.5), channel_id=1, source_target_pairs={{0,2},{1,3},{2,0},{3,1},{4,6},{5,7},{6,4},{7,5},{8,10},{9,11},{10,... | collective-permute-start | bytes 442376 | tf_op jit(solution)/shard_map/ppermute | solution.py:528
  274.9 7.6 %collective-permute-start.52 = (bf16[4,1,48,384]{3,2,1,0:T(8,128)(2,1)S(1)}, bf16[4,1,48,384]{3,2,1,0:T(8,128)(2,1)S(1)}, u32[]{:S(2)}, u32[]{:S(2)}) collective-permute-start(bf16[4,1,48,384]{3,2,1,0:T(8,128)(2,1)S(1)} %constant_dynamic-slice_fusion.1), channel_id=1, source_target_pairs={{0,1},{1,0},{2,3},{3,2},{4,5},{5,4},{6,7},{7,6},{8,9},{9,8},{10,11... | collective-permute-start | bytes 442376 | tf_op jit(solution)/shard_map/ppermute | solution.py:528
  283.6 6.0 %collective-permute-start.49 = (bf16[48,384]{1,0:T(8,128)(2,1)S(1)}, bf16[48,384]{1,0:T(8,128)(2,1)S(1)}, u32[]{:S(2)}, u32[]{:S(2)}) collective-permute-start(bf16[48,384]{1,0:T(8,128)(2,1)S(1)} %get-tuple-element.162), channel_id=1, source_target_pairs={{0,8},{1,9},{2,10},{3,11},{4,12},{5,13},{6,14},{7,15},{8,0},{9,1},... | collective-permute-start | bytes 110600 | tf_op jit(solution)/shard_map/ppermute | solution.py:550
  286.4 6.0 %collective-permute-start.50 = (bf16[48,384]{1,0:T(8,128)(2,1)S(1)}, bf16[48,384]{1,0:T(8,128)(2,1)S(1)}, u32[]{:S(2)}, u32[]{:S(2)}) collective-permute-start(bf16[48,384]{1,0:T(8,128)(2,1)S(1)} %get-tuple-element.161), channel_id=1, source_target_pairs={{0,12},{1,13},{2,14},{3,15},{4,8},{5,9},{6,10},{7,11},{8,4},{9,5},... | collective-permute-start | bytes 110600 | tf_op jit(solution)/shard_map/ppermute | solution.py:550
  292.4 5.9 %collective-permute-start.55 = (bf16[48,384]{1,0:T(8,128)(2,1)S(1)}, bf16[48,384]{1,0:T(8,128)(2,1)S(1)}, u32[]{:S(2)}, u32[]{:S(2)}) collective-permute-start(bf16[48,384]{1,0:T(8,128)(2,1)S(1)} %get-tuple-element.164), channel_id=1, source_target_pairs={{0,12},{1,13},{2,14},{3,15},{4,8},{5,9},{6,10},{7,11},{8,4},{9,5},... | collective-permute-start | bytes 110600 | tf_op jit(solution)/shard_map/ppermute | solution.py:550
  293.9 5.7 %collective-permute-start.59 = (bf16[48,384]{1,0:T(8,128)(2,1)S(1)}, bf16[48,384]{1,0:T(8,128)(2,1)S(1)}, u32[]{:S(2)}, u32[]{:S(2)}) collective-permute-start(bf16[48,384]{1,0:T(8,128)(2,1)S(1)} %get-tuple-element.166), channel_id=1, source_target_pairs={{0,4},{1,5},{2,6},{3,7},{4,0},{5,1},{6,2},{7,3},{8,12},{9,13},{10,... | collective-permute-start | bytes 110600 | tf_op jit(solution)/shard_map/ppermute | solution.py:550
  298.3 5.8 %collective-permute-start.61 = (bf16[48,384]{1,0:T(8,128)(2,1)S(1)}, bf16[48,384]{1,0:T(8,128)(2,1)S(1)}, u32[]{:S(2)}, u32[]{:S(2)}) collective-permute-start(bf16[48,384]{1,0:T(8,128)(2,1)S(1)} %get-tuple-element.167), channel_id=1, source_target_pairs={{0,12},{1,13},{2,14},{3,15},{4,8},{5,9},{6,10},{7,11},{8,4},{9,5},... | collective-permute-start | bytes 110600 | tf_op jit(solution)/shard_map/ppermute | solution.py:550
  299.6 5.7 %collective-permute-start.64 = (bf16[48,384]{1,0:T(8,128)(2,1)S(1)}, bf16[48,384]{1,0:T(8,128)(2,1)S(1)}, u32[]{:S(2)}, u32[]{:S(2)}) collective-permute-start(bf16[48,384]{1,0:T(8,128)(2,1)S(1)} %get-tuple-element.169), channel_id=1, source_target_pairs={{0,4},{1,5},{2,6},{3,7},{4,0},{5,1},{6,2},{7,3},{8,12},{9,13},{10,... | collective-permute-start | bytes 110600 | tf_op jit(solution)/shard_map/ppermute | solution.py:550
  304.0 5.8 %collective-permute-start.66 = (bf16[48,384]{1,0:T(8,128)(2,1)S(1)}, bf16[48,384]{1,0:T(8,128)(2,1)S(1)}, u32[]{:S(2)}, u32[]{:S(2)}) collective-permute-start(bf16[48,384]{1,0:T(8,128)(2,1)S(1)} %get-tuple-element.170), channel_id=1, source_target_pairs={{0,12},{1,13},{2,14},{3,15},{4,8},{5,9},{6,10},{7,11},{8,4},{9,5},... | collective-permute-start | bytes 110600 | tf_op jit(solution)/shard_map/ppermute | solution.py:550
  (57 other events, 355.4 us)

commit v2 on v0

v2 whole, which is shorter than its diff:
```python
import jax
import jax.numpy as jnp
from jax import lax
from jax.experimental import pallas as pl
from jax.experimental.pallas import tpu as pltpu
from jax.sharding import PartitionSpec as P

HEAD = 64
EPSILON = 1e-06
BF16 = jnp.bfloat16
F32 = jnp.float32
GROUP = 2
VMEM_LIMIT = 58 * 1024 * 1024


def dot(a, b):
    return lax.dot_general(a, b, (((1,), (0,)), ((), ())), preferred_element_type=F32)


def dot_nt(a, b):
    return lax.dot_general(a, b, (((1,), (1,)), ((), ())), preferred_element_type=F32)


def dot_tn(a, b):
    return lax.dot_general(a, b, (((0,), (0,)), ((), ())), preferred_element_type=F32)


def normalized(rows):
    centered = rows - jnp.mean(rows, axis=-1, keepdims=True)
    spread = jnp.mean(centered * centered, axis=-1, keepdims=True)
    inverse = lax.rsqrt(spread + EPSILON)
    return centered * inverse, inverse


def norm_backward(rows, grad, gain):
    hat, inverse = normalized(rows)
    scaled = grad * gain
    inner = jnp.mean(scaled * hat, axis=-1, keepdims=True)
    dx = inverse * (scaled - jnp.mean(scaled, axis=-1, keepdims=True) - hat * inner)
    return dx, grad * hat


def gelu_and_slope(x):
    bell = jnp.exp(x * x * -0.5)
    t = 1.0 / (1.0 + jnp.abs(x) * (0.3275911 * 0.7071067811865476))
    poly = t * (
        0.5 * 0.254829592
        + t
        * (
            0.5 * -0.284496736
            + t * (0.5 * 1.421413741 + t * (0.5 * -1.453152027 + t * (0.5 * 1.061405429)))
        )
    )
    tail = poly * bell
    cdf = jnp.where(x >= 0.0, 1.0 - tail, tail)
    return x * cdf, cdf + x * (bell * 0.3989422804014327)


def fold(rows):
    total = rows[0:8]
    for at in range(8, rows.shape[0], 8):
        total = total + rows[at : at + 8]
    return total


def row_chunks(total, size=32):
    return [(at, min(size, total - at)) for at in range(0, total, size)]


def layers_kernel(
    padded,
    keys,
    meta,
    h_ref,
    cot_ref,
    own_vec,
    got_vec,
    own_qkv,
    own_out,
    own_up,
    own_down,
    got_qkv,
    got_out,
    got_up,
    got_down,
    mine_ref,
    away_ref,
    mine_wide,
    away_wide,
    mine_tall,
    away_tall,
    w_qkv,
    w_out,
    w_up,
    w_down,
    vecs,
    hidden,
    normed,
    joined,
    weights,
    attended,
    middle,
    second,
    active,
    slope,
    before,
    grad_out,
    grad_low,
    grad_before,
    grad_joined,
    grad_norm,
    sum_up,
    sum_down,
    sum_att,
    vec_one,
    vec_up,
    vec_qkv,
    wide,
    tall,
    load_sem,
    store_sem,
):
    step = pl.program_id(0)
    count = meta[0]
    core = meta[1]
    tokens, features = h_ref.shape[2:]
    heads = features // HEAD
    rows = GROUP * padded
    units = w_up.shape[2]
    own = (own_qkv, own_out, own_up, own_down)
    got = (got_qkv, got_out, got_up, got_down)
    held = (w_qkv, w_out, w_up, w_down)
    at_g1, at_b1, at_qkv = 0, features, 2 * features
    at_bo, at_g2, at_b2, at_bd, at_up = (n * features for n in (5, 6, 7, 8, 9))

    def vec(layer, at, size=features):
        return vecs[pl.ds(layer, 1), at : at + size]

    def load(source, n, layer):
        return pltpu.make_async_copy(source[n].at[0], held[n].at[layer], load_sem.at[layer, n])

    @pl.when(step == 0)
    def _():
        for layer in range(2):
            for n in range(4):

                @pl.when(core == layer)
                def _():
                    load(own, n, layer).start()

                @pl.when(core != layer)
                def _():
                    load(got, n, layer).start()

        for layer in range(2):
            mine = jnp.full(own_vec.shape, core == layer)
            vecs[layer : layer + 1] = jnp.where(mine, own_vec[...], got_vec[...])
        for ref in (sum_up, sum_down, sum_att, vec_one, vec_up, vec_qkv):
            for layer in range(2):
                ref[layer] = jnp.zeros(ref.shape[1:], F32)
        for layer in range(2):
            for j in range(GROUP):
                joined[layer, j * keys + padded : (j + 1) * keys] = jnp.zeros(
                    (keys - padded, 3 * features), BF16
                )

    def leave(layer, kind, j, value):
        @pl.when(core == layer)
        def _():
            mine_ref[kind, j] = value

        @pl.when(core != layer)
        def _():
            away_ref[kind, j] = value

    lane = lax.broadcasted_iota(jnp.int32, (padded, 2 * HEAD), 1)

    def forward(layer):
        @pl.when(step == 0)
        def _():
            for n in range(4):
                load(own, n, layer).wait()

        for at, size in row_chunks(rows):
            hat, _ = normalized(hidden[layer, at : at + size])
            value = hat * vec(layer, at_g1) + vec(layer, at_b1)
            normed[layer, at : at + size] = value.astype(BF16)
        for j in range(GROUP):
            lines = normed[layer, j * padded : (j + 1) * padded]
            for part in range(3):
                columns = slice(part * features, (part + 1) * features)
                value = dot(lines, w_qkv[layer, :, columns]) + vec(
                    layer, at_qkv + part * features
                )
                value = value.astype(BF16)
                if part == 0:
                    value = value * jnp.asarray(HEAD**-0.5, BF16)
                joined[layer, j * keys : j * keys + padded, columns] = value
        real = lax.broadcasted_iota(jnp.int32, (padded, keys), 1) < tokens
        for j in range(GROUP):
            for pair in range(heads // 2):
                at = pair * 2 * HEAD
                span = slice(j * keys, (j + 1) * keys)
                q = joined[layer, j * keys : j * keys + padded, at : at + 2 * HEAD]
                k = joined[layer, span, features + at : features + at + 2 * HEAD]
                v = joined[layer, span, 2 * features + at : 2 * features + at + 2 * HEAD]
                parts = []
                for half in range(2):
                    mine = (lane < HEAD) if half == 0 else (lane >= HEAD)
                    s = dot_nt(jnp.where(mine, q, jnp.zeros_like(q)), k)
                    s = jnp.where(real, s, -1e30)
                    e = jnp.exp(s - jnp.max(s, axis=-1, keepdims=True))
                    p = (e * (1.0 / jnp.sum(e, axis=-1, keepdims=True))).astype(BF16)
                    weights[layer, j, 2 * pair + half] = p
                    parts.append(dot(p, v))
                attended[layer, j * padded : (j + 1) * padded, at : at + 2 * HEAD] = jnp.where(
                    lane < HEAD, parts[0], parts[1]
                ).astype(BF16)
        middle[layer] = dot(attended[layer], w_out[layer])
        for at, size in row_chunks(rows):
            value = middle[layer, at : at + size] + hidden[layer, at : at + size]
            value = value + vec(layer, at_bo)
            middle[layer, at : at + size] = value
            hat, _ = normalized(value)
            value = hat * vec(layer, at_g2) + vec(layer, at_b2)
            second[layer, at : at + size] = value.astype(BF16)
        width = features
        for j in range(GROUP):
            lines = slice(j * padded, (j + 1) * padded)
            for c in range(units // width):
                columns = slice(c * width, (c + 1) * width)
                before[lines, columns] = dot(second[layer, lines], w_up[layer, :, columns])
                for at, size in row_chunks(padded, 16):
                    piece = slice(j * padded + at, j * padded + at + size)
                    value, change = gelu_and_slope(
                        before[piece, columns] + vec(layer, at_up + c * width, width)
                    )
                    active[layer, piece, columns] = value.astype(BF16)
                    slope[layer, piece, columns] = change.astype(BF16)
            keep = jnp.where(step * GROUP + j < count, 1.0, 0.0)
            result = dot(active[layer, lines], w_down[layer]) + middle[layer, lines]
            result = ((result + vec(layer, at_bd)) * keep).astype(BF16)
            leave(layer, 0, j, result[:tokens])
            hidden[layer + 1, lines] = result.astype(F32)

    def backward(layer):
        for at, size in row_chunks(rows):
            value = grad_out[at : at + size]
            grad_low[at : at + size] = value.astype(BF16)
            vec_one[layer, 0:8] += fold(value)
        width = features
        sum_down[layer] += dot_tn(grad_low[...], active[layer])
        for j in range(GROUP):
            lines = slice(j * padded, (j + 1) * padded)
            for c in range(units // width):
                columns = slice(c * width, (c + 1) * width)
                piece = dot_nt(grad_low[lines], w_down[layer, columns, :])
                piece = (piece * slope[layer, lines, columns].astype(F32)).astype(BF16)
                grad_before[lines, columns] = piece
                vec_up[layer, :, columns] += fold(piece.astype(F32))
            grad_norm[lines] = dot_nt(grad_before[lines], w_up[layer])
        sum_up[layer] += dot_tn(second[layer], grad_before[...])
        for at, size in row_chunks(rows):
            grad = grad_norm[at : at + size]
            dx, by_hat = norm_backward(middle[layer, at : at + size], grad, vec(layer, at_g2))
            vec_one[layer, 8:16] += fold(by_hat)
            vec_one[layer, 16:24] += fold(grad)
            value = grad_out[at : at + size] + dx
            grad_out[at : at + size] = value
            value = value.astype(BF16)
            grad_low[at : at + size] = value
            vec_one[layer, 24:32] += fold(value.astype(F32))
        sum_att[layer, :, 3 * features :] += dot_tn(attended[layer], grad_low[...])
        grad_low[...] = dot_nt(grad_low[...], w_out[layer]).astype(BF16)
        for j in range(GROUP):
            lines = slice(j * padded, (j + 1) * padded)
            for pair in range(heads // 2):
                at = pair * 2 * HEAD
                span = slice(j * keys, (j + 1) * keys)
                q = joined[layer, j * keys : j * keys + padded, at : at + 2 * HEAD]
                k = joined[layer, span, features + at : features + at + 2 * HEAD]
                v = joined[layer, span, 2 * features + at : 2 * features + at + 2 * HEAD]
                ga = grad_low[lines, at : at + 2 * HEAD]
                gq, gk, gv = [], [], []
                for half in range(2):
                    mine = (lane < HEAD) if half == 0 else (lane >= HEAD)
                    gp = dot_nt(jnp.where(mine, ga, jnp.zeros_like(ga)), v)
                    p = weights[layer, j, 2 * pair + half]
                    p_wide = p.astype(F32)
                    by = p_wide * gp
                    gs = (by - p_wide * jnp.sum(by, axis=-1, keepdims=True)).astype(BF16)
                    gq.append(dot(gs, k))
                    gk.append(dot_tn(gs, q)[:padded])
                    gv.append(dot_tn(p, ga)[:padded])
                left = lane < HEAD
                parts = (
                    jnp.where(left, gq[0], gq[1]) * HEAD**-0.5,
                    jnp.where(left, gk[0], gk[1]),
                    jnp.where(left, gv[0], gv[1]),
                )
                for n, part in enumerate(parts):
                    column = n * features + at
                    part = part.astype(BF16)
                    grad_joined[lines, column : column + 2 * HEAD] = part
                    vec_qkv[layer, :, column : column + 2 * HEAD] += fold(part.astype(F32))
        sum_att[layer, :, : 3 * features] += dot_tn(normed[layer], grad_joined[...])
        grad_norm[...] = dot_nt(grad_joined[...], w_qkv[layer])
        for at, size in row_chunks(rows):
            grad = grad_norm[at : at + size]
            dx, by_hat = norm_backward(hidden[layer, at : at + size], grad, vec(layer, at_g1))
            vec_one[layer, 32:40] += fold(by_hat)
            vec_one[layer, 40:48] += fold(grad)
            value = grad_out[at : at + size] + dx
            grad_out[at : at + size] = value.astype(BF16).astype(F32)
        for j in range(GROUP):
            leave(layer, 1, j, grad_out[j * padded : j * padded + tokens].astype(BF16))

    @pl.when(step * GROUP >= count)
    def _():
        mine_ref[...] = jnp.zeros_like(mine_ref)
        away_ref[...] = jnp.zeros_like(away_ref)

    @pl.when(step * GROUP < count)
    def _():
        for j in range(GROUP):
            tail = slice(j * padded + padded - 16, (j + 1) * padded)
            hidden[0, tail] = jnp.zeros((16, features), F32)
            hidden[0, j * padded : j * padded + tokens] = h_ref[0, j].astype(F32)
        lax.fori_loop(0, 2, lambda layer, carry: (forward(layer), carry)[1], 0)
        for j in range(GROUP):
            keep = jnp.where(step * GROUP + j < count, 1.0, 0.0)
            tail = slice(j * padded + padded - 16, (j + 1) * padded)
            grad_out[tail] = jnp.zeros((16, features), F32)
            grad_out[j * padded : j * padded + tokens] = cot_ref[0, j].astype(F32) * keep
        lax.fori_loop(0, 2, lambda at, carry: (backward(1 - at), carry)[1], 0)

    def store(layer, kind, target):
        stage = (wide, tall)[kind].at[layer]
        return pltpu.make_async_copy(stage, target, store_sem.at[layer, kind])

    @pl.when(step == pl.num_programs(0) - 1)
    def _():
        for layer in range(2):
            for c in range(units // features):
                columns = slice(c * features, (c + 1) * features)
                tall[layer, columns, :] = sum_down[layer, :, columns].T.astype(BF16)
            wide[layer, :, :units] = sum_up[layer].astype(BF16)
            wide[layer, :, units : units + 4 * features] = sum_att[layer].astype(BF16)
            line = lax.broadcasted_iota(jnp.int32, (128, features), 0)
            plain = jnp.zeros((128, features), F32)
            for n, group in enumerate((4, 5, 3, 1, 2, 0)):
                total = jnp.sum(vec_one[layer, 8 * group : 8 * group + 8], axis=0, keepdims=True)
                plain = plain + jnp.where(line == n, total, 0.0)
            qkv = jnp.sum(vec_qkv[layer], axis=0, keepdims=True)
            qv = jnp.concatenate([qkv[:, :features], qkv[:, 2 * features :]], axis=1)
            up = jnp.sum(vec_up[layer], axis=0, keepdims=True)
            columns = jnp.zeros((features, 128), F32)
            for first_line, total in ((0, plain), (6, qv), (8, up)):
                size = total.shape[1]
                each = size // features
                position = lax.broadcasted_iota(jnp.int32, (128, size), 1)
                row = lax.broadcasted_iota(jnp.int32, (128, size), 0)
                if each > 1:
                    total = jnp.where(row - first_line == position % each, total, 0.0)
                target = lax.broadcasted_iota(jnp.int32, (features, size), 0)
                source = lax.broadcasted_iota(jnp.int32, (features, size), 1)
                pick = jnp.where(source // each == target, 1.0, 0.0).astype(BF16)
                columns = columns + dot_nt(pick, total.astype(BF16))
            wide[layer, :, units + 4 * features :] = columns.astype(BF16)
            for kind, (mine, away) in enumerate(((mine_wide, away_wide), (mine_tall, away_tall))):

                @pl.when(core == layer)
                def _():
                    store(layer, kind, mine).start()

                @pl.when(core != layer)
                def _():
                    store(layer, kind, away).start()

        for layer in range(2):
            for kind, mine in enumerate((mine_wide, mine_tall)):
                store(layer, kind, mine).wait()


def run_layers(meta, inputs, cotangent, vectors, weights):
    slots, tokens, features = inputs.shape[1:]
    padded = -(-tokens // 16) * 16
    keys = -(-tokens // 128) * 128
    heads = features // HEAD
    steps = slots // GROUP
    block = GROUP * padded
    units = weights[0][2].shape[2]
    packed = vectors[0].shape[1]
    wide = units + 4 * features + 128
    images = pl.BlockSpec((1, GROUP, tokens, features), lambda i, meta: (meta[1], i, 0, 0))
    kinds = pl.BlockSpec((2, GROUP, tokens, features), lambda i, meta: (0, i, 0, 0))
    vector = pl.BlockSpec((1, packed), lambda i, meta: (0, 0))
    anywhere = pl.BlockSpec(memory_space=pl.ANY)
    both = (
        ((features, 3 * features), BF16),
        ((features, features), BF16),
        ((features, units), BF16),
        ((units, features), BF16),
        ((packed,), F32),
    )
    saved = (
        ((block, features), BF16),
        ((GROUP * keys, 3 * features), BF16),
        ((GROUP, heads, padded, keys), BF16),
        ((block, features), BF16),
        ((block, features), F32),
        ((block, features), BF16),
        ((block, units), BF16),
        ((block, units), BF16),
    )
    sums = (
        ((features, units), F32),
        ((features, units), F32),
        ((features, 4 * features), F32),
        ((48, features), F32),
        ((8, units), F32),
        ((8, 3 * features), F32),
        ((features, wide), BF16),
        ((units, features), BF16),
    )

    def two(shapes):
        return [pltpu.VMEM((2,) + shape, kind) for shape, kind in shapes]

    scratch = (
        two(both)
        + [pltpu.VMEM((3, block, features), F32)]
        + two(saved)
        + [
            pltpu.VMEM((block, units), F32),
            pltpu.VMEM((block, features), F32),
            pltpu.VMEM((block, features), BF16),
            pltpu.VMEM((block, units), BF16),
            pltpu.VMEM((block, 3 * features), BF16),
            pltpu.VMEM((block, features), F32),
        ]
        + two(sums)
        + [pltpu.SemaphoreType.DMA((2, 4)), pltpu.SemaphoreType.DMA((2, 2))]
    )
    return pl.pallas_call(
        lambda *refs: layers_kernel(padded, keys, *refs),
        grid_spec=pltpu.PrefetchScalarGridSpec(
            num_scalar_prefetch=1,
            grid=(steps,),
            in_specs=[images, images, vector, vector] + [anywhere] * 8,
            out_specs=[kinds, kinds] + [anywhere] * 4,
            scratch_shapes=scratch,
        ),
        out_shape=[jax.ShapeDtypeStruct((2, slots, tokens, features), BF16)] * 2
        + [jax.ShapeDtypeStruct((features, wide), BF16)] * 2
        + [jax.ShapeDtypeStruct((units, features), BF16)] * 2,
        compiler_params=pltpu.CompilerParams(
            vmem_limit_bytes=VMEM_LIMIT, dimension_semantics=("arbitrary",)
        ),
        cost_estimate=pl.CostEstimate(
            flops=80_000_000_000, bytes_accessed=30_000_000, transcendentals=0
        ),
    )(meta, inputs, cotangent, *vectors, *weights[0], *weights[1])


def swap_cores(block):
    return lax.ppermute(block, "segment", [(0, 1), (1, 0)])


def reduce_shards(mine, got, orders, first):
    dp = lax.axis_size("dp")
    me = lax.axis_index("dp")
    bits = dp.bit_length() - 1
    rest = (mine.shape[0] // dp, mine.shape[1])
    block = mine.astype(F32) + got.astype(F32)
    held = [list(range(bits)) for _ in orders]
    for n in range(bits):
        below = [left.index(order[n]) for order, left in zip(orders, held)]
        bit = [(me >> order[n]) & 1 for order in orders]
        for order, left in zip(orders, held):
            left.remove(order[n])

        def part(at, index):
            view = block.reshape((-1, 2, 1 << at) + rest)
            taken = lax.dynamic_index_in_dim(view, index, 1, keepdims=False)
            return taken.reshape((-1,) + rest)

        if below[0] == below[1]:
            mine = jnp.where(first, bit[0], bit[1])
            keep, send = part(below[0], mine), part(below[0], 1 - mine)
        else:
            keep = jnp.where(first, part(below[0], bit[0]), part(below[1], bit[1]))
            send = jnp.where(first, part(below[0], 1 - bit[0]), part(below[1], 1 - bit[1]))
        route = [
            (core * dp + i, core * dp + (i ^ (1 << order[n])))
            for core, order in enumerate(orders)
            for i in range(dp)
        ]
        arrived = lax.ppermute(send.astype(BF16), ("segment", "dp"), route)
        block = keep.astype(F32) + arrived.astype(F32)
        if n < bits - 1:
            block = block.astype(BF16)
    return block.reshape(rest)


def on_device(inputs, image_count, cotangent, *params):
    dp = lax.axis_size("dp")
    core = lax.axis_index("segment")
    first = core == 0
    features = inputs.shape[3]
    g1, b1, w_qkv, b_qv, w_out, b_out, g2, b2, w_up, b_up, w_down, b_down = params
    units = w_up.shape[2]
    own_weights = (w_qkv, w_out, w_up, w_down)
    got_weights = tuple(swap_cores(w) for w in own_weights)
    zeros = jnp.zeros((1, features), F32)
    own_vec = jnp.concatenate(
        [g1, b1, b_qv[:, :features], zeros, b_qv[:, features:], b_out, g2, b2, b_down, b_up], axis=1
    )
    got_vec = swap_cores(own_vec)
    count = lax.dynamic_index_in_dim(image_count[:, 0], core, 0, keepdims=False)
    meta = jnp.stack([count, core.astype(jnp.int32)])
    mine, away, mine_wide, away_wide, mine_tall, away_tall = run_layers(
        meta, inputs, cotangent, (own_vec, got_vec), (own_weights, got_weights)
    )
    got_wide = swap_cores(away_wide)
    got_tall = swap_cores(away_tall)
    got = swap_cores(away)
    bits = dp.bit_length() - 1
    near = list(range(min(bits, 3)))
    far = list(range(len(near), bits))

    def turned(by):
        return near[by % len(near) :] + near[: by % len(near)] + far

    wide = reduce_shards(mine_wide, got_wide, (turned(0), turned(2)), first)
    tall = reduce_shards(mine_tall, got_tall, (turned(1), turned(1)), first)
    both = jnp.stack([jnp.where(first, mine, got), jnp.where(first, got, mine)], axis=1)
    share = features // dp
    g_up = wide[:, :units]
    g_qkv = wide[:, units : units + 3 * features]
    g_out = wide[:, units + 3 * features : units + 4 * features]
    columns = wide[:, units + 4 * features :]
    ln1_gain, ln1_bias, g_bo, ln2_gain, ln2_bias, g_bd = (columns[:, n] for n in range(6))
    g_bqv = columns[:, 6:8].reshape(2 * share)
    g_bup = columns[:, 8 : 8 + units // features].reshape(-1)
    outs = (ln1_gain, ln1_bias, g_qkv, g_bqv, g_out, g_bo, ln2_gain, ln2_bias, g_up, g_bup, tall, g_bd)
    return (both[0][None], both[1][None]) + tuple(o[None] for o in outs)


def solution(mesh):
    in_specs = (
        P(None, "dp", None, None),
        P(None, "dp"),
        P(None, "dp", None, None),
        P("segment", None),
        P("segment", None),
        P("segment", None, None),
        P("segment", None),
        P("segment", None, None),
        P("segment", None),
        P("segment", None),
        P("segment", None),
        P("segment", None, None),
        P("segment", None),
        P("segment", None, None),
        P("segment", None),
    )
    out_specs = (
        P("segment", None, "dp", None, None),
        P("segment", None, "dp", None, None),
        P("segment", "dp"),
        P("segment", "dp"),
        P("segment", "dp", None),
        P("segment", "dp"),
        P("segment", "dp", None),
        P("segment", "dp"),
        P("segment", "dp"),
        P("segment", "dp"),
        P("segment", "dp", None),
        P("segment", "dp"),
        P("segment", "dp", None),
        P("segment", "dp"),
    )
    return jax.shard_map(
        on_device, mesh=mesh, in_specs=in_specs, out_specs=out_specs, check_vma=False
    )
```

time: 885 us -> 191 us (0.22)
  waiting for transfers between devices: 361 us -> 29.5 us
  matrix products: 225 us -> 0 us
  other arithmetic: 110 us -> 10.8 us
  blocking collectives: 78 us -> 0 us
  starting transfers between devices: 7.63 us -> 79.8 us
  local copies, waits for them, and re-layouts: 78.7 us -> 26.2 us
  Pallas kernels: 0 us -> 43.5 us
  between operations: 18.4 us -> 0.87 us
    reduce_scatter x2 -> x0, waiting for transfers between devices: 265 us -> none  [on_device(): totals = lax.psum_scatter(totals, 'dp', scatter_dimension=0, tiled=True)]
    dot_general x57 -> x0, matrix products: 225 us -> none  [the longest x3 63.2 us: backward(): jnp.einsum('nsd,fd->nsf', down_in, w_down, preferred_element_type=jnp.flo...]
    unnamed x6 -> x0, waiting for transfers between devices: 96.5 us -> none
    unnamed x1 -> x0, blocking collectives: 78 us -> none
    ppermute x4 -> x16, starting transfers between devices: 7.3 us -> 79.8 us  [the longest x8 66.7 us: swap_cores(): return lax.ppermute(block, 'segment', [(0, 1), (1, 0)])]
    convert_element_type x9 -> x7, other arithmetic: 66.6 us -> 4.05 us  [the longest x6 2.34 us: reduce_shards(): block = block.astype(BF16)]
    pallas_call x0 -> x1, Pallas kernels: none -> 43.5 us  [run_layers(): pl.pallas_call(lambda *refs: layers_kernel(padded, keys, *refs), grid_spe...]
    reduce_sum x31 -> x0, other arithmetic: 36 us -> none  [the longest x9 8.3 us: norm_rows(): centered = rows - jnp.mean(rows, axis=-1, keepdims=True)]
  transfers between devices with their start and end apart: 8 -> 16, of which waited for: 3 -> 8; matrix products, arithmetic and copies ran while one was open for 14% -> 16% of each run, Pallas kernels for 0% -> 0%
where the time goes in v2:
time: 191 us
  starting transfers between devices  79.8 us (42%)
  Pallas kernels  43.5 us (23%)
  waiting for transfers between devices  29.5 us (15%)
  local copies, waits for them, and re-layouts  26.2 us (14%)
  other arithmetic  10.8 us (6%)
    ppermute x8, starting transfers between devices, swap_cores(): return lax.ppermute(block, 'segment', [(0, 1), (1, 0)])  66.7 us
    pallas_call x1, Pallas kernels, run_layers(): pl.pallas_call(lambda *refs: layers_kernel(padded, keys, *refs), grid_spe...  43.5 us
    ppermute x8, waiting for transfers between devices, reduce_shards(): arrived = lax.ppermute(send.astype(BF16), ('segment', 'dp'), route)  23.4 us
    unnamed x33, local copies, waits for them, and re-layouts  17.1 us
    ppermute x8, starting transfers between devices, reduce_shards(): arrived = lax.ppermute(send.astype(BF16), ('segment', 'dp'), route)  13.1 us
    ppermute x8, waiting for transfers between devices, swap_cores(): return lax.ppermute(block, 'segment', [(0, 1), (1, 0)])  6.01 us
    add x2, other arithmetic, reduce_shards(): block = mine.astype(F32) + got.astype(F32)  3.9 us
  transfers between devices with their start and end apart: 16, of which 8 were waited for; matrix products, arithmetic and copies ran while one was open for 16% of the time, Pallas kernels for 0%

profile of v2, /device:TPU:0, one launch (start us, length us, event | category | flops | bytes accessed | tf_op | source)
XLA Modules:
  0.0 190.7 jit_solution(91801147302794720)
XLA Ops:
  2.5 0.7 constant_dynamic-update-slice_fusion.8
  3.8 0.7 constant_dynamic-update-slice_fusion.5
  7.3 0.8 constant_dynamic-update-slice_fusion.refs_3_
  9.1 1.2 pad_add_fusion.refs_0_
  10.4 3.0 %copy.41.refs_1_ = bf16[2,6,197,384]{3,2,1,0:T(8,128)(2,1)} copy(bf16[2,6,197,384]{3,0,2,1:T(2,128)(2,1)} %param.15) | data formatting | bytes 3631104 | tf_op args[0]
  13.3 1.6 copy.42.refs_2_
  16.0 43.5 %shard_map.254 = (bf16[2,6,197,384]{3,2,1,0:T(8,128)(2,1)}, bf16[2,6,197,384]{3,2,1,0:T(8,128)(2,1)}, bf16[384,3200]{1,0:T(8,128)(2,1)}, bf16[384,3200]{1,0:T(8,...) custom-call(s32[2]{0:T(128)} %pad_add_fusion.refs_0_, bf16[2,6,197,384]{3,2,1,0:T(8,128)(2,1)} %copy.41.refs_1_, ...), custom_call_target="tpu_custom_call" | custom-call | flops 80000000000 | bytes 30000000 | tf_op jit(solution)/shard_map/pallas_call | solution.py:445
  59.5 64.0 %collective-permute-start.6 = (bf16[384,3200]{1,0:T(8,128)(2,1)}, bf16[384,3200]{1,0:T(8,128)(2,1)}, u32[]{:S(2)}, u32[]{:S(2)}) collective-permute-start(bf16[384,3200]{1,0:T(8,128)(2,1)} %get-tuple-element.23), channel_id=1, source_target_pairs={{0,16},{16,0},{1,17},{17,1},{2,18},{18,2},{3,19},{19,3},{4,20},{20... | collective-permute-start | bytes 7372808 | tf_op jit(solution)/shard_map/ppermute | solution.py:467
  123.6 6.0 %collective-permute-done.11 = bf16[1536,384]{1,0:T(8,128)(2,1)S(1)} collective-permute-done((bf16[1536,384]{1,0:T(8,128)(2,1)}, bf16[1536,384]{1,0:T(8,128)(2,1)S(1)}, u32[]{:S(2)}, u32[]{:S(2)}) %collective-permute-start.11) | collective-permute-done | bytes 1179680 | tf_op jit(solution)/shard_map/ppermute | solution.py:467
  129.6 1.7 convert_add_fusion.1
  131.4 3.2 %collective-permute-start.12 = (bf16[8,96,384]{2,1,0:T(8,128)(2,1)S(1)}, bf16[8,96,384]{2,1,0:T(8,128)(2,1)S(1)}, u32[]{:S(2)}, u32[]{:S(2)}) collective-permute-start(bf16[8,96,384]{2,1,0:T(8,128)(2,1)S(1)} %bitcast.78), channel_id=1, source_target_pairs={{0,2},{1,3},{2,0},{3,1},{4,6},{5,7},{6,4},{7,5},{8,10},{9,11},{10,... | collective-permute-start | bytes 1769480 | tf_op jit(solution)/shard_map/ppermute | solution.py:499
  134.6 2.2 %convert_add_fusion = f32[384,3200]{1,0:T(8,128)S(1)} fusion(bf16[384,3200]{1,0:T(8,128)(2,1)} %collective-permute-done.6, bf16[384,3200]{1,0:T(8,128)(2,1)S(1)} %copy-done.3), kind=kLoop, calls=%fused_computation | loop fusion | flops 3686400 | bytes 9830400 | tf_op jit(solution)/shard_map/add | solution.py:475
  136.9 1.7 fusion
  138.6 0.8 copy-done.1
  139.5 2.9 %copy.43 = bf16[2,6,197,384]{3,0,2,1:T(2,128)(2,1)S(1)} copy(bf16[2,6,197,384]{3,2,1,0:T(8,128)(2,1)} %get-tuple-element.21) | data formatting | bytes 3631104 | tf_op jit(solution)/shard_map/pallas_call | solution.py:445
  142.4 1.1 collective-permute-start.5
  143.6 4.6 %collective-permute-done.12 = bf16[8,96,384]{2,1,0:T(8,128)(2,1)S(1)} collective-permute-done((bf16[8,96,384]{2,1,0:T(8,128)(2,1)S(1)}, bf16[8,96,384]{2,1,0:T(8,128)(2,1)S(1)}, u32[]{:S(2)}, u32[]{:S(2)}) %collective-permute-start.12) | collective-permute-done | bytes 589856 | tf_op jit(solution)/shard_map/ppermute | solution.py:499
  148.4 1.6 collective-permute-start.13
  150.2 6.2 %collective-permute-done.7 = bf16[8,24,3200]{2,1,0:T(8,128)(2,1)} collective-permute-done((bf16[8,24,3200]{2,1,0:T(8,128)(2,1)}, bf16[8,24,3200]{2,1,0:T(8,128)(2,1)}, u32[]{:S(2)}, u32[]{:S(2)}) %collective-permute-start.7) | collective-permute-done | bytes 1228832 | tf_op jit(solution)/shard_map/ppermute | solution.py:499
  156.4 1.8 fusion.2
  159.5 2.6 %copy.46 = bf16[1,2,6,197,384]{4,1,3,2,0:T(2,128)(2,1)} copy(bf16[1,2,6,197,384]{4,3,2,0,1:T(8,128)(2,1)S(1)} %get-tuple-element.89) | data formatting | bytes 3631104
  162.1 2.6 %copy.47 = bf16[1,2,6,197,384]{4,1,3,2,0:T(2,128)(2,1)} copy(bf16[1,2,6,197,384]{4,3,2,0,1:T(8,128)(2,1)S(1)} %get-tuple-element.88) | data formatting | bytes 3631104
  164.9 2.0 %collective-permute-start.14 = (bf16[2,96,384]{2,1,0:T(8,128)(2,1)S(1)}, bf16[2,96,384]{2,1,0:T(8,128)(2,1)S(1)}, u32[]{:S(2)}, u32[]{:S(2)}) collective-permute-start(bf16[2,96,384]{2,1,0:T(8,128)(2,1)S(1)} %dynamic-slice_bitcast_fusion.2), channel_id=1, source_target_pairs={{0,1},{1,0},{2,3},{3,2},{4,5},{5,4},{6,7},{7,6},{8,9},{9,8},{10,11... | collective-permute-start | bytes 442376 | tf_op jit(solution)/shard_map/ppermute | solution.py:499
  166.9 1.6 collective-permute-done.8
  168.7 1.6 collective-permute-start.9
  170.3 1.4 collective-permute-done.14
  171.8 2.0 %collective-permute-start.15 = (bf16[1,96,384]{2,1,0:T(8,128)(2,1)S(1)}, bf16[1,96,384]{2,1,0:T(8,128)(2,1)S(1)}, u32[]{:S(2)}, u32[]{:S(2)}) collective-permute-start(bf16[1,96,384]{2,1,0:T(8,128)(2,1)S(1)} %constant_dynamic-slice_fusion), channel_id=1, source_target_pairs={{0,8},{1,9},{2,10},{3,11},{4,12},{5,13},{6,14},{7,15},{8,0},{9,1},... | collective-permute-start | bytes 221192 | tf_op jit(solution)/shard_map/ppermute | solution.py:499
  173.8 1.8 collective-permute-done.9
  175.7 2.3 %collective-permute-start.10 = (bf16[1,24,3200]{2,1,0:T(8,128)(2,1)S(1)}, bf16[1,24,3200]{2,1,0:T(8,128)(2,1)S(1)}, u32[]{:S(2)}, u32[]{:S(2)}) collective-permute-start(bf16[1,24,3200]{2,1,0:T(8,128)(2,1)S(1)} %constant_dynamic-slice_fusion.4), channel_id=1, source_target_pairs={{0,8},{1,9},{2,10},{3,11},{4,12},{5,13},{6,14},{7,15},{8,0},{9,1},... | collective-permute-start | bytes 460808 | tf_op jit(solution)/shard_map/ppermute | solution.py:499
  178.0 1.3 collective-permute-done.15
  180.0 6.5 %collective-permute-done.10 = bf16[1,24,3200]{2,1,0:T(8,128)(2,1)S(1)} collective-permute-done((bf16[1,24,3200]{2,1,0:T(8,128)(2,1)S(1)}, bf16[1,24,3200]{2,1,0:T(8,128)(2,1)S(1)}, u32[]{:S(2)}, u32[]{:S(2)}) %collective-permute-start.10) | collective-permute-done | bytes 153632 | tf_op jit(solution)/shard_map/ppermute | solution.py:499
  188.7 0.8 slice_reduce_fusion
  (69 shorter events, 13.9 us)
Async XLA Ops:
  0.6 7.9 %copy-start = (s32[2,1]{0,1:T(1,128)S(1)}, s32[2,1]{0,1:T(1,128)}, u32[]{:S(2)}) copy-start(s32[2,1]{0,1:T(1,128)} %param.16) | copy-start | bytes 28
  0.7 14.3 %collective-permute-start.3 = (bf16[1,384,1536]{2,1,0:T(8,128)(2,1)}, bf16[1,384,1536]{2,1,0:T(8,128)(2,1)S(1)}, u32[]{:S(2)}, u32[]{:S(2)}) collective-permute-start(bf16[1,384,1536]{2,1,0:T(8,128)(2,1)} %refs_7_.1), channel_id=1, source_target_pairs={{0,16},{16,0},{1,17},{17,1},{2,18},{18,2},{3,19},{19,3},{4,20},{20... | collective-permute-start | bytes 3538952 | tf_op jit(solution)/shard_map/ppermute | solution.py:467
  1.2 13.8 %collective-permute-start.4 = (bf16[1,1536,384]{2,1,0:T(8,128)(2,1)}, bf16[1,1536,384]{2,1,0:T(8,128)(2,1)}, u32[]{:S(2)}, u32[]{:S(2)}) collective-permute-start(bf16[1,1536,384]{2,1,0:T(8,128)(2,1)} %refs_8_.1), channel_id=1, source_target_pairs={{0,16},{16,0},{1,17},{17,1},{2,18},{18,2},{3,19},{19,3},{4,20},{20... | collective-permute-start | bytes 3538952 | tf_op jit(solution)/shard_map/ppermute | solution.py:467
  1.3 13.7 %collective-permute-start.1 = (bf16[1,384,1152]{2,1,0:T(8,128)(2,1)}, bf16[1,384,1152]{2,1,0:T(8,128)(2,1)}, u32[]{:S(2)}, u32[]{:S(2)}) collective-permute-start(bf16[1,384,1152]{2,1,0:T(8,128)(2,1)} %refs_5_.1), channel_id=1, source_target_pairs={{0,16},{16,0},{1,17},{17,1},{2,18},{18,2},{3,19},{19,3},{4,20},{20... | collective-permute-start | bytes 2654216 | tf_op jit(solution)/shard_map/ppermute | solution.py:467
  1.7 13.2 %collective-permute-start.2 = (bf16[1,384,384]{2,1,0:T(8,128)(2,1)}, bf16[1,384,384]{2,1,0:T(8,128)(2,1)S(1)}, u32[]{:S(2)}, u32[]{:S(2)}) collective-permute-start(bf16[1,384,384]{2,1,0:T(8,128)(2,1)} %refs_6_.1), channel_id=1, source_target_pairs={{0,16},{16,0},{1,17},{17,1},{2,18},{18,2},{3,19},{19,3},{4,20},{20... | collective-permute-start | bytes 884744 | tf_op jit(solution)/shard_map/ppermute | solution.py:467
  7.3 6.0 %copy-start.5 = (bf16[2,6,197,384]{3,0,2,1:T(2,128)(2,1)S(1)}, bf16[2,6,197,384]{3,0,2,1:T(2,128)(2,1)}, u32[]{:S(2)}) copy-start(bf16[2,6,197,384]{3,0,2,1:T(2,128)(2,1)} %param.17) | copy-start | bytes 5446660
  8.1 6.8 %copy-start.6 = (f32[1,4992]{1,0:T(1,128)}, f32[1,4992]{1,0:T(1,128)S(1)}, u32[]{:S(2)}) copy-start(f32[1,4992]{1,0:T(1,128)S(1)} %constant_dynamic-update-slice_fusion.refs_3_) | copy-start | bytes 59908
  8.1 6.8 %collective-permute-start = (f32[1,4992]{1,0:T(1,128)S(1)}, f32[1,4992]{1,0:T(1,128)S(1)}, u32[]{:S(2)}, u32[]{:S(2)}) collective-permute-start(f32[1,4992]{1,0:T(1,128)S(1)} %constant_dynamic-update-slice_fusion.refs_3_), channel_id=1, source_target_pairs={{0,16},{16,0},{1,17},{17,1},{2,18},{18,2},{3,19},{19,3},{4,20},{20... | collective-permute-start | bytes 59912 | tf_op jit(solution)/shard_map/ppermute | solution.py:467
  14.9 0.6 copy-start.9
  14.9 0.7 copy-start.8
  14.9 1.1 copy-start.7
  59.5 75.0 %collective-permute-start.6 = (bf16[384,3200]{1,0:T(8,128)(2,1)}, bf16[384,3200]{1,0:T(8,128)(2,1)}, u32[]{:S(2)}, u32[]{:S(2)}) collective-permute-start(bf16[384,3200]{1,0:T(8,128)(2,1)} %get-tuple-element.23), channel_id=1, source_target_pairs={{0,16},{16,0},{1,17},{17,1},{2,18},{18,2},{3,19},{19,3},{4,20},{20... | collective-permute-start | bytes 7372808 | tf_op jit(solution)/shard_map/ppermute | solution.py:467
  123.5 6.1 %collective-permute-start.11 = (bf16[1536,384]{1,0:T(8,128)(2,1)}, bf16[1536,384]{1,0:T(8,128)(2,1)S(1)}, u32[]{:S(2)}, u32[]{:S(2)}) collective-permute-start(bf16[1536,384]{1,0:T(8,128)(2,1)} %get-tuple-element.25), channel_id=1, source_target_pairs={{0,16},{16,0},{1,17},{17,1},{2,18},{18,2},{3,19},{19,3},{4,20},{20... | collective-permute-start | bytes 3538952 | tf_op jit(solution)/shard_map/ppermute | solution.py:467
  129.6 5.0 %copy-start.3 = (bf16[384,3200]{1,0:T(8,128)(2,1)S(1)}, bf16[384,3200]{1,0:T(8,128)(2,1)}, u32[]{:S(2)}) copy-start(bf16[384,3200]{1,0:T(8,128)(2,1)} %get-tuple-element.22) | copy-start | bytes 7372804
  131.4 16.8 %collective-permute-start.12 = (bf16[8,96,384]{2,1,0:T(8,128)(2,1)S(1)}, bf16[8,96,384]{2,1,0:T(8,128)(2,1)S(1)}, u32[]{:S(2)}, u32[]{:S(2)}) collective-permute-start(bf16[8,96,384]{2,1,0:T(8,128)(2,1)S(1)} %bitcast.78), channel_id=1, source_target_pairs={{0,2},{1,3},{2,0},{3,1},{4,6},{5,7},{6,4},{7,5},{8,10},{9,11},{10,... | collective-permute-start | bytes 1769480 | tf_op jit(solution)/shard_map/ppermute | solution.py:499
  136.7 2.6 %copy-start.1 = (f32[384,3200]{1,0:T(8,128)}, f32[384,3200]{1,0:T(8,128)S(1)}, u32[]{:S(2)}) copy-start(f32[384,3200]{1,0:T(8,128)S(1)} %convert_add_fusion) | copy-start | bytes 14745604
  139.3 17.0 %collective-permute-start.7 = (bf16[8,24,3200]{2,1,0:T(8,128)(2,1)}, bf16[8,24,3200]{2,1,0:T(8,128)(2,1)}, u32[]{:S(2)}, u32[]{:S(2)}) collective-permute-start(bf16[8,24,3200]{2,1,0:T(8,128)(2,1)} %fusion), channel_id=1, source_target_pairs={{0,1},{1,0},{2,3},{3,2},{4,5},{5,4},{6,7},{7,6},{8,9},{9,8},{10,11... | collective-permute-start | bytes 3686408 | tf_op jit(solution)/shard_map/ppermute | solution.py:499
  142.4 16.1 %collective-permute-start.5 = (bf16[2,6,197,384]{3,0,2,1:T(2,128)(2,1)S(1)}, bf16[2,6,197,384]{3,0,2,1:T(2,128)(2,1)S(1)}, u32[]{:S(2)}, u32[]{:S(2)}) collective-permute-start(bf16[2,6,197,384]{3,0,2,1:T(2,128)(2,1)S(1)} %copy.43), channel_id=1, source_target_pairs={{0,16},{16,0},{1,17},{17,1},{2,18},{18,2},{3,19},{19,3},{4,20},{20... | collective-permute-start | bytes 5446664 | tf_op jit(solution)/shard_map/ppermute | solution.py:467
  143.5 6.6 %copy-start.2 = (f32[384,3200]{1,0:T(8,128)S(1)}, f32[384,3200]{1,0:T(8,128)}, u32[]{:S(2)}) copy-start(f32[384,3200]{1,0:T(8,128)} %copy-done.1) | copy-start | bytes 14745604
  148.4 16.3 %collective-permute-start.13 = (bf16[4,96,384]{2,1,0:T(8,128)(2,1)S(1)}, bf16[4,96,384]{2,1,0:T(8,128)(2,1)S(1)}, u32[]{:S(2)}, u32[]{:S(2)}) collective-permute-start(bf16[4,96,384]{2,1,0:T(8,128)(2,1)S(1)} %bitcast.79), channel_id=1, source_target_pairs={{0,4},{1,5},{2,6},{3,7},{4,0},{5,1},{6,2},{7,3},{8,12},{9,13},{10,... | collective-permute-start | bytes 884744 | tf_op jit(solution)/shard_map/ppermute | solution.py:499
  156.4 2.1 %copy-start.4 = (bf16[2,6,197,384]{3,2,1,0:T(8,128)(2,1)S(1)}, bf16[2,6,197,384]{3,2,1,0:T(8,128)(2,1)}, u32[]{:S(2)}) copy-start(bf16[2,6,197,384]{3,2,1,0:T(8,128)(2,1)} %get-tuple-element.20) | copy-start | bytes 5446660
  158.3 10.2 %collective-permute-start.8 = (bf16[4,24,3200]{2,1,0:T(8,128)(2,1)S(1)}, bf16[4,24,3200]{2,1,0:T(8,128)(2,1)S(1)}, u32[]{:S(2)}, u32[]{:S(2)}) collective-permute-start(bf16[4,24,3200]{2,1,0:T(8,128)(2,1)S(1)} %dynamic-slice_bitcast_fusion), channel_id=1, source_target_pairs={{0,2},{1,3},{2,0},{3,1},{4,6},{5,7},{6,4},{7,5},{8,10},{9,11},{10,... | collective-permute-start | bytes 1843208 | tf_op jit(solution)/shard_map/ppermute | solution.py:499
  164.9 6.9 %collective-permute-start.14 = (bf16[2,96,384]{2,1,0:T(8,128)(2,1)S(1)}, bf16[2,96,384]{2,1,0:T(8,128)(2,1)S(1)}, u32[]{:S(2)}, u32[]{:S(2)}) collective-permute-start(bf16[2,96,384]{2,1,0:T(8,128)(2,1)S(1)} %dynamic-slice_bitcast_fusion.2), channel_id=1, source_target_pairs={{0,1},{1,0},{2,3},{3,2},{4,5},{5,4},{6,7},{7,6},{8,9},{9,8},{10,11... | collective-permute-start | bytes 442376 | tf_op jit(solution)/shard_map/ppermute | solution.py:499
  168.7 6.9 %collective-permute-start.9 = (bf16[2,24,3200]{2,1,0:T(8,128)(2,1)S(1)}, bf16[2,24,3200]{2,1,0:T(8,128)(2,1)S(1)}, u32[]{:S(2)}, u32[]{:S(2)}) collective-permute-start(bf16[2,24,3200]{2,1,0:T(8,128)(2,1)S(1)} %dynamic-slice_bitcast_fusion.1), channel_id=1, source_target_pairs={{0,4},{1,5},{2,6},{3,7},{4,0},{5,1},{6,2},{7,3},{8,12},{9,13},{10,... | collective-permute-start | bytes 921608 | tf_op jit(solution)/shard_map/ppermute | solution.py:499
  171.8 7.6 %collective-permute-start.15 = (bf16[1,96,384]{2,1,0:T(8,128)(2,1)S(1)}, bf16[1,96,384]{2,1,0:T(8,128)(2,1)S(1)}, u32[]{:S(2)}, u32[]{:S(2)}) collective-permute-start(bf16[1,96,384]{2,1,0:T(8,128)(2,1)S(1)} %constant_dynamic-slice_fusion), channel_id=1, source_target_pairs={{0,8},{1,9},{2,10},{3,11},{4,12},{5,13},{6,14},{7,15},{8,0},{9,1},... | collective-permute-start | bytes 221192 | tf_op jit(solution)/shard_map/ppermute | solution.py:499
  175.7 10.8 %collective-permute-start.10 = (bf16[1,24,3200]{2,1,0:T(8,128)(2,1)S(1)}, bf16[1,24,3200]{2,1,0:T(8,128)(2,1)S(1)}, u32[]{:S(2)}, u32[]{:S(2)}) collective-permute-start(bf16[1,24,3200]{2,1,0:T(8,128)(2,1)S(1)} %constant_dynamic-slice_fusion.4), channel_id=1, source_target_pairs={{0,8},{1,9},{2,10},{3,11},{4,12},{5,13},{6,14},{7,15},{8,0},{9,1},... | collective-permute-start | bytes 460808 | tf_op jit(solution)/shard_map/ppermute | solution.py:499

commit v3 on v2

v3 whole, which is shorter than its diff:
```python
import jax
import jax.numpy as jnp
from jax import lax
from jax.experimental import pallas as pl
from jax.experimental.pallas import tpu as pltpu
from jax.sharding import PartitionSpec as P

HEAD = 64
EPSILON = 1e-06
BF16 = jnp.bfloat16
F32 = jnp.float32
GROUP = 2
VMEM_LIMIT = 62 * 1024 * 1024


def dot(a, b):
    return lax.dot_general(a, b, (((1,), (0,)), ((), ())), preferred_element_type=F32)


def dot_nt(a, b):
    return lax.dot_general(a, b, (((1,), (1,)), ((), ())), preferred_element_type=F32)


def dot_tn(a, b):
    return lax.dot_general(a, b, (((0,), (0,)), ((), ())), preferred_element_type=F32)


def normalized(rows):
    centered = rows - jnp.mean(rows, axis=-1, keepdims=True)
    spread = jnp.mean(centered * centered, axis=-1, keepdims=True)
    inverse = lax.rsqrt(spread + EPSILON)
    return centered * inverse, inverse


def norm_backward(rows, grad, gain):
    hat, inverse = normalized(rows)
    scaled = grad * gain
    inner = jnp.mean(scaled * hat, axis=-1, keepdims=True)
    dx = inverse * (scaled - jnp.mean(scaled, axis=-1, keepdims=True) - hat * inner)
    return dx, grad * hat


def gelu_and_slope(x):
    bell = jnp.exp(x * x * -0.5)
    under = 1.0 + jnp.abs(x) * (0.3275911 * 0.7071067811865476)
    t = pl.reciprocal(under, approx=True)
    t = t * (2.0 - under * t)
    poly = t * (
        0.5 * 0.254829592
        + t
        * (
            0.5 * -0.284496736
            + t * (0.5 * 1.421413741 + t * (0.5 * -1.453152027 + t * (0.5 * 1.061405429)))
        )
    )
    tail = poly * bell
    cdf = jnp.where(x >= 0.0, 1.0 - tail, tail)
    return x * cdf, cdf + x * (bell * 0.3989422804014327)


def fold(rows):
    total = rows[0:8]
    for at in range(8, rows.shape[0], 8):
        total = total + rows[at : at + 8]
    return total


def row_chunks(total, size=32):
    return [(at, min(size, total - at)) for at in range(0, total, size)]


def spans(total, width):
    return [slice(at, min(at + width, total)) for at in range(0, total, width)]


def layers_kernel(
    padded,
    keys,
    meta,
    h_ref,
    cot_ref,
    own_vec,
    got_vec,
    own_qkv,
    own_out,
    own_up,
    own_down,
    got_qkv,
    got_out,
    got_up,
    got_down,
    mine_ref,
    away_ref,
    mine_wide,
    away_wide,
    mine_tall,
    away_tall,
    w_qkv,
    w_out,
    w_up,
    w_down,
    vecs,
    hidden,
    normed,
    queries,
    kv,
    weights,
    attended,
    middle,
    second,
    active,
    slope,
    before,
    grad_out,
    grad_low,
    out_low,
    grad_heads,
    grad_before,
    grad_joined,
    grad_norm,
    scores,
    grad_scores,
    sum_up,
    sum_down,
    sum_att,
    vec_one,
    vec_up,
    vec_qkv,
    wide,
    tall,
    load_sem,
    store_sem,
):
    step = pl.program_id(0)
    last = pl.num_programs(0) - 1
    count = meta[0]
    core = meta[1]
    running = step * GROUP < count
    tokens, features = h_ref.shape[2:]
    heads = features // HEAD
    rows = GROUP * padded
    units = w_up.shape[2]
    couple = 2 * HEAD
    own = (own_qkv, own_out, own_up, own_down)
    got = (got_qkv, got_out, got_up, got_down)
    held = (w_qkv, w_out, w_up, w_down)
    at_g1, at_b1, at_qkv = 0, features, 2 * features
    at_bo, at_g2, at_b2, at_bd, at_up = (n * features for n in (5, 6, 7, 8, 9))

    def vec(layer, at, size=features):
        return vecs[pl.ds(layer, 1), at : at + size]

    def load(source, n, layer):
        return pltpu.make_async_copy(source[n].at[0], held[n].at[layer], load_sem.at[layer, n])

    @pl.when(step == 0)
    def _():
        for layer in range(2):
            for n in range(4):

                @pl.when(core == layer)
                def _():
                    load(own, n, layer).start()

                @pl.when(core != layer)
                def _():
                    load(got, n, layer).start()

        for layer in range(2):
            mine = jnp.full(own_vec.shape, core == layer)
            vecs[layer : layer + 1] = jnp.where(mine, own_vec[...], got_vec[...])
        for ref in (sum_up, sum_down, sum_att, vec_one, vec_up, vec_qkv):
            for layer in range(2):
                ref[layer] = jnp.zeros(ref.shape[1:], F32)
        for layer in range(2):
            for j in range(GROUP):
                kv[layer, j * keys + padded : (j + 1) * keys] = jnp.zeros(
                    (keys - padded, 2 * features), BF16
                )

    def leave(layer, kind, j, value):
        @pl.when(core == layer)
        def _():
            mine_ref[kind, j] = value

        @pl.when(core != layer)
        def _():
            away_ref[kind, j] = value

    lane = lax.broadcasted_iota(jnp.int32, (padded, couple), 1)
    left = lane < HEAD
    image = [slice(j * padded, (j + 1) * padded) for j in range(GROUP)]
    images_keys = [slice(j * keys, (j + 1) * keys) for j in range(GROUP)]
    pairs = [slice(n * couple, (n + 1) * couple) for n in range(heads // 2)]
    tasks = [(j, n) for j in range(GROUP) for n in range(heads // 2)]
    chunks = spans(units, 512)

    def stacked(value):
        nothing = jnp.zeros_like(value)
        return jnp.where(left, value, nothing), jnp.where(left, nothing, value)

    def key_of(layer, j, n):
        return kv[layer, images_keys[j], pairs[n]]

    def value_of(layer, j, n):
        at = features + n * couple
        return kv[layer, images_keys[j], at : at + couple]

    def unstacked(value):
        return jnp.where(left, value[:padded], value[padded:])

    def forward(layer):
        @pl.when(step == 0)
        def _():
            for n in range(4):
                load(own, n, layer).wait()

        for at, size in row_chunks(rows):
            hat, _ = normalized(hidden[layer, at : at + size])
            value = hat * vec(layer, at_g1) + vec(layer, at_b1)
            normed[layer, at : at + size] = value.astype(BF16)
        value = dot(normed[layer], w_qkv[layer, :, :features]) + vec(layer, at_qkv)
        value = value.astype(BF16) * jnp.asarray(HEAD**-0.5, BF16)
        for j, n in tasks:
            for half, part in enumerate(stacked(value[image[j], pairs[n]])):
                queries[layer, j, n, half * padded : (half + 1) * padded] = part
        for columns in spans(2 * features, 512):
            at, size = features + columns.start, columns.stop - columns.start
            value = dot(normed[layer], w_qkv[layer, :, at : at + size])
            value = (value + vec(layer, at_qkv + at, size)).astype(BF16)
            for j in range(GROUP):
                kv[layer, j * keys : j * keys + padded, columns] = value[image[j]]

        def score(u):
            j, n = tasks[u]
            scores[u % 2] = dot_nt(queries[layer, j, n], key_of(layer, j, n))

        def soften(u):
            j, n = tasks[u]
            for at, size in row_chunks(2 * padded):
                real = lax.broadcasted_iota(jnp.int32, (size, keys), 1) < tokens
                s = jnp.where(real, scores[u % 2, at : at + size], -1e30)
                e = jnp.exp(s - jnp.max(s, axis=-1, keepdims=True))
                p = e * (1.0 / jnp.sum(e, axis=-1, keepdims=True))
                weights[layer, j, n, at : at + size] = p.astype(BF16)

        def attend(u):
            j, n = tasks[u]
            value = unstacked(dot(weights[layer, j, n], value_of(layer, j, n)))
            attended[layer, image[j], pairs[n]] = value.astype(BF16)

        def project(j):
            middle[layer, image[j]] = dot(attended[layer, image[j]], w_out[layer])

        def norm_two(j):
            for at, size in row_chunks(padded, 16):
                at = j * padded + at
                value = middle[layer, at : at + size] + hidden[layer, at : at + size]
                value = value + vec(layer, at_bo)
                middle[layer, at : at + size] = value
                hat, _ = normalized(value)
                value = hat * vec(layer, at_g2) + vec(layer, at_b2)
                second[layer, at : at + size] = value.astype(BF16)

        score(0)
        for u in range(len(tasks)):
            if u + 1 < len(tasks):
                score(u + 1)
            if u:
                attend(u - 1)
                if tasks[u - 1][1] == heads // 2 - 1:
                    project(tasks[u - 1][0])
            soften(u)
            if u and tasks[u - 1][1] == heads // 2 - 1:
                norm_two(tasks[u - 1][0])
        attend(len(tasks) - 1)
        project(GROUP - 1)
        norm_two(GROUP - 1)

        def up(c):
            before[:, chunks[c]] = dot(second[layer], w_up[layer, :, chunks[c]])

        def curve(c):
            columns = chunks[c]
            for at, size in row_chunks(rows, 16):
                value, change = gelu_and_slope(
                    before[at : at + size, columns]
                    + vec(layer, at_up + columns.start, columns.stop - columns.start)
                )
                active[layer, at : at + size, columns] = value.astype(BF16)
                slope[layer, at : at + size, columns] = change.astype(BF16)

        def down(c):
            value = dot(active[layer, :, chunks[c]], w_down[layer, chunks[c]])
            if c:
                value = value + grad_norm[...]
            grad_norm[...] = value

        up(0)
        for c in range(len(chunks)):
            if c + 1 < len(chunks):
                up(c + 1)
            if c:
                down(c - 1)
            curve(c)
        down(len(chunks) - 1)
        for j in range(GROUP):
            keep = jnp.where(step * GROUP + j < count, 1.0, 0.0)
            result = grad_norm[image[j]] + middle[layer, image[j]]
            result = ((result + vec(layer, at_bd)) * keep).astype(BF16)
            leave(layer, 0, j, result[:tokens])
            hidden[layer + 1, image[j]] = result.astype(F32)

    def backward(layer):
        for at, size in row_chunks(rows):
            value = grad_out[at : at + size]
            grad_low[at : at + size] = value.astype(BF16)
            vec_one[layer, 0:8] += fold(value)

        def activation(c):
            before[:, chunks[c]] = dot_nt(grad_low[...], w_down[layer, chunks[c]])

        def multiply(c):
            columns = chunks[c]
            total = jnp.zeros((8, columns.stop - columns.start), F32)
            for at, size in row_chunks(rows, 16):
                lines = slice(at, at + size)
                piece = before[lines, columns] * slope[layer, lines, columns].astype(F32)
                piece = piece.astype(BF16)
                grad_before[lines, columns] = piece
                total = total + fold(piece.astype(F32))
            vec_up[layer, :, columns] += total

        activation(0)
        for c in range(len(chunks)):
            if c + 1 < len(chunks):
                activation(c + 1)
            sum_down[layer, :, chunks[c]] += dot_tn(grad_low[...], active[layer, :, chunks[c]])
            multiply(c)

        def norm_two(j):
            one, two, three = (jnp.zeros((8, features), F32) for _ in range(3))
            for at, size in row_chunks(padded, 16):
                lines = slice(j * padded + at, j * padded + at + size)
                grad = grad_norm[lines]
                dx, by_hat = norm_backward(middle[layer, lines], grad, vec(layer, at_g2))
                one = one + fold(by_hat)
                two = two + fold(grad)
                value = grad_out[lines] + dx
                grad_out[lines] = value
                value = value.astype(BF16)
                out_low[lines] = value
                three = three + fold(value.astype(F32))
            vec_one[layer, 8:16] += one
            vec_one[layer, 16:24] += two
            vec_one[layer, 24:32] += three

        for j in range(GROUP):
            grad_norm[image[j]] = dot_nt(grad_before[image[j]], w_up[layer])
        for c in range(len(chunks)):
            sum_up[layer, :, chunks[c]] += dot_tn(second[layer], grad_before[:, chunks[c]])
            if c < GROUP:
                norm_two(c)
        for j in range(GROUP):
            value = dot_nt(out_low[image[j]], w_out[layer]).astype(BF16)
            for n in range(heads // 2):
                for half, part in enumerate(stacked(value[:, pairs[n]])):
                    grad_heads[j, n, half * padded : (half + 1) * padded] = part

        def grad_weights(u):
            j, n = tasks[u]
            scores[u % 2] = dot_nt(grad_heads[j, n], value_of(layer, j, n))

        def soften_back(u):
            j, n = tasks[u]
            for at, size in row_chunks(2 * padded):
                p = weights[layer, j, n, at : at + size].astype(F32)
                by = p * scores[u % 2, at : at + size]
                by = by - p * jnp.sum(by, axis=-1, keepdims=True)
                grad_scores[u % 2, at : at + size] = by.astype(BF16)

        def into(layer, j, column, part):
            part = part.astype(BF16)
            grad_joined[image[j], column : column + couple] = part
            vec_qkv[layer, :, column : column + couple] += fold(part.astype(F32))

        def attention_value(u):
            j, n = tasks[u]
            part = dot_tn(weights[layer, j, n], grad_heads[j, n])[:padded]
            into(layer, j, 2 * features + n * couple, part)

        def attention_rest(u):
            j, n = tasks[u]
            part = unstacked(dot(grad_scores[u % 2], key_of(layer, j, n))) * HEAD**-0.5
            into(layer, j, n * couple, part)
            part = dot_tn(grad_scores[u % 2], queries[layer, j, n])[:padded]
            into(layer, j, features + n * couple, part)

        grad_weights(0)
        for u in range(len(tasks)):
            if u + 1 < len(tasks):
                grad_weights(u + 1)
            if u:
                attention_rest(u - 1)
            else:
                sum_att[layer, :, 3 * features :] += dot_tn(attended[layer], out_low[...])
            attention_value(u)
            soften_back(u)
        attention_rest(len(tasks) - 1)

        def norm_one(j):
            one, two = (jnp.zeros((8, features), F32) for _ in range(2))
            for at, size in row_chunks(padded, 16):
                lines = slice(j * padded + at, j * padded + at + size)
                grad = grad_norm[lines]
                dx, by_hat = norm_backward(hidden[layer, lines], grad, vec(layer, at_g1))
                one = one + fold(by_hat)
                two = two + fold(grad)
                value = grad_out[lines] + dx
                grad_out[lines] = value.astype(BF16).astype(F32)
            vec_one[layer, 32:40] += one
            vec_one[layer, 40:48] += two

        for j in range(GROUP):
            grad_norm[image[j]] = dot_nt(grad_joined[image[j]], w_qkv[layer])
        for c, columns in enumerate(spans(3 * features, 512)):
            sum_att[layer, :, columns] += dot_tn(normed[layer], grad_joined[:, columns])
            if c < GROUP:
                norm_one(c)
        for j in range(GROUP):
            leave(layer, 1, j, grad_out[j * padded : j * padded + tokens].astype(BF16))

    def store(layer, kind, target):
        stage = (wide, tall)[kind].at[layer]
        return pltpu.make_async_copy(stage, target, store_sem.at[layer, kind])

    def finish(layer):
        wide[layer, :, :units] = sum_up[layer].astype(BF16)
        wide[layer, :, units : units + 4 * features] = sum_att[layer].astype(BF16)
        line = lax.broadcasted_iota(jnp.int32, (128, features), 0)
        plain = jnp.zeros((128, features), F32)
        for n, group in enumerate((4, 5, 3, 1, 2, 0)):
            total = jnp.sum(vec_one[layer, 8 * group : 8 * group + 8], axis=0, keepdims=True)
            plain = plain + jnp.where(line == n, total, 0.0)
        qkv = jnp.sum(vec_qkv[layer], axis=0, keepdims=True)
        qv = jnp.concatenate([qkv[:, :features], qkv[:, 2 * features :]], axis=1)
        total_up = jnp.sum(vec_up[layer], axis=0, keepdims=True)
        columns = jnp.zeros((features, 128), F32)
        for first_line, total in ((0, plain), (6, qv), (8, total_up)):
            size = total.shape[1]
            each = size // features
            position = lax.broadcasted_iota(jnp.int32, (128, size), 1)
            row = lax.broadcasted_iota(jnp.int32, (128, size), 0)
            if each > 1:
                total = jnp.where(row - first_line == position % each, total, 0.0)
            target = lax.broadcasted_iota(jnp.int32, (features, size), 0)
            source = lax.broadcasted_iota(jnp.int32, (features, size), 1)
            pick = jnp.where(source // each == target, 1.0, 0.0).astype(BF16)
            columns = columns + dot_nt(pick, total.astype(BF16))
        wide[layer, :, units + 4 * features :] = columns.astype(BF16)

        def send(kind, mine, away):
            @pl.when(core == layer)
            def _():
                store(layer, kind, mine).start()

            @pl.when(core != layer)
            def _():
                store(layer, kind, away).start()

        send(0, mine_wide, away_wide)
        for columns in spans(units, features):
            tall[layer, columns, :] = sum_down[layer, :, columns].T.astype(BF16)
        send(1, mine_tall, away_tall)

    @pl.when(jnp.logical_not(running))
    def _():
        mine_ref[...] = jnp.zeros_like(mine_ref)
        away_ref[...] = jnp.zeros_like(away_ref)

    @pl.when(running)
    def _():
        for j in range(GROUP):
            tail = slice(j * padded + padded - 16, (j + 1) * padded)
            hidden[0, tail] = jnp.zeros((16, features), F32)
            hidden[0, j * padded : j * padded + tokens] = h_ref[0, j].astype(F32)
        lax.fori_loop(0, 2, lambda layer, carry: (forward(layer), carry)[1], 0)
        for j in range(GROUP):
            keep = jnp.where(step * GROUP + j < count, 1.0, 0.0)
            tail = slice(j * padded + padded - 16, (j + 1) * padded)
            grad_out[tail] = jnp.zeros((16, features), F32)
            grad_out[j * padded : j * padded + tokens] = cot_ref[0, j].astype(F32) * keep

    def second_half(at, carry):
        layer = 1 - at

        @pl.when(running)
        def _():
            backward(layer)

        @pl.when(step == last)
        def _():
            finish(layer)

        return carry

    lax.fori_loop(0, 2, second_half, 0)

    @pl.when(step == last)
    def _():
        for layer in range(2):
            for kind, mine in enumerate((mine_wide, mine_tall)):
                store(layer, kind, mine).wait()


def run_layers(meta, inputs, cotangent, vectors, weights):
    slots, tokens, features = inputs.shape[1:]
    padded = -(-tokens // 16) * 16
    keys = -(-tokens // 128) * 128
    heads = features // HEAD
    steps = slots // GROUP
    block = GROUP * padded
    units = weights[0][2].shape[2]
    packed = vectors[0].shape[1]
    wide = units + 4 * features + 128
    images = pl.BlockSpec((1, GROUP, tokens, features), lambda i, meta: (meta[1], i, 0, 0))
    kinds = pl.BlockSpec((2, GROUP, tokens, features), lambda i, meta: (0, i, 0, 0))
    vector = pl.BlockSpec((1, packed), lambda i, meta: (0, 0))
    anywhere = pl.BlockSpec(memory_space=pl.ANY)
    both = (
        ((features, 3 * features), BF16),
        ((features, features), BF16),
        ((features, units), BF16),
        ((units, features), BF16),
        ((packed,), F32),
    )
    saved = (
        ((block, features), BF16),
        ((GROUP, heads // 2, 2 * padded, 2 * HEAD), BF16),
        ((GROUP * keys, 2 * features), BF16),
        ((GROUP, heads // 2, 2 * padded, keys), BF16),
        ((block, features), BF16),
        ((block, features), F32),
        ((block, features), BF16),
        ((block, units), BF16),
        ((block, units), BF16),
    )
    sums = (
        ((features, units), F32),
        ((features, units), F32),
        ((features, 4 * features), F32),
        ((48, features), F32),
        ((8, units), F32),
        ((8, 3 * features), F32),
        ((features, wide), BF16),
        ((units, features), BF16),
    )

    def two(shapes):
        return [pltpu.VMEM((2,) + shape, kind) for shape, kind in shapes]

    scratch = (
        two(both)
        + [pltpu.VMEM((3, block, features), F32)]
        + two(saved)
        + [
            pltpu.VMEM((block, units), F32),
            pltpu.VMEM((block, features), F32),
            pltpu.VMEM((block, features), BF16),
            pltpu.VMEM((block, features), BF16),
            pltpu.VMEM((GROUP, heads // 2, 2 * padded, 2 * HEAD), BF16),
            pltpu.VMEM((block, units), BF16),
            pltpu.VMEM((block, 3 * features), BF16),
            pltpu.VMEM((block, features), F32),
            pltpu.VMEM((2, 2 * padded, keys), F32),
            pltpu.VMEM((2, 2 * padded, keys), BF16),
        ]
        + two(sums)
        + [pltpu.SemaphoreType.DMA((2, 4)), pltpu.SemaphoreType.DMA((2, 2))]
    )
    return pl.pallas_call(
        lambda *refs: layers_kernel(padded, keys, *refs),
        grid_spec=pltpu.PrefetchScalarGridSpec(
            num_scalar_prefetch=1,
            grid=(steps,),
            in_specs=[images, images, vector, vector] + [anywhere] * 8,
            out_specs=[kinds, kinds] + [anywhere] * 4,
            scratch_shapes=scratch,
        ),
        out_shape=[jax.ShapeDtypeStruct((2, slots, tokens, features), BF16)] * 2
        + [jax.ShapeDtypeStruct((features, wide), BF16)] * 2
        + [jax.ShapeDtypeStruct((units, features), BF16)] * 2,
        compiler_params=pltpu.CompilerParams(
            vmem_limit_bytes=VMEM_LIMIT, dimension_semantics=("arbitrary",)
        ),
        cost_estimate=pl.CostEstimate(
            flops=80_000_000_000, bytes_accessed=30_000_000, transcendentals=0
        ),
    )(meta, inputs, cotangent, *vectors, *weights[0], *weights[1])


def pack_vectors(arrays):
    total = sum(a.shape[1] for a in arrays)

    def body(*refs):
        at = 0
        for ref in refs[:-1]:
            refs[-1][:, at : at + ref.shape[1]] = ref[...]
            at += ref.shape[1]

    return pl.pallas_call(body, out_shape=jax.ShapeDtypeStruct((1, total), F32))(*arrays)


def swap_cores(block):
    return lax.ppermute(block, "segment", [(0, 1), (1, 0)])


def reduce_shards(mine, got, orders, first):
    dp = lax.axis_size("dp")
    me = lax.axis_index("dp")
    bits = dp.bit_length() - 1
    rest = (mine.shape[0] // dp, mine.shape[1])
    block = (mine, got)
    held = [list(range(bits)) for _ in orders]
    for n in range(bits):
        below = [left.index(order[n]) for order, left in zip(orders, held)]
        bit = [(me >> order[n]) & 1 for order in orders]
        for order, left in zip(orders, held):
            left.remove(order[n])

        def part(at, index):
            total = 0.0
            for term in block:
                view = term.reshape((-1, 2, 1 << at) + rest)
                taken = lax.dynamic_index_in_dim(view, index, 1, keepdims=False)
                total = total + taken.reshape((-1,) + rest).astype(F32)
            return total

        if below[0] == below[1]:
            mine = jnp.where(first, bit[0], bit[1])
            keep, send = part(below[0], mine), part(below[0], 1 - mine)
        else:
            keep = jnp.where(first, part(below[0], bit[0]), part(below[1], bit[1]))
            send = jnp.where(first, part(below[0], 1 - bit[0]), part(below[1], 1 - bit[1]))
        route = [
            (core * dp + i, core * dp + (i ^ (1 << order[n])))
            for core, order in enumerate(orders)
            for i in range(dp)
        ]
        arrived = lax.ppermute(send.astype(BF16), ("segment", "dp"), route)
        total = keep + arrived.astype(F32)
        block = (total.astype(BF16),)
    return total.reshape(rest)


def on_device(inputs, image_count, cotangent, *params):
    dp = lax.axis_size("dp")
    core = lax.axis_index("segment")
    first = core == 0
    features = inputs.shape[3]
    g1, b1, w_qkv, b_qv, w_out, b_out, g2, b2, w_up, b_up, w_down, b_down = params
    units = w_up.shape[2]
    own_weights = (w_qkv, w_out, w_up, w_down)
    got_weights = tuple(swap_cores(w) for w in own_weights)
    zeros = jnp.zeros((1, features), F32)
    own_vec = pack_vectors(
        [g1, b1, b_qv[:, :features], zeros, b_qv[:, features:], b_out, g2, b2, b_down, b_up]
    )
    got_vec = swap_cores(own_vec)
    count = lax.dynamic_index_in_dim(image_count[:, 0], core, 0, keepdims=False)
    meta = jnp.stack([count, core.astype(jnp.int32)])
    mine, away, mine_wide, away_wide, mine_tall, away_tall = run_layers(
        meta, inputs, cotangent, (own_vec, got_vec), (own_weights, got_weights)
    )
    got_wide = swap_cores(away_wide)
    away_tall, got_wide = lax.optimization_barrier((away_tall, got_wide))
    got_tall = swap_cores(away_tall)
    got = swap_cores(away)
    bits = dp.bit_length() - 1
    near = list(range(min(bits, 3)))
    far = list(range(len(near), bits))

    def turned(by):
        return near[by % len(near) :] + near[: by % len(near)] + far

    wide = reduce_shards(mine_wide, got_wide, (turned(0), turned(2)), first)
    tall = reduce_shards(mine_tall, got_tall, (turned(1), turned(1)), first)
    both = jnp.stack([jnp.where(first, mine, got), jnp.where(first, got, mine)], axis=1)
    share = features // dp
    g_up = wide[:, :units]
    g_qkv = wide[:, units : units + 3 * features]
    g_out = wide[:, units + 3 * features : units + 4 * features]
    columns = wide[:, units + 4 * features :]
    ln1_gain, ln1_bias, g_bo, ln2_gain, ln2_bias, g_bd = (columns[:, n] for n in range(6))
    g_bqv = columns[:, 6:8].reshape(2 * share)
    g_bup = columns[:, 8 : 8 + units // features].reshape(-1)
    outs = (ln1_gain, ln1_bias, g_qkv, g_bqv, g_out, g_bo, ln2_gain, ln2_bias, g_up, g_bup, tall, g_bd)
    return (both[0][None], both[1][None]) + tuple(o[None] for o in outs)


def solution(mesh):
    in_specs = (
        P(None, "dp", None, None),
        P(None, "dp"),
        P(None, "dp", None, None),
        P("segment", None),
        P("segment", None),
        P("segment", None, None),
        P("segment", None),
        P("segment", None, None),
        P("segment", None),
        P("segment", None),
        P("segment", None),
        P("segment", None, None),
        P("segment", None),
        P("segment", None, None),
        P("segment", None),
    )
    out_specs = (
        P("segment", None, "dp", None, None),
        P("segment", None, "dp", None, None),
        P("segment", "dp"),
        P("segment", "dp"),
        P("segment", "dp", None),
        P("segment", "dp"),
        P("segment", "dp", None),
        P("segment", "dp"),
        P("segment", "dp"),
        P("segment", "dp"),
        P("segment", "dp", None),
        P("segment", "dp"),
        P("segment", "dp", None),
        P("segment", "dp"),
    )
    return jax.shard_map(
        on_device, mesh=mesh, in_specs=in_specs, out_specs=out_specs, check_vma=False
    )
```

time: 191 us -> 166 us (0.87)
  starting transfers between devices: 79.8 us -> 15.4 us
  Pallas kernels: 43.5 us -> 86.8 us
  other arithmetic: 10.8 us -> 15.6 us
  waiting for transfers between devices: 29.5 us -> 24.9 us
  local copies, waits for them, and re-layouts: 26.2 us -> 21.9 us
    ppermute x8, starting transfers between devices: 66.7 us -> 2.25 us  [swap_cores(): return lax.ppermute(block, 'segment', [(0, 1), (1, 0)])]
    pallas_call x1, Pallas kernels: 43.5 us -> 85.3 us  [run_layers(): pl.pallas_call(lambda *refs: layers_kernel(padded, keys, *refs), grid_spe...]
    unnamed x33 -> x18, local copies, waits for them, and re-layouts: 17.1 us -> 10.9 us
    ppermute x8, waiting for transfers between devices: 6.01 us -> 0.25 us  [swap_cores(): return lax.ppermute(block, 'segment', [(0, 1), (1, 0)])]
    convert_element_type x1 -> x2, other arithmetic: 1.71 us -> 4.42 us  [reduce_shards(): arrived = lax.ppermute(send.astype(BF16), ('segment', 'dp'), route)]
    another operation x2, other arithmetic: 0.93 us -> 2.97 us  [on_device(): jnp.stack([jnp.where(first, mine, got), jnp.where(first, got, mine)], axi...]
  transfers between devices with their start and end apart: 16 -> 16, of which waited for: 8 -> 8; matrix products, arithmetic and copies ran while one was open for 16% -> 19% of each run, Pallas kernels for 0% -> 1%
where the time goes in v3:
time: 166 us; the launch traced here: 165 us
  Pallas kernels  86.8 us (52%)
  waiting for transfers between devices  24.9 us (15%)
  local copies, waits for them, and re-layouts  21.9 us (13%)
  other arithmetic  15.6 us (9%)
  starting transfers between devices  15.4 us (9%)
    pallas_call x1, Pallas kernels, run_layers(): pl.pallas_call(lambda *refs: layers_kernel(padded, keys, *refs), grid_spe...  85.3 us
    ppermute x8, waiting for transfers between devices, reduce_shards(): arrived = lax.ppermute(send.astype(BF16), ('segment', 'dp'), route)  24.7 us
    ppermute x8, starting transfers between devices, reduce_shards(): arrived = lax.ppermute(send.astype(BF16), ('segment', 'dp'), route)  13.1 us
    unnamed x18, local copies, waits for them, and re-layouts  10.9 us
    convert_element_type x2, other arithmetic, reduce_shards(): arrived = lax.ppermute(send.astype(BF16), ('segment', 'dp'), route)  4.42 us
    pallas_call x1, local copies, waits for them, and re-layouts, run_layers(): pl.pallas_call(lambda *refs: layers_kernel(padded, keys, *refs), grid_spe...  4.28 us
    add x2, other arithmetic, part(): total = total + taken.reshape((-1,) + rest).astype(F32)  3.36 us
  transfers between devices with their start and end apart: 16, of which 8 were waited for; matrix products, arithmetic and copies ran while one was open for 19% of the time, Pallas kernels for 1%

profile of v3, /device:TPU:0, one launch (start us, length us, event | category | flops | bytes accessed | tf_op | source)
XLA Modules:
  0.0 165.4 jit_solution(8914803728993748146)
XLA Ops:
  1.8 1.3 fusion.9
  3.6 1.4 shard_map.254.refs_3_
  6.1 1.2 pad_add_fusion.refs_0_
  7.3 3.0 %copy.49.refs_1_ = bf16[2,6,197,384]{3,2,1,0:T(8,128)(2,1)} copy(bf16[2,6,197,384]{3,0,2,1:T(2,128)(2,1)} %param.15) | data formatting | bytes 3631104 | tf_op args[0]
  10.3 1.5 copy.50.refs_2_
  13.0 85.3 %shard_map.255 = (bf16[2,6,197,384]{3,2,1,0:T(8,128)(2,1)}, bf16[2,6,197,384]{3,2,1,0:T(8,128)(2,1)}, bf16[384,3200]{1,0:T(8,128)(2,1)}, bf16[384,3200]{1,0:T(8,...) custom-call(s32[2]{0:T(128)} %pad_add_fusion.refs_0_, bf16[2,6,197,384]{3,2,1,0:T(8,128)(2,1)} %copy.49.refs_1_, ...), custom_call_target="tpu_custom_call" | custom-call | flops 80000000000 | bytes 30000000 | tf_op jit(solution)/shard_map/pallas_call | solution.py:581
  98.4 4.3 %copy.51 = bf16[2,6,197,384]{3,0,2,1:T(2,128)(2,1)} copy(bf16[2,6,197,384]{3,2,1,0:T(8,128)(2,1)} %get-tuple-element.23) | data formatting | bytes 3631104 | tf_op jit(solution)/shard_map/pallas_call | solution.py:581
  103.5 1.6 convert_add_fusion
  105.1 2.9 %fusion = bf16[8,24,3200]{2,1,0:T(8,128)(2,1)} fusion(bf16[2,1,4,24,3200]{4,3,2,1,0:T(8,128)(2,1)S(1)} %convert_add_fusion, bf16[8,2,1,24,3200]{4,3,1,0,2:T(8,128)(2,1)} %bitcast.5, s32[]{:T(128)S(6)} %select_n.105, bf16[8,2,1,24,3200]{4,3,1,0,2:T(8,128)(2,1)S(1)} %bitcast.77, pred[]{:T(512)S(6)} %eq.3), kind=kLoop, calls=%fused_computation.3 | loop fusion | flops 2457600 | bytes 4915205 | tf_op jit(solution)/shard_map/convert_element_type | solution.py:650
  108.0 2.8 %collective-permute-start.7 = (bf16[8,24,3200]{2,1,0:T(8,128)(2,1)}, bf16[8,24,3200]{2,1,0:T(8,128)(2,1)}, u32[]{:S(2)}, u32[]{:S(2)}) collective-permute-start(bf16[8,24,3200]{2,1,0:T(8,128)(2,1)} %fusion), channel_id=1, source_target_pairs={{0,1},{1,0},{2,3},{3,2},{4,5},{5,4},{6,7},{7,6},{8,9},{9,8},{10,11... | collective-permute-start | bytes 3686408 | tf_op jit(solution)/shard_map/ppermute | solution.py:650
  110.9 2.5 %select_bitcast_fusion = (bf16[2,1,6,197,384]{4,3,2,0,1:T(8,128)(2,1)S(1)}, bf16[2,1,6,197,384]{4,3,2,0,1:T(8,128)(2,1)S(1)}) fusion(bf16[2,6,197,384]{3,2,1,0:T(8,128)(2,1)} %get-tuple-element.22, pred[]{:T(512)S(6)} %eq.3, bf16[2,6,197,384]{3,0,2,1:T(2,128)(2,1)} %collective-permute-done.5), kind=kLoop, calls=%fused_computation.11 | loop fusion | flops 1815552 | bytes 7262209 | tf_op jit(solution)/shard_map/stack | solution.py:688
  113.4 1.7 %convert_add_fusion.1 = f32[2,1,4,24,3200]{4,3,2,1,0:T(8,128)S(1)} fusion(bf16[2,2,4,24,3200]{4,3,2,1,0:T(8,128)(2,1)} %bitcast.8, s32[]{:T(128)S(6)} %select_n.103, bf16[2,2,4,24,3200]{4,3,2,1,0:T(8,128)(2,1)S(1)} %bitcast.78), kind=kLoop, calls=%fused_computation.8 | loop fusion | flops 1843200 | bytes 4915204 | tf_op jit(solution)/shard_map/add | solution.py:636
  115.2 1.5 add_convert_fusion
  116.7 1.6 collective-permute-start.12
  118.3 7.6 %collective-permute-done.7 = bf16[8,24,3200]{2,1,0:T(8,128)(2,1)} collective-permute-done((bf16[8,24,3200]{2,1,0:T(8,128)(2,1)}, bf16[8,24,3200]{2,1,0:T(8,128)(2,1)}, u32[]{:S(2)}, u32[]{:S(2)}) %collective-permute-start.7) | collective-permute-done | bytes 1228832 | tf_op jit(solution)/shard_map/ppermute | solution.py:650
  125.9 2.4 %fusion.2 = bf16[8,24,3200]{2,1,0:T(8,128)(2,1)S(1)} fusion(f32[2,1,4,24,3200]{4,3,2,1,0:T(8,128)S(1)} %convert_add_fusion.1, bf16[8,24,3200]{2,1,0:T(8,128)(2,1)} %collective-permute-done.7, bf16[8,2,1,24,3200]{4,3,1,0,2:T(8,128)(2,1)} %bitcast.5, s32[]{:T(128)S(6)} %select_n.102, bf16[8,2,1,24,3200]{4,3,1,0,2:T(8,128)(2,1)S(1)} %bitcast.79, pred[]{:T(512)S(6)} %eq.3), kind=kLoop, calls=%fused_computation.6 | loop fusion | flops 4300800 | bytes 7372805 | tf_op jit(solution)/shard_map/convert_element_type | solution.py:652
  128.4 1.6 collective-permute-start.8
  130.4 2.6 %copy.58 = bf16[1,2,6,197,384]{4,1,3,2,0:T(2,128)(2,1)} copy(bf16[1,2,6,197,384]{4,3,2,0,1:T(8,128)(2,1)S(1)} %get-tuple-element.93) | data formatting | bytes 3631104
  133.0 2.6 %copy.59 = bf16[1,2,6,197,384]{4,1,3,2,0:T(2,128)(2,1)} copy(bf16[1,2,6,197,384]{4,3,2,0,1:T(8,128)(2,1)S(1)} %get-tuple-element.92) | data formatting | bytes 3631104
  135.8 1.7 %collective-permute-start.13 = (bf16[4,96,384]{2,1,0:T(8,128)(2,1)S(1)}, bf16[4,96,384]{2,1,0:T(8,128)(2,1)S(1)}, u32[]{:S(2)}, u32[]{:S(2)}) collective-permute-start(bf16[4,96,384]{2,1,0:T(8,128)(2,1)S(1)} %bitcast.89), channel_id=1, source_target_pairs={{0,4},{1,5},{2,6},{3,7},{4,0},{5,1},{6,2},{7,3},{8,12},{9,13},{10,... | collective-permute-start | bytes 884744 | tf_op jit(solution)/shard_map/ppermute | solution.py:650
  137.5 1.1 collective-permute-done.8
  138.8 2.0 %collective-permute-start.9 = (bf16[2,24,3200]{2,1,0:T(8,128)(2,1)S(1)}, bf16[2,24,3200]{2,1,0:T(8,128)(2,1)S(1)}, u32[]{:S(2)}, u32[]{:S(2)}) collective-permute-start(bf16[2,24,3200]{2,1,0:T(8,128)(2,1)S(1)} %dynamic-slice_bitcast_fusion.1), channel_id=1, source_target_pairs={{0,4},{1,5},{2,6},{3,7},{4,0},{5,1},{6,2},{7,3},{8,12},{9,13},{10,... | collective-permute-start | bytes 921608 | tf_op jit(solution)/shard_map/ppermute | solution.py:650
  140.7 3.6 %collective-permute-done.13 = bf16[4,96,384]{2,1,0:T(8,128)(2,1)S(1)} collective-permute-done((bf16[4,96,384]{2,1,0:T(8,128)(2,1)S(1)}, bf16[4,96,384]{2,1,0:T(8,128)(2,1)S(1)}, u32[]{:S(2)}, u32[]{:S(2)}) %collective-permute-start.13) | collective-permute-done | bytes 294944 | tf_op jit(solution)/shard_map/ppermute | solution.py:650
  144.9 2.7 %collective-permute-done.9 = bf16[2,24,3200]{2,1,0:T(8,128)(2,1)S(1)} collective-permute-done((bf16[2,24,3200]{2,1,0:T(8,128)(2,1)S(1)}, bf16[2,24,3200]{2,1,0:T(8,128)(2,1)S(1)}, u32[]{:S(2)}, u32[]{:S(2)}) %collective-permute-start.9) | collective-permute-done | bytes 307232 | tf_op jit(solution)/shard_map/ppermute | solution.py:650
  147.7 2.0 %collective-permute-done.14 = bf16[2,96,384]{2,1,0:T(8,128)(2,1)S(1)} collective-permute-done((bf16[2,96,384]{2,1,0:T(8,128)(2,1)S(1)}, bf16[2,96,384]{2,1,0:T(8,128)(2,1)S(1)}, u32[]{:S(2)}, u32[]{:S(2)}) %collective-permute-start.14) | collective-permute-done | bytes 147488 | tf_op jit(solution)/shard_map/ppermute | solution.py:650
  149.8 2.5 %collective-permute-start.15 = (bf16[1,96,384]{2,1,0:T(8,128)(2,1)S(1)}, bf16[1,96,384]{2,1,0:T(8,128)(2,1)S(1)}, u32[]{:S(2)}, u32[]{:S(2)}) collective-permute-start(bf16[1,96,384]{2,1,0:T(8,128)(2,1)S(1)} %constant_dynamic-slice_fusion.3), channel_id=1, source_target_pairs={{0,8},{1,9},{2,10},{3,11},{4,12},{5,13},{6,14},{7,15},{8,0},{9,1},... | collective-permute-start | bytes 221192 | tf_op jit(solution)/shard_map/ppermute | solution.py:650
  152.8 5.1 %collective-permute-done.15 = bf16[1,96,384]{2,1,0:T(8,128)(2,1)S(1)} collective-permute-done((bf16[1,96,384]{2,1,0:T(8,128)(2,1)S(1)}, bf16[1,96,384]{2,1,0:T(8,128)(2,1)S(1)}, u32[]{:S(2)}, u32[]{:S(2)}) %collective-permute-start.15) | collective-permute-done | bytes 73760 | tf_op jit(solution)/shard_map/ppermute | solution.py:650
  158.0 0.7 convert_add_fusion.7
  158.6 2.6 %collective-permute-done.10 = bf16[1,24,3200]{2,1,0:T(8,128)(2,1)S(1)} collective-permute-done((bf16[1,24,3200]{2,1,0:T(8,128)(2,1)S(1)}, bf16[1,24,3200]{2,1,0:T(8,128)(2,1)S(1)}, u32[]{:S(2)}, u32[]{:S(2)}) %collective-permute-start.10) | collective-permute-done | bytes 153632 | tf_op jit(solution)/shard_map/ppermute | solution.py:650
  161.3 0.7 slice_bitcast_fusion
  162.0 0.7 slice_bitcast_fusion.1
  163.4 0.8 slice_reduce_fusion
  (53 shorter events, 8.9 us)
Async XLA Ops:
  0.6 4.8 %copy-start = (s32[2,1]{0,1:T(1,128)S(1)}, s32[2,1]{0,1:T(1,128)}, u32[]{:S(2)}) copy-start(s32[2,1]{0,1:T(1,128)} %param.16) | copy-start | bytes 28
  0.7 11.2 %collective-permute-start.3 = (bf16[1,384,1536]{2,1,0:T(8,128)(2,1)}, bf16[1,384,1536]{2,1,0:T(8,128)(2,1)S(1)}, u32[]{:S(2)}, u32[]{:S(2)}) collective-permute-start(bf16[1,384,1536]{2,1,0:T(8,128)(2,1)} %refs_7_.3), channel_id=1, source_target_pairs={{0,16},{16,0},{1,17},{17,1},{2,18},{18,2},{3,19},{19,3},{4,20},{20... | collective-permute-start | bytes 3538952 | tf_op jit(solution)/shard_map/ppermute | solution.py:615
  1.2 10.7 %collective-permute-start.4 = (bf16[1,1536,384]{2,1,0:T(8,128)(2,1)}, bf16[1,1536,384]{2,1,0:T(8,128)(2,1)}, u32[]{:S(2)}, u32[]{:S(2)}) collective-permute-start(bf16[1,1536,384]{2,1,0:T(8,128)(2,1)} %refs_8_.3), channel_id=1, source_target_pairs={{0,16},{16,0},{1,17},{17,1},{2,18},{18,2},{3,19},{19,3},{4,20},{20... | collective-permute-start | bytes 3538952 | tf_op jit(solution)/shard_map/ppermute | solution.py:615
  1.3 10.6 %collective-permute-start.1 = (bf16[1,384,1152]{2,1,0:T(8,128)(2,1)}, bf16[1,384,1152]{2,1,0:T(8,128)(2,1)}, u32[]{:S(2)}, u32[]{:S(2)}) collective-permute-start(bf16[1,384,1152]{2,1,0:T(8,128)(2,1)} %refs_5_.3), channel_id=1, source_target_pairs={{0,16},{16,0},{1,17},{17,1},{2,18},{18,2},{3,19},{19,3},{4,20},{20... | collective-permute-start | bytes 2654216 | tf_op jit(solution)/shard_map/ppermute | solution.py:615
  1.7 10.2 %collective-permute-start.2 = (bf16[1,384,384]{2,1,0:T(8,128)(2,1)}, bf16[1,384,384]{2,1,0:T(8,128)(2,1)S(1)}, u32[]{:S(2)}, u32[]{:S(2)}) collective-permute-start(bf16[1,384,384]{2,1,0:T(8,128)(2,1)} %refs_6_.3), channel_id=1, source_target_pairs={{0,16},{16,0},{1,17},{17,1},{2,18},{18,2},{3,19},{19,3},{4,20},{20... | collective-permute-start | bytes 884744 | tf_op jit(solution)/shard_map/ppermute | solution.py:615
  5.0 5.3 %copy-start.2 = (bf16[2,6,197,384]{3,0,2,1:T(2,128)(2,1)S(1)}, bf16[2,6,197,384]{3,0,2,1:T(2,128)(2,1)}, u32[]{:S(2)}) copy-start(bf16[2,6,197,384]{3,0,2,1:T(2,128)(2,1)} %param.17) | copy-start | bytes 5446660
  5.0 6.8 %collective-permute-start = (f32[1,4992]{1,0:T(1,128)}, f32[1,4992]{1,0:T(1,128)S(1)}, u32[]{:S(2)}, u32[]{:S(2)}) collective-permute-start(f32[1,4992]{1,0:T(1,128)} %shard_map.254.refs_3_), channel_id=1, source_target_pairs={{0,16},{16,0},{1,17},{17,1},{2,18},{18,2},{3,19},{19,3},{4,20},{20... | collective-permute-start | bytes 59912 | tf_op jit(solution)/shard_map/ppermute | solution.py:615
  11.9 0.6 copy-start.6
  11.9 0.7 copy-start.5
  11.9 1.1 copy-start.4
  98.3 5.1 %collective-permute-start.6 = (bf16[384,3200]{1,0:T(8,128)(2,1)}, bf16[384,3200]{1,0:T(8,128)(2,1)}, u32[]{:S(2)}, u32[]{:S(2)}) collective-permute-start(bf16[384,3200]{1,0:T(8,128)(2,1)} %get-tuple-element.26), channel_id=1, source_target_pairs={{0,16},{16,0},{1,17},{17,1},{2,18},{18,2},{3,19},{19,3},{4,20},{20... | collective-permute-start | bytes 7372808 | tf_op jit(solution)/shard_map/ppermute | solution.py:615
  98.4 5.1 %copy-start.1 = (bf16[384,3200]{1,0:T(8,128)(2,1)S(1)}, bf16[384,3200]{1,0:T(8,128)(2,1)}, u32[]{:S(2)}) copy-start(bf16[384,3200]{1,0:T(8,128)(2,1)} %get-tuple-element.24) | copy-start | bytes 7372804
  102.7 8.2 %collective-permute-start.5 = (bf16[2,6,197,384]{3,0,2,1:T(2,128)(2,1)}, bf16[2,6,197,384]{3,0,2,1:T(2,128)(2,1)}, u32[]{:S(2)}, u32[]{:S(2)}) collective-permute-start(bf16[2,6,197,384]{3,0,2,1:T(2,128)(2,1)} %copy.51), channel_id=1, source_target_pairs={{0,16},{16,0},{1,17},{17,1},{2,18},{18,2},{3,19},{19,3},{4,20},{20... | collective-permute-start | bytes 5446664 | tf_op jit(solution)/shard_map/ppermute | solution.py:615
  103.4 11.8 %collective-permute-start.11 = (bf16[1536,384]{1,0:T(8,128)(2,1)}, bf16[1536,384]{1,0:T(8,128)(2,1)}, u32[]{:S(2)}, u32[]{:S(2)}) collective-permute-start(bf16[1536,384]{1,0:T(8,128)(2,1)} %get-tuple-element.29), channel_id=1, source_target_pairs={{0,16},{16,0},{1,17},{17,1},{2,18},{18,2},{3,19},{19,3},{4,20},{20... | collective-permute-start | bytes 3538952 | tf_op jit(solution)/shard_map/ppermute | solution.py:615
  108.0 17.8 %collective-permute-start.7 = (bf16[8,24,3200]{2,1,0:T(8,128)(2,1)}, bf16[8,24,3200]{2,1,0:T(8,128)(2,1)}, u32[]{:S(2)}, u32[]{:S(2)}) collective-permute-start(bf16[8,24,3200]{2,1,0:T(8,128)(2,1)} %fusion), channel_id=1, source_target_pairs={{0,1},{1,0},{2,3},{3,2},{4,5},{5,4},{6,7},{7,6},{8,9},{9,8},{10,11... | collective-permute-start | bytes 3686408 | tf_op jit(solution)/shard_map/ppermute | solution.py:650
  113.4 1.8 %copy-start.3 = (bf16[1536,384]{1,0:T(8,128)(2,1)S(1)}, bf16[1536,384]{1,0:T(8,128)(2,1)}, u32[]{:S(2)}) copy-start(bf16[1536,384]{1,0:T(8,128)(2,1)} %get-tuple-element.28) | copy-start | bytes 3538948
  116.7 18.9 %collective-permute-start.12 = (bf16[8,96,384]{2,1,0:T(8,128)(2,1)S(1)}, bf16[8,96,384]{2,1,0:T(8,128)(2,1)S(1)}, u32[]{:S(2)}, u32[]{:S(2)}) collective-permute-start(bf16[8,96,384]{2,1,0:T(8,128)(2,1)S(1)} %bitcast.88), channel_id=1, source_target_pairs={{0,2},{1,3},{2,0},{3,1},{4,6},{5,7},{6,4},{7,5},{8,10},{9,11},{10,... | collective-permute-start | bytes 1769480 | tf_op jit(solution)/shard_map/ppermute | solution.py:650
  128.4 10.2 %collective-permute-start.8 = (bf16[4,24,3200]{2,1,0:T(8,128)(2,1)S(1)}, bf16[4,24,3200]{2,1,0:T(8,128)(2,1)S(1)}, u32[]{:S(2)}, u32[]{:S(2)}) collective-permute-start(bf16[4,24,3200]{2,1,0:T(8,128)(2,1)S(1)} %dynamic-slice_bitcast_fusion), channel_id=1, source_target_pairs={{0,2},{1,3},{2,0},{3,1},{4,6},{5,7},{6,4},{7,5},{8,10},{9,11},{10,... | collective-permute-start | bytes 1843208 | tf_op jit(solution)/shard_map/ppermute | solution.py:650
  135.8 8.5 %collective-permute-start.13 = (bf16[4,96,384]{2,1,0:T(8,128)(2,1)S(1)}, bf16[4,96,384]{2,1,0:T(8,128)(2,1)S(1)}, u32[]{:S(2)}, u32[]{:S(2)}) collective-permute-start(bf16[4,96,384]{2,1,0:T(8,128)(2,1)S(1)} %bitcast.89), channel_id=1, source_target_pairs={{0,4},{1,5},{2,6},{3,7},{4,0},{5,1},{6,2},{7,3},{8,12},{9,13},{10,... | collective-permute-start | bytes 884744 | tf_op jit(solution)/shard_map/ppermute | solution.py:650
  138.8 8.8 %collective-permute-start.9 = (bf16[2,24,3200]{2,1,0:T(8,128)(2,1)S(1)}, bf16[2,24,3200]{2,1,0:T(8,128)(2,1)S(1)}, u32[]{:S(2)}, u32[]{:S(2)}) collective-permute-start(bf16[2,24,3200]{2,1,0:T(8,128)(2,1)S(1)} %dynamic-slice_bitcast_fusion.1), channel_id=1, source_target_pairs={{0,4},{1,5},{2,6},{3,7},{4,0},{5,1},{6,2},{7,3},{8,12},{9,13},{10,... | collective-permute-start | bytes 921608 | tf_op jit(solution)/shard_map/ppermute | solution.py:650
  144.5 5.2 %collective-permute-start.14 = (bf16[2,96,384]{2,1,0:T(8,128)(2,1)S(1)}, bf16[2,96,384]{2,1,0:T(8,128)(2,1)S(1)}, u32[]{:S(2)}, u32[]{:S(2)}) collective-permute-start(bf16[2,96,384]{2,1,0:T(8,128)(2,1)S(1)} %dynamic-slice_bitcast_fusion.2), channel_id=1, source_target_pairs={{0,1},{1,0},{2,3},{3,2},{4,5},{5,4},{6,7},{7,6},{8,9},{9,8},{10,11... | collective-permute-start | bytes 442376 | tf_op jit(solution)/shard_map/ppermute | solution.py:650
  149.8 8.2 %collective-permute-start.15 = (bf16[1,96,384]{2,1,0:T(8,128)(2,1)S(1)}, bf16[1,96,384]{2,1,0:T(8,128)(2,1)S(1)}, u32[]{:S(2)}, u32[]{:S(2)}) collective-permute-start(bf16[1,96,384]{2,1,0:T(8,128)(2,1)S(1)} %constant_dynamic-slice_fusion.3), channel_id=1, source_target_pairs={{0,8},{1,9},{2,10},{3,11},{4,12},{5,13},{6,14},{7,15},{8,0},{9,1},... | collective-permute-start | bytes 221192 | tf_op jit(solution)/shard_map/ppermute | solution.py:650
  152.3 8.9 %collective-permute-start.10 = (bf16[1,24,3200]{2,1,0:T(8,128)(2,1)S(1)}, bf16[1,24,3200]{2,1,0:T(8,128)(2,1)S(1)}, u32[]{:S(2)}, u32[]{:S(2)}) collective-permute-start(bf16[1,24,3200]{2,1,0:T(8,128)(2,1)S(1)} %constant_dynamic-slice_fusion.2), channel_id=1, source_target_pairs={{0,8},{1,9},{2,10},{3,11},{4,12},{5,13},{6,14},{7,15},{8,0},{9,1},... | collective-permute-start | bytes 460808 | tf_op jit(solution)/shard_map/ppermute | solution.py:650

commit v4 on v3

--- a/solution.py
+++ b/solution.py
@@ -40,11 +40,14 @@
     return dx, grad * hat
 
 
+def reciprocal(x):
+    guess = pl.reciprocal(x, approx=True)
+    return guess * (2.0 - x * guess)
+
+
 def gelu_and_slope(x):
     bell = jnp.exp(x * x * -0.5)
-    under = 1.0 + jnp.abs(x) * (0.3275911 * 0.7071067811865476)
-    t = pl.reciprocal(under, approx=True)
-    t = t * (2.0 - under * t)
+    t = reciprocal(1.0 + jnp.abs(x) * (0.3275911 * 0.7071067811865476))
     poly = t * (
         0.5 * 0.254829592
         + t
@@ -65,7 +68,7 @@
     return total
 
 
-def row_chunks(total, size=32):
+def row_chunks(total, size=64):
     return [(at, min(size, total - at)) for at in range(0, total, size)]
 
 
@@ -76,7 +79,8 @@
 def layers_kernel(
     padded,
     keys,
-    meta,
+    counts,
+    which,
     h_ref,
     cot_ref,
     own_vec,
@@ -133,8 +137,8 @@
 ):
     step = pl.program_id(0)
     last = pl.num_programs(0) - 1
-    count = meta[0]
-    core = meta[1]
+    core = which[0]
+    count = counts[core]
     running = step * GROUP < count
     tokens, features = h_ref.shape[2:]
     heads = features // HEAD
@@ -241,7 +245,7 @@
                 real = lax.broadcasted_iota(jnp.int32, (size, keys), 1) < tokens
                 s = jnp.where(real, scores[u % 2, at : at + size], -1e30)
                 e = jnp.exp(s - jnp.max(s, axis=-1, keepdims=True))
-                p = e * (1.0 / jnp.sum(e, axis=-1, keepdims=True))
+                p = e * reciprocal(jnp.sum(e, axis=-1, keepdims=True))
                 weights[layer, j, n, at : at + size] = p.astype(BF16)
 
         def attend(u):
@@ -253,7 +257,7 @@
             middle[layer, image[j]] = dot(attended[layer, image[j]], w_out[layer])
 
         def norm_two(j):
-            for at, size in row_chunks(padded, 16):
+            for at, size in row_chunks(padded):
                 at = j * padded + at
                 value = middle[layer, at : at + size] + hidden[layer, at : at + size]
                 value = value + vec(layer, at_bo)
@@ -340,7 +344,7 @@
 
         def norm_two(j):
             one, two, three = (jnp.zeros((8, features), F32) for _ in range(3))
-            for at, size in row_chunks(padded, 16):
+            for at, size in row_chunks(padded):
                 lines = slice(j * padded + at, j * padded + at + size)
                 grad = grad_norm[lines]
                 dx, by_hat = norm_backward(middle[layer, lines], grad, vec(layer, at_g2))
@@ -410,7 +414,7 @@
 
         def norm_one(j):
             one, two = (jnp.zeros((8, features), F32) for _ in range(2))
-            for at, size in row_chunks(padded, 16):
+            for at, size in row_chunks(padded):
                 lines = slice(j * padded + at, j * padded + at + size)
                 grad = grad_norm[lines]
                 dx, by_hat = norm_backward(hidden[layer, lines], grad, vec(layer, at_g1))
@@ -452,10 +456,11 @@
             position = lax.broadcasted_iota(jnp.int32, (128, size), 1)
             row = lax.broadcasted_iota(jnp.int32, (128, size), 0)
             if each > 1:
-                total = jnp.where(row - first_line == position % each, total, 0.0)
+                total = jnp.where(row - first_line == (position & (each - 1)), total, 0.0)
             target = lax.broadcasted_iota(jnp.int32, (features, size), 0)
             source = lax.broadcasted_iota(jnp.int32, (features, size), 1)
-            pick = jnp.where(source // each == target, 1.0, 0.0).astype(BF16)
+            inside = (source >= target * each) & (source < target * each + each)
+            pick = jnp.where(inside, 1.0, 0.0).astype(BF16)
             columns = columns + dot_nt(pick, total.astype(BF16))
         wide[layer, :, units + 4 * features :] = columns.astype(BF16)
 
@@ -513,7 +518,7 @@
                 store(layer, kind, mine).wait()
 
 
-def run_layers(meta, inputs, cotangent, vectors, weights):
+def run_layers(counts, which, inputs, cotangent, vectors, weights):
     slots, tokens, features = inputs.shape[1:]
     padded = -(-tokens // 16) * 16
     keys = -(-tokens // 128) * 128
@@ -523,9 +528,9 @@
     units = weights[0][2].shape[2]
     packed = vectors[0].shape[1]
     wide = units + 4 * features + 128
-    images = pl.BlockSpec((1, GROUP, tokens, features), lambda i, meta: (meta[1], i, 0, 0))
-    kinds = pl.BlockSpec((2, GROUP, tokens, features), lambda i, meta: (0, i, 0, 0))
-    vector = pl.BlockSpec((1, packed), lambda i, meta: (0, 0))
+    images = pl.BlockSpec((1, GROUP, tokens, features), lambda i, counts, which: (which[0], i, 0, 0))
+    kinds = pl.BlockSpec((2, GROUP, tokens, features), lambda i, counts, which: (0, i, 0, 0))
+    vector = pl.BlockSpec((1, packed), lambda i, counts, which: (0, 0))
     anywhere = pl.BlockSpec(memory_space=pl.ANY)
     both = (
         ((features, 3 * features), BF16),
@@ -581,7 +586,7 @@
     return pl.pallas_call(
         lambda *refs: layers_kernel(padded, keys, *refs),
         grid_spec=pltpu.PrefetchScalarGridSpec(
-            num_scalar_prefetch=1,
+            num_scalar_prefetch=2,
             grid=(steps,),
             in_specs=[images, images, vector, vector] + [anywhere] * 8,
             out_specs=[kinds, kinds] + [anywhere] * 4,
@@ -596,17 +601,26 @@
         cost_estimate=pl.CostEstimate(
             flops=80_000_000_000, bytes_accessed=30_000_000, transcendentals=0
         ),
-    )(meta, inputs, cotangent, *vectors, *weights[0], *weights[1])
-
-
-def pack_vectors(arrays):
-    total = sum(a.shape[1] for a in arrays)
+    )(counts, which, inputs, cotangent, *vectors, *weights[0], *weights[1])
+
+
+def pack_vectors(g1, b1, b_qv, *rest):
+    features = g1.shape[1]
+    arrays = (g1, b1, b_qv) + rest
+    total = sum(a.shape[1] for a in arrays) + features
 
     def body(*refs):
+        out = refs[-1]
         at = 0
-        for ref in refs[:-1]:
-            refs[-1][:, at : at + ref.shape[1]] = ref[...]
-            at += ref.shape[1]
+        for n, ref in enumerate(refs[:-1]):
+            if n == 2:
+                out[:, at : at + features] = ref[:, :features]
+                out[:, at + features : at + 2 * features] = jnp.zeros((1, features), F32)
+                out[:, at + 2 * features : at + 3 * features] = ref[:, features:]
+                at += 3 * features
+            else:
+                out[:, at : at + ref.shape[1]] = ref[...]
+                at += ref.shape[1]
 
     return pl.pallas_call(body, out_shape=jax.ShapeDtypeStruct((1, total), F32))(*arrays)
 
@@ -620,37 +634,81 @@
     me = lax.axis_index("dp")
     bits = dp.bit_length() - 1
     rest = (mine.shape[0] // dp, mine.shape[1])
-    block = (mine, got)
+    terms = (mine, got)
     held = [list(range(bits)) for _ in orders]
+    first_send = None
     for n in range(bits):
         below = [left.index(order[n]) for order, left in zip(orders, held)]
         bit = [(me >> order[n]) & 1 for order in orders]
         for order, left in zip(orders, held):
             left.remove(order[n])
 
-        def part(at, index):
-            total = 0.0
-            for term in block:
+        def slices(at, index):
+            taken = []
+            for term in terms:
                 view = term.reshape((-1, 2, 1 << at) + rest)
-                taken = lax.dynamic_index_in_dim(view, index, 1, keepdims=False)
-                total = total + taken.reshape((-1,) + rest).astype(F32)
-            return total
-
-        if below[0] == below[1]:
-            mine = jnp.where(first, bit[0], bit[1])
-            keep, send = part(below[0], mine), part(below[0], 1 - mine)
-        else:
-            keep = jnp.where(first, part(below[0], bit[0]), part(below[1], bit[1]))
-            send = jnp.where(first, part(below[0], 1 - bit[0]), part(below[1], 1 - bit[1]))
+                part = lax.dynamic_index_in_dim(view, index, 1, keepdims=False)
+                taken.append(part.reshape((-1,) + rest))
+            return taken
+
+        def half(other):
+            if below[0] == below[1]:
+                index = jnp.where(first, bit[0], bit[1])
+                taken = slices(below[0], 1 - index if other else index)
+            else:
+                index = [1 - b if other else b for b in bit]
+                sides = zip(slices(below[0], index[0]), slices(below[1], index[1]))
+                taken = [jnp.where(first, a, b) for a, b in sides]
+            total = sum(part.astype(F32) for part in taken)
+            return total.astype(BF16)
+
+        send = half(True)
+        first_send = send if n == 0 else first_send
+        keep = half(False)
+        if n == 0:
+            keep, _ = lax.optimization_barrier((keep, send))
         route = [
             (core * dp + i, core * dp + (i ^ (1 << order[n])))
             for core, order in enumerate(orders)
             for i in range(dp)
         ]
-        arrived = lax.ppermute(send.astype(BF16), ("segment", "dp"), route)
-        total = keep + arrived.astype(F32)
-        block = (total.astype(BF16),)
-    return total.reshape(rest)
+        arrived = lax.ppermute(send, ("segment", "dp"), route)
+        terms = (keep, arrived)
+    return tuple(t.reshape(rest) for t in terms), first_send
+
+
+def split_wide(terms, features, units):
+    share = terms[0].shape[0]
+    plain = 6
+
+    def body(one, two, up, qkv, out, qv, bias_up, *vectors):
+        total = one[...].astype(F32) + two[...].astype(F32)
+        up[0] = total[:, :units]
+        qkv[0] = total[:, units : units + 3 * features]
+        out[0] = total[:, units + 3 * features : units + 4 * features]
+        columns = total[:, units + 4 * features :]
+
+        def spread(ref, first_column):
+            size = ref.shape[1]
+            width = size // share
+            lane = lax.broadcasted_iota(jnp.int32, (share, size), 1)
+            row = lax.broadcasted_iota(jnp.int32, (share, size), 0)
+            value = jnp.zeros((share, size), F32)
+            for n in range(width):
+                column = columns[:, first_column + n : first_column + n + 1]
+                value = value + jnp.where(lane == row * width + n, column, 0.0)
+            ref[...] = jnp.sum(value, axis=0, keepdims=True)
+
+        for n, ref in enumerate(vectors):
+            spread(ref, n)
+        spread(qv, plain)
+        spread(bias_up, plain + 2)
+
+    shapes = [(1, share, units), (1, share, 3 * features), (1, share, features)]
+    shapes += [(1, 2 * share), (1, units // features * share)] + [(1, share)] * plain
+    return pl.pallas_call(
+        body, out_shape=[jax.ShapeDtypeStruct(shape, F32) for shape in shapes]
+    )(*terms)
 
 
 def on_device(inputs, image_count, cotangent, *params):
@@ -662,15 +720,11 @@
     units = w_up.shape[2]
     own_weights = (w_qkv, w_out, w_up, w_down)
     got_weights = tuple(swap_cores(w) for w in own_weights)
-    zeros = jnp.zeros((1, features), F32)
-    own_vec = pack_vectors(
-        [g1, b1, b_qv[:, :features], zeros, b_qv[:, features:], b_out, g2, b2, b_down, b_up]
-    )
+    own_vec = pack_vectors(g1, b1, b_qv, b_out, g2, b2, b_down, b_up)
     got_vec = swap_cores(own_vec)
-    count = lax.dynamic_index_in_dim(image_count[:, 0], core, 0, keepdims=False)
-    meta = jnp.stack([count, core.astype(jnp.int32)])
+    counts, which = image_count.reshape(-1), core.astype(jnp.int32).reshape(1)
     mine, away, mine_wide, away_wide, mine_tall, away_tall = run_layers(
-        meta, inputs, cotangent, (own_vec, got_vec), (own_weights, got_weights)
+        counts, which, inputs, cotangent, (own_vec, got_vec), (own_weights, got_weights)
     )
     got_wide = swap_cores(away_wide)
     away_tall, got_wide = lax.optimization_barrier((away_tall, got_wide))
@@ -683,19 +737,15 @@
     def turned(by):
         return near[by % len(near) :] + near[: by % len(near)] + far
 
-    wide = reduce_shards(mine_wide, got_wide, (turned(0), turned(2)), first)
-    tall = reduce_shards(mine_tall, got_tall, (turned(1), turned(1)), first)
+    wide, _ = reduce_shards(mine_wide, got_wide, (turned(0), turned(2)), first)
+    tall, tall_sent = reduce_shards(mine_tall, got_tall, (turned(1), turned(1)), first)
+    got, _ = lax.optimization_barrier((got, tall_sent))
     both = jnp.stack([jnp.where(first, mine, got), jnp.where(first, got, mine)], axis=1)
-    share = features // dp
-    g_up = wide[:, :units]
-    g_qkv = wide[:, units : units + 3 * features]
-    g_out = wide[:, units + 3 * features : units + 4 * features]
-    columns = wide[:, units + 4 * features :]
-    ln1_gain, ln1_bias, g_bo, ln2_gain, ln2_bias, g_bd = (columns[:, n] for n in range(6))
-    g_bqv = columns[:, 6:8].reshape(2 * share)
-    g_bup = columns[:, 8 : 8 + units // features].reshape(-1)
-    outs = (ln1_gain, ln1_bias, g_qkv, g_bqv, g_out, g_bo, ln2_gain, ln2_bias, g_up, g_bup, tall, g_bd)
-    return (both[0][None], both[1][None]) + tuple(o[None] for o in outs)
+    g_up, g_qkv, g_out, g_bqv, g_bup, *vectors = split_wide(wide, features, units)
+    ln1_gain, ln1_bias, g_bo, ln2_gain, ln2_bias, g_bd = vectors
+    g_down = (tall[0].astype(F32) + tall[1].astype(F32))[None]
+    outs = (ln1_gain, ln1_bias, g_qkv, g_bqv, g_out, g_bo, ln2_gain, ln2_bias, g_up, g_bup)
+    return (both[0][None], both[1][None]) + outs + (g_down, g_bd)
 
 
 def solution(mesh):

time: 166 us -> 162 us (0.976)
  starting transfers between devices: 15.4 us -> 51.6 us
  Pallas kernels: 86.8 us -> 63.3 us
  waiting for transfers between devices: 24.9 us -> 12.3 us
  local copies, waits for them, and re-layouts: 21.9 us -> 18.4 us
    ppermute x8, starting transfers between devices: 13.1 us -> 49.4 us  [reduce_shards(): arrived = lax.ppermute(send, ('segment', 'dp'), route)]
    pallas_call x1, Pallas kernels: 85.3 us -> 60.1 us  [run_layers(): pl.pallas_call(lambda *refs: layers_kernel(padded, keys, *refs), grid_spe...]
    ppermute x8, waiting for transfers between devices: 24.7 us -> 12.1 us  [reduce_shards(): arrived = lax.ppermute(send, ('segment', 'dp'), route)]
    convert_element_type x8, other arithmetic: 7.34 us -> 11.7 us  [half(): return total.astype(BF16)]
    add x3 -> x1, other arithmetic: 4.03 us -> 0.69 us  [on_device(): g_down = (tall[0].astype(F32) + tall[1].astype(F32))[None]]
    unnamed x18 -> x24, local copies, waits for them, and re-layouts: 10.9 us -> 13.6 us
    broadcast_in_dim x4 -> x0, local copies, waits for them, and re-layouts: 2.51 us -> none  [the longest x3 1.94 us: on_device(): return (both[0][None], both[1][None]) + tuple((o[None] for o in outs))]
    slice x4 -> x0, local copies, waits for them, and re-layouts: 2.19 us -> none  [the longest x1 1.26 us: on_device(): b_qv[:, features:]]
  transfers between devices with their start and end apart: 16 -> 16, of which waited for: 8 -> 4; matrix products, arithmetic and copies ran while one was open for 19% -> 18% of each run, Pallas kernels for 1% -> 1%
where the time goes in v4:
time: 162 us; the launch traced here: 161 us
  Pallas kernels  63.3 us (39%)
  starting transfers between devices  51.6 us (32%)
  local copies, waits for them, and re-layouts  18.4 us (11%)
  other arithmetic  14.8 us (9%)
  waiting for transfers between devices  12.3 us (8%)
    pallas_call x1, Pallas kernels, run_layers(): pl.pallas_call(lambda *refs: layers_kernel(padded, keys, *refs), grid_spe...  60.1 us
    ppermute x8, starting transfers between devices, reduce_shards(): arrived = lax.ppermute(send, ('segment', 'dp'), route)  49.4 us
    unnamed x24, local copies, waits for them, and re-layouts  13.6 us
    ppermute x8, waiting for transfers between devices, reduce_shards(): arrived = lax.ppermute(send, ('segment', 'dp'), route)  12.1 us
    convert_element_type x8, other arithmetic, half(): return total.astype(BF16)  11.7 us
    pallas_call x1, local copies, waits for them, and re-layouts, run_layers(): pl.pallas_call(lambda *refs: layers_kernel(padded, keys, *refs), grid_spe...  4.28 us
  transfers between devices with their start and end apart: 16, of which 4 were waited for; matrix products, arithmetic and copies ran while one was open for 18% of the time, Pallas kernels for 1%

profile of v4, /device:TPU:0, one launch (start us, length us, event | category | flops | bytes accessed | tf_op | source)
XLA Modules:
  0.0 161.4 jit_solution(14522852837848624545)
XLA Ops:
  0.6 0.5 collective-permute-start.3
  1.8 1.4 shard_map.254.refs_4_
  3.6 3.2 %copy.37.refs_2_ = bf16[2,6,197,384]{3,2,1,0:T(8,128)(2,1)} copy(bf16[2,6,197,384]{3,0,2,1:T(2,128)(2,1)} %param.15) | data formatting | bytes 3631104 | tf_op args[0]
  6.8 1.5 copy.38.refs_3_
  8.3 0.9 copy-done.7
  9.3 1.0 copy-done.6
  10.3 60.1 %shard_map.255 = (bf16[2,6,197,384]{3,2,1,0:T(8,128)(2,1)}, bf16[2,6,197,384]{3,2,1,0:T(8,128)(2,1)}, bf16[384,3200]{1,0:T(8,128)(2,1)}, bf16[384,3200]{1,0:T(8,...) custom-call(s32[2]{0:T(128)} %bitcast.79, s32[1]{0:T(128)} %bitcast.1.refs_1_, ...), custom_call_target="tpu_custom_call" | custom-call | flops 80000000000 | bytes 30000000 | tf_op jit(solution)/shard_map/pallas_call | solution.py:586
  70.5 4.3 %copy.39 = bf16[2,6,197,384]{3,0,2,1:T(2,128)(2,1)} copy(bf16[2,6,197,384]{3,2,1,0:T(8,128)(2,1)} %get-tuple-element.37) | data formatting | bytes 3631104 | tf_op jit(solution)/shard_map/pallas_call | solution.py:586
  74.8 0.5 collective-permute-start.5
  75.5 0.6 constant_dynamic-slice_fusion.2
  76.1 3.1 %add_convert_fusion.1 = (bf16[8,24,3200]{2,1,0:T(8,128)(2,1)}, bf16[8,24,3200]{2,1,0:T(8,128)(2,1)}) fusion(bf16[2,1,4,24,3200]{4,3,2,1,0:T(8,128)(2,1)S(1)} %get-tuple-element.110, bf16[2,1,4,24,3200]{4,3,2,1,0:T(8,128)(2,1)S(1)} %get-tuple-element.123, bf16[8,2,1,24,3200]{4,3,1,0,2:T(8,128)(2,1)S(1)} %bitcast.70, s32[]{:T(128)S(6)} %select_n.125, ...), kind=kLoop, calls=%fused_computation.3 | loop fusion | flops 7372800 | bytes 12288009 | tf_op jit(solution)/shard_map/convert_element_type | solution.py:663
  79.2 2.9 %collective-permute-start.8 = (bf16[8,24,3200]{2,1,0:T(8,128)(2,1)}, bf16[8,24,3200]{2,1,0:T(8,128)(2,1)S(1)}, u32[]{:S(2)}, u32[]{:S(2)}) collective-permute-start(bf16[8,24,3200]{2,1,0:T(8,128)(2,1)} %get-tuple-element.101), channel_id=1, source_target_pairs={{0,1},{1,0},{2,3},{3,2},{4,5},{5,4},{6,7},{7,6},{8,9},{9,8},{10,11... | collective-permute-start | bytes 3686408 | tf_op jit(solution)/shard_map/ppermute | solution.py:675
  82.1 2.8 %add_convert_fusion.4 = (bf16[4,1,2,96,384]{4,3,2,1,0:T(8,128)(2,1)S(1)}, bf16[4,1,2,96,384]{4,3,2,1,0:T(8,128)(2,1)}) fusion(bf16[4,2,2,96,384]{4,3,2,1,0:T(8,128)(2,1)} %bitcast.3, s32[]{:T(128)S(6)} %select_n.141, bf16[4,2,2,96,384]{4,3,2,1,0:T(8,128)(2,1)} %bitcast.75, s32[]{:T(128)S(6)} %select_n.121), kind=kLoop, calls=%fused_computation.14 | loop fusion | flops 2359296 | bytes 3538952 | tf_op jit(solution)/shard_map/convert_element_type | solution.py:663
  84.9 26.7 %collective-permute-start.12 = (bf16[8,96,384]{2,1,0:T(8,128)(2,1)}, bf16[8,96,384]{2,1,0:T(8,128)(2,1)}, u32[]{:S(2)}, u32[]{:S(2)}) collective-permute-start(bf16[8,96,384]{2,1,0:T(8,128)(2,1)} %bitcast.4), channel_id=1, source_target_pairs={{0,2},{1,3},{2,0},{3,1},{4,6},{5,7},{6,4},{7,5},{8,10},{9,11},{10,... | collective-permute-start | bytes 1769480 | tf_op jit(solution)/shard_map/ppermute | solution.py:675
  111.6 1.1 copy-done.4
  112.6 2.5 %add_convert_fusion.3 = (bf16[4,1,1,24,3200]{4,3,1,0,2:T(8,128)(2,1)S(1)}, bf16[4,24,3200]{2,1,0:T(8,128)(2,1)}) fusion(bf16[4,2,1,24,3200]{4,3,1,0,2:T(8,128)(2,1)} %bitcast.74, s32[]{:T(128)S(6)} %select_n.134, bf16[4,2,1,24,3200]{4,3,1,0,2:T(8,128)(2,1)S(1)} %bitcast.71, s32[]{:T(128)S(6)} %select_n.137), kind=kLoop, calls=%fused_computation.13 | loop fusion | flops 2457600 | bytes 3686408 | tf_op jit(solution)/shard_map/convert_element_type | solution.py:663
  115.1 12.6 %collective-permute-start.9 = (bf16[4,24,3200]{2,1,0:T(8,128)(2,1)}, bf16[4,24,3200]{2,1,0:T(8,128)(2,1)}, u32[]{:S(2)}, u32[]{:S(2)}) collective-permute-start(bf16[4,24,3200]{2,1,0:T(8,128)(2,1)} %get-tuple-element.107), channel_id=1, source_target_pairs={{0,2},{1,3},{2,0},{3,1},{4,6},{5,7},{6,4},{7,5},{8,10},{9,11},{10,... | collective-permute-start | bytes 1843208 | tf_op jit(solution)/shard_map/ppermute | solution.py:675
  127.7 2.0 %select_bitcast_fusion = (bf16[2,1,6,197,384]{4,3,2,0,1:T(8,128)(2,1)S(1)}, bf16[2,1,6,197,384]{4,3,2,0,1:T(8,128)(2,1)S(1)}) fusion(bf16[2,6,197,384]{3,2,1,0:T(8,128)(2,1)S(1)} %copy-done.2, pred[]{:T(512)S(6)} %eq.3, bf16[2,6,197,384]{3,0,2,1:T(2,128)(2,1)} %collective-permute-done.5), kind=kLoop, calls=%fused_computation.6 | loop fusion | flops 1815552 | bytes 7262209 | tf_op jit(solution)/shard_map/stack | solution.py:743
  129.8 1.2 add_convert_fusion.9
  131.0 1.3 collective-permute-start.13
  132.3 3.9 %collective-permute-done.9 = bf16[4,24,3200]{2,1,0:T(8,128)(2,1)} collective-permute-done((bf16[4,24,3200]{2,1,0:T(8,128)(2,1)}, bf16[4,24,3200]{2,1,0:T(8,128)(2,1)}, u32[]{:S(2)}, u32[]{:S(2)}) %collective-permute-start.9) | collective-permute-done | bytes 614432 | tf_op jit(solution)/shard_map/ppermute | solution.py:675
  136.2 1.2 add_convert_fusion.7
  137.4 1.3 collective-permute-start.10
  139.3 2.6 %copy.42 = bf16[1,2,6,197,384]{4,1,3,2,0:T(2,128)(2,1)} copy(bf16[1,2,6,197,384]{4,3,2,0,1:T(8,128)(2,1)S(1)} %get-tuple-element.103) | data formatting | bytes 3631104
  141.9 2.6 %copy.43 = bf16[1,2,6,197,384]{4,1,3,2,0:T(2,128)(2,1)} copy(bf16[1,2,6,197,384]{4,3,2,0,1:T(8,128)(2,1)S(1)} %get-tuple-element.102) | data formatting | bytes 3631104
  144.6 4.5 %collective-permute-start.15 = (bf16[1,96,384]{2,1,0:T(8,128)(2,1)S(1)}, bf16[1,96,384]{2,1,0:T(8,128)(2,1)S(1)}, u32[]{:S(2)}, u32[]{:S(2)}) collective-permute-start(bf16[1,96,384]{2,1,0:T(8,128)(2,1)S(1)} %fusion.7), channel_id=1, source_target_pairs={{0,8},{1,9},{2,10},{3,11},{4,12},{5,13},{6,14},{7,15},{8,0},{9,1},... | collective-permute-start | bytes 221192 | tf_op jit(solution)/shard_map/ppermute | solution.py:675
  149.0 0.7 fusion.3
  149.8 6.3 %collective-permute-done.15 = bf16[1,96,384]{2,1,0:T(8,128)(2,1)S(1)} collective-permute-done((bf16[1,96,384]{2,1,0:T(8,128)(2,1)S(1)}, bf16[1,96,384]{2,1,0:T(8,128)(2,1)S(1)}, u32[]{:S(2)}, u32[]{:S(2)}) %collective-permute-start.15) | collective-permute-done | bytes 73760 | tf_op jit(solution)/shard_map/ppermute | solution.py:675
  156.1 0.7 convert_add_fusion.4
  156.8 1.9 %collective-permute-done.11 = bf16[1,24,3200]{2,1,0:T(8,128)(2,1)S(1)} collective-permute-done((bf16[1,24,3200]{2,1,0:T(8,128)(2,1)S(1)}, bf16[1,24,3200]{2,1,0:T(8,128)(2,1)S(1)}, u32[]{:S(2)}, u32[]{:S(2)}) %collective-permute-start.11) | collective-permute-done | bytes 153632 | tf_op jit(solution)/shard_map/ppermute | solution.py:675
  158.8 0.7 copy-done.5
  159.4 1.8 %shard_map.256 = (f32[1,24,1536]{2,1,0:T(8,128)}, f32[1,24,1152]{2,1,0:T(8,128)}, f32[1,24,384]{2,1,0:T(8,128)}, f32[1,48]{1,0:T(1,128)}, f32[1,96]{1,0:T(1,128)...) custom-call(bf16[24,3200]{1,0:T(8,128)(2,1)} %get-tuple-element.119., ...), custom_call_target="tpu_custom_call" | custom-call | tf_op jit(solution)/shard_map/pallas_call | solution.py:709
  (40 shorter events, 2.0 us)
Async XLA Ops:
  0.6 7.7 %collective-permute-start.3 = (bf16[1,384,1536]{2,1,0:T(8,128)(2,1)}, bf16[1,384,1536]{2,1,0:T(8,128)(2,1)S(1)}, u32[]{:S(2)}, u32[]{:S(2)}) collective-permute-start(bf16[1,384,1536]{2,1,0:T(8,128)(2,1)} %refs_8_.1), channel_id=1, source_target_pairs={{0,16},{16,0},{1,17},{17,1},{2,18},{18,2},{3,19},{19,3},{4,20},{20... | collective-permute-start | bytes 3538952 | tf_op jit(solution)/shard_map/ppermute | solution.py:629
  1.2 8.1 %collective-permute-start.4 = (bf16[1,1536,384]{2,1,0:T(8,128)(2,1)}, bf16[1,1536,384]{2,1,0:T(8,128)(2,1)}, u32[]{:S(2)}, u32[]{:S(2)}) collective-permute-start(bf16[1,1536,384]{2,1,0:T(8,128)(2,1)} %refs_9_.1), channel_id=1, source_target_pairs={{0,16},{16,0},{1,17},{17,1},{2,18},{18,2},{3,19},{19,3},{4,20},{20... | collective-permute-start | bytes 3538952 | tf_op jit(solution)/shard_map/ppermute | solution.py:629
  1.2 7.0 %collective-permute-start.1 = (bf16[1,384,1152]{2,1,0:T(8,128)(2,1)}, bf16[1,384,1152]{2,1,0:T(8,128)(2,1)S(1)}, u32[]{:S(2)}, u32[]{:S(2)}) collective-permute-start(bf16[1,384,1152]{2,1,0:T(8,128)(2,1)} %refs_6_.3), channel_id=1, source_target_pairs={{0,16},{16,0},{1,17},{17,1},{2,18},{18,2},{3,19},{19,3},{4,20},{20... | collective-permute-start | bytes 2654216 | tf_op jit(solution)/shard_map/ppermute | solution.py:629
  1.7 6.6 %collective-permute-start.2 = (bf16[1,384,384]{2,1,0:T(8,128)(2,1)}, bf16[1,384,384]{2,1,0:T(8,128)(2,1)S(1)}, u32[]{:S(2)}, u32[]{:S(2)}) collective-permute-start(bf16[1,384,384]{2,1,0:T(8,128)(2,1)} %refs_7_.3), channel_id=1, source_target_pairs={{0,16},{16,0},{1,17},{17,1},{2,18},{18,2},{3,19},{19,3},{4,20},{20... | collective-permute-start | bytes 884744 | tf_op jit(solution)/shard_map/ppermute | solution.py:629
  3.2 5.1 %collective-permute-start = (f32[1,4992]{1,0:T(1,128)}, f32[1,4992]{1,0:T(1,128)S(1)}, u32[]{:S(2)}, u32[]{:S(2)}) collective-permute-start(f32[1,4992]{1,0:T(1,128)} %shard_map.254.refs_4_), channel_id=1, source_target_pairs={{0,16},{16,0},{1,17},{17,1},{2,18},{18,2},{3,19},{19,3},{4,20},{20... | collective-permute-start | bytes 59912 | tf_op jit(solution)/shard_map/ppermute | solution.py:629
  3.6 3.2 %copy-start.3 = (bf16[2,6,197,384]{3,0,2,1:T(2,128)(2,1)S(1)}, bf16[2,6,197,384]{3,0,2,1:T(2,128)(2,1)}, u32[]{:S(2)}) copy-start(bf16[2,6,197,384]{3,0,2,1:T(2,128)(2,1)} %param.17) | copy-start | bytes 5446660
  8.3 1.0 copy-start.9
  8.3 1.0 copy-start.8
  8.3 1.0 copy-start.7
  9.3 1.0 copy-start.6
  70.4 5.0 %collective-permute-start.6 = (bf16[384,3200]{1,0:T(8,128)(2,1)}, bf16[384,3200]{1,0:T(8,128)(2,1)S(1)}, u32[]{:S(2)}, u32[]{:S(2)}) collective-permute-start(bf16[384,3200]{1,0:T(8,128)(2,1)} %get-tuple-element.40), channel_id=1, source_target_pairs={{0,16},{16,0},{1,17},{17,1},{2,18},{18,2},{3,19},{19,3},{4,20},{20... | collective-permute-start | bytes 7372808 | tf_op jit(solution)/shard_map/ppermute | solution.py:629
  70.5 5.0 %copy-start = (bf16[384,3200]{1,0:T(8,128)(2,1)S(1)}, bf16[384,3200]{1,0:T(8,128)(2,1)}, u32[]{:S(2)}) copy-start(bf16[384,3200]{1,0:T(8,128)(2,1)} %get-tuple-element.43) | copy-start | bytes 7372804
  74.8 52.9 %collective-permute-start.5 = (bf16[2,6,197,384]{3,0,2,1:T(2,128)(2,1)}, bf16[2,6,197,384]{3,0,2,1:T(2,128)(2,1)}, u32[]{:S(2)}, u32[]{:S(2)}) collective-permute-start(bf16[2,6,197,384]{3,0,2,1:T(2,128)(2,1)} %copy.39), channel_id=1, source_target_pairs={{0,16},{16,0},{1,17},{17,1},{2,18},{18,2},{3,19},{19,3},{4,20},{20... | collective-permute-start | bytes 5446664 | tf_op jit(solution)/shard_map/ppermute | solution.py:629
  75.4 6.7 %collective-permute-start.7 = (bf16[1536,384]{1,0:T(8,128)(2,1)}, bf16[1536,384]{1,0:T(8,128)(2,1)}, u32[]{:S(2)}, u32[]{:S(2)}) collective-permute-start(bf16[1536,384]{1,0:T(8,128)(2,1)} %get-tuple-element.41), channel_id=1, source_target_pairs={{0,16},{16,0},{1,17},{17,1},{2,18},{18,2},{3,19},{19,3},{4,20},{20... | collective-permute-start | bytes 3538952 | tf_op jit(solution)/shard_map/ppermute | solution.py:629
  79.2 32.4 %collective-permute-start.8 = (bf16[8,24,3200]{2,1,0:T(8,128)(2,1)}, bf16[8,24,3200]{2,1,0:T(8,128)(2,1)S(1)}, u32[]{:S(2)}, u32[]{:S(2)}) collective-permute-start(bf16[8,24,3200]{2,1,0:T(8,128)(2,1)} %get-tuple-element.101), channel_id=1, source_target_pairs={{0,1},{1,0},{2,3},{3,2},{4,5},{5,4},{6,7},{7,6},{8,9},{9,8},{10,11... | collective-permute-start | bytes 3686408 | tf_op jit(solution)/shard_map/ppermute | solution.py:675
  82.1 30.6 %copy-start.1 = (bf16[8,24,3200]{2,1,0:T(8,128)(2,1)S(1)}, bf16[8,24,3200]{2,1,0:T(8,128)(2,1)}, u32[]{:S(2)}) copy-start(bf16[8,24,3200]{2,1,0:T(8,128)(2,1)} %get-tuple-element.45) | copy-start | bytes 3686404
  84.9 44.9 %collective-permute-start.12 = (bf16[8,96,384]{2,1,0:T(8,128)(2,1)}, bf16[8,96,384]{2,1,0:T(8,128)(2,1)}, u32[]{:S(2)}, u32[]{:S(2)}) collective-permute-start(bf16[8,96,384]{2,1,0:T(8,128)(2,1)} %bitcast.4), channel_id=1, source_target_pairs={{0,2},{1,3},{2,0},{3,1},{4,6},{5,7},{6,4},{7,5},{8,10},{9,11},{10,... | collective-permute-start | bytes 1769480 | tf_op jit(solution)/shard_map/ppermute | solution.py:675
  111.6 1.1 copy-start.4
  112.6 15.1 %copy-start.2 = (bf16[2,6,197,384]{3,2,1,0:T(8,128)(2,1)S(1)}, bf16[2,6,197,384]{3,2,1,0:T(8,128)(2,1)}, u32[]{:S(2)}) copy-start(bf16[2,6,197,384]{3,2,1,0:T(8,128)(2,1)} %get-tuple-element.36) | copy-start | bytes 5446660
  115.1 21.0 %collective-permute-start.9 = (bf16[4,24,3200]{2,1,0:T(8,128)(2,1)}, bf16[4,24,3200]{2,1,0:T(8,128)(2,1)}, u32[]{:S(2)}, u32[]{:S(2)}) collective-permute-start(bf16[4,24,3200]{2,1,0:T(8,128)(2,1)} %get-tuple-element.107), channel_id=1, source_target_pairs={{0,2},{1,3},{2,0},{3,1},{4,6},{5,7},{6,4},{7,5},{8,10},{9,11},{10,... | collective-permute-start | bytes 1843208 | tf_op jit(solution)/shard_map/ppermute | solution.py:675
  131.0 7.7 %collective-permute-start.13 = (bf16[4,96,384]{2,1,0:T(8,128)(2,1)S(1)}, bf16[4,96,384]{2,1,0:T(8,128)(2,1)S(1)}, u32[]{:S(2)}, u32[]{:S(2)}) collective-permute-start(bf16[4,96,384]{2,1,0:T(8,128)(2,1)S(1)} %bitcast.77), channel_id=1, source_target_pairs={{0,4},{1,5},{2,6},{3,7},{4,0},{5,1},{6,2},{7,3},{8,12},{9,13},{10,... | collective-permute-start | bytes 884744 | tf_op jit(solution)/shard_map/ppermute | solution.py:675
  137.4 11.7 %collective-permute-start.10 = (bf16[2,24,3200]{2,1,0:T(8,128)(2,1)S(1)}, bf16[2,24,3200]{2,1,0:T(8,128)(2,1)S(1)}, u32[]{:S(2)}, u32[]{:S(2)}) collective-permute-start(bf16[2,24,3200]{2,1,0:T(8,128)(2,1)S(1)} %get-tuple-element.115), channel_id=1, source_target_pairs={{0,4},{1,5},{2,6},{3,7},{4,0},{5,1},{6,2},{7,3},{8,12},{9,13},{10,... | collective-permute-start | bytes 921608 | tf_op jit(solution)/shard_map/ppermute | solution.py:675
  138.8 5.8 %collective-permute-start.14 = (bf16[2,96,384]{2,1,0:T(8,128)(2,1)S(1)}, bf16[2,96,384]{2,1,0:T(8,128)(2,1)S(1)}, u32[]{:S(2)}, u32[]{:S(2)}) collective-permute-start(bf16[2,96,384]{2,1,0:T(8,128)(2,1)S(1)} %get-tuple-element.121), channel_id=1, source_target_pairs={{0,1},{1,0},{2,3},{3,2},{4,5},{5,4},{6,7},{7,6},{8,9},{9,8},{10,11... | collective-permute-start | bytes 442376 | tf_op jit(solution)/shard_map/ppermute | solution.py:675
  144.6 11.5 %collective-permute-start.15 = (bf16[1,96,384]{2,1,0:T(8,128)(2,1)S(1)}, bf16[1,96,384]{2,1,0:T(8,128)(2,1)S(1)}, u32[]{:S(2)}, u32[]{:S(2)}) collective-permute-start(bf16[1,96,384]{2,1,0:T(8,128)(2,1)S(1)} %fusion.7), channel_id=1, source_target_pairs={{0,8},{1,9},{2,10},{3,11},{4,12},{5,13},{6,14},{7,15},{8,0},{9,1},... | collective-permute-start | bytes 221192 | tf_op jit(solution)/shard_map/ppermute | solution.py:675
  149.8 9.0 %collective-permute-start.11 = (bf16[1,24,3200]{2,1,0:T(8,128)(2,1)S(1)}, bf16[1,24,3200]{2,1,0:T(8,128)(2,1)S(1)}, u32[]{:S(2)}, u32[]{:S(2)}) collective-permute-start(bf16[1,24,3200]{2,1,0:T(8,128)(2,1)S(1)} %get-tuple-element.118), channel_id=1, source_target_pairs={{0,8},{1,9},{2,10},{3,11},{4,12},{5,13},{6,14},{7,15},{8,0},{9,1},... | collective-permute-start | bytes 460808 | tf_op jit(solution)/shard_map/ppermute | solution.py:675
  158.7 0.7 copy-start.5

commit v5 on v4

--- a/solution.py
+++ b/solution.py
@@ -475,7 +475,7 @@
 
         send(0, mine_wide, away_wide)
         for columns in spans(units, features):
-            tall[layer, columns, :] = sum_down[layer, :, columns].T.astype(BF16)
+            tall[layer, columns, :] = sum_down[layer, :, columns].astype(BF16).T
         send(1, mine_tall, away_tall)
 
     @pl.when(jnp.logical_not(running))
@@ -629,7 +629,7 @@
     return lax.ppermute(block, "segment", [(0, 1), (1, 0)])
 
 
-def reduce_shards(mine, got, orders, first):
+def reduce_shards(mine, got, orders, first, after=None):
     dp = lax.axis_size("dp")
     me = lax.axis_index("dp")
     bits = dp.bit_length() - 1
@@ -643,7 +643,7 @@
         for order, left in zip(orders, held):
             left.remove(order[n])
 
-        def slices(at, index):
+        def slices(terms, at, index):
             taken = []
             for term in terms:
                 view = term.reshape((-1, 2, 1 << at) + rest)
@@ -651,22 +651,23 @@
                 taken.append(part.reshape((-1,) + rest))
             return taken
 
-        def half(other):
+        def half(terms, other):
             if below[0] == below[1]:
                 index = jnp.where(first, bit[0], bit[1])
-                taken = slices(below[0], 1 - index if other else index)
+                taken = slices(terms, below[0], 1 - index if other else index)
             else:
                 index = [1 - b if other else b for b in bit]
-                sides = zip(slices(below[0], index[0]), slices(below[1], index[1]))
+                sides = zip(slices(terms, below[0], index[0]), slices(terms, below[1], index[1]))
                 taken = [jnp.where(first, a, b) for a, b in sides]
             total = sum(part.astype(F32) for part in taken)
             return total.astype(BF16)
 
-        send = half(True)
-        first_send = send if n == 0 else first_send
-        keep = half(False)
+        send = half(terms, True)
         if n == 0:
-            keep, _ = lax.optimization_barrier((keep, send))
+            first_send = send
+            if after is not None:
+                terms = lax.optimization_barrier(terms + (after,))[:2]
+        keep = half(terms, False)
         route = [
             (core * dp + i, core * dp + (i ^ (1 << order[n])))
             for core, order in enumerate(orders)
@@ -730,15 +731,11 @@
     away_tall, got_wide = lax.optimization_barrier((away_tall, got_wide))
     got_tall = swap_cores(away_tall)
     got = swap_cores(away)
-    bits = dp.bit_length() - 1
-    near = list(range(min(bits, 3)))
-    far = list(range(len(near), bits))
-
-    def turned(by):
-        return near[by % len(near) :] + near[: by % len(near)] + far
-
-    wide, _ = reduce_shards(mine_wide, got_wide, (turned(0), turned(2)), first)
-    tall, tall_sent = reduce_shards(mine_tall, got_tall, (turned(1), turned(1)), first)
+    bits = list(range(dp.bit_length() - 1))
+    near, far = bits[:3], bits[3:]
+    plain, turned, crossed = near + far, near[2:] + near[:2] + far, near[1:] + far + near[:1]
+    tall, tall_sent = reduce_shards(mine_tall, got_tall, (crossed, crossed), first)
+    wide, _ = reduce_shards(mine_wide, got_wide, (plain, turned), first, after=tall_sent)
     got, _ = lax.optimization_barrier((got, tall_sent))
     both = jnp.stack([jnp.where(first, mine, got), jnp.where(first, got, mine)], axis=1)
     g_up, g_qkv, g_out, g_bqv, g_bup, *vectors = split_wide(wide, features, units)

time: 162 us -> 156 us (0.963)
  other arithmetic: 14.8 us -> 10.1 us
    convert_element_type x8 -> x9, other arithmetic: 11.7 us -> 7 us  [half(): return total.astype(BF16)]
  transfers between devices with their start and end apart: 16 -> 16, of which waited for: 4 -> 5; matrix products, arithmetic and copies ran while one was open for 18% -> 16% of each run, Pallas kernels for 1% -> 1%
where the time goes in v5:
time: 156 us
  Pallas kernels  63.2 us (41%)
  starting transfers between devices  52.1 us (33%)
  local copies, waits for them, and re-layouts  17.6 us (11%)
  waiting for transfers between devices  11.6 us (7%)
  other arithmetic  10.1 us (6%)
    pallas_call x1, Pallas kernels, run_layers(): pl.pallas_call(lambda *refs: layers_kernel(padded, keys, *refs), grid_spe...  60 us
    ppermute x8, starting transfers between devices, reduce_shards(): arrived = lax.ppermute(send, ('segment', 'dp'), route)  49.9 us
    unnamed x24, local copies, waits for them, and re-layouts  12.6 us
    ppermute x8, waiting for transfers between devices, reduce_shards(): arrived = lax.ppermute(send, ('segment', 'dp'), route)  10.7 us
    convert_element_type x9, other arithmetic, half(): return total.astype(BF16)  7 us
    pallas_call x1, local copies, waits for them, and re-layouts, run_layers(): pl.pallas_call(lambda *refs: layers_kernel(padded, keys, *refs), grid_spe...  4.28 us
  transfers between devices with their start and end apart: 16, of which 5 were waited for; matrix products, arithmetic and copies ran while one was open for 16% of the time, Pallas kernels for 1%

profile of v5, /device:TPU:0, one launch (start us, length us, event | category | flops | bytes accessed | tf_op | source)
XLA Modules:
  0.0 155.6 jit_solution(16757615714810257439)
XLA Ops:
  1.8 1.4 shard_map.254.refs_4_
  3.6 3.2 %copy.41.refs_2_ = bf16[2,6,197,384]{3,2,1,0:T(8,128)(2,1)} copy(bf16[2,6,197,384]{3,0,2,1:T(2,128)(2,1)} %param.15) | data formatting | bytes 3631104 | tf_op args[0]
  6.8 1.5 copy.42.refs_3_
  8.3 1.0 copy-done.7
  9.3 1.0 copy-done.6
  10.3 60.0 %shard_map.255 = (bf16[2,6,197,384]{3,2,1,0:T(8,128)(2,1)}, bf16[2,6,197,384]{3,2,1,0:T(8,128)(2,1)}, bf16[384,3200]{1,0:T(8,128)(2,1)}, bf16[384,3200]{1,0:T(8,...) custom-call(s32[2]{0:T(128)} %bitcast.97, s32[1]{0:T(128)} %bitcast.1.refs_1_, ...), custom_call_target="tpu_custom_call" | custom-call | flops 80000000000 | bytes 30000000 | tf_op jit(solution)/shard_map/pallas_call | solution.py:586
  70.5 4.3 %copy.43 = bf16[2,6,197,384]{3,0,2,1:T(2,128)(2,1)} copy(bf16[2,6,197,384]{3,2,1,0:T(8,128)(2,1)} %get-tuple-element.37) | data formatting | bytes 3631104 | tf_op jit(solution)/shard_map/pallas_call | solution.py:586
  75.7 0.8 add_convert_fusion
  76.5 3.0 %collective-permute-start.8 = (bf16[8,24,3200]{2,1,0:T(8,128)(2,1)S(1)}, bf16[8,24,3200]{2,1,0:T(8,128)(2,1)S(1)}, u32[]{:S(2)}, u32[]{:S(2)}) collective-permute-start(bf16[8,24,3200]{2,1,0:T(8,128)(2,1)S(1)} %add_convert_fusion), channel_id=1, source_target_pairs={{0,1},{1,0},{2,3},{3,2},{4,5},{5,4},{6,7},{7,6},{8,9},{9,8},{10,11... | collective-permute-start | bytes 3686408 | tf_op jit(solution)/shard_map/ppermute | solution.py:676
  79.5 0.8 collective-permute-done.7
  80.3 1.2 add_convert_fusion.4
  81.5 28.0 %collective-permute-start.12 = (bf16[8,96,384]{2,1,0:T(8,128)(2,1)}, bf16[8,96,384]{2,1,0:T(8,128)(2,1)}, u32[]{:S(2)}, u32[]{:S(2)}) collective-permute-start(bf16[8,96,384]{2,1,0:T(8,128)(2,1)} %bitcast.4), channel_id=1, source_target_pairs={{0,2},{1,3},{2,0},{3,1},{4,6},{5,7},{6,4},{7,5},{8,10},{9,11},{10,... | collective-permute-start | bytes 1769480 | tf_op jit(solution)/shard_map/ppermute | solution.py:676
  110.0 0.6 add_convert_fusion.1
  110.7 1.2 add_convert_fusion.3
  111.8 10.7 %collective-permute-start.9 = (bf16[4,24,3200]{2,1,0:T(8,128)(2,1)}, bf16[4,24,3200]{2,1,0:T(8,128)(2,1)}, u32[]{:S(2)}, u32[]{:S(2)}) collective-permute-start(bf16[4,24,3200]{2,1,0:T(8,128)(2,1)} %get-tuple-element.105), channel_id=1, source_target_pairs={{0,2},{1,3},{2,0},{3,1},{4,6},{5,7},{6,4},{7,5},{8,10},{9,11},{10,... | collective-permute-start | bytes 1843208 | tf_op jit(solution)/shard_map/ppermute | solution.py:676
  122.5 2.0 %select_bitcast_fusion = (bf16[2,1,6,197,384]{4,3,2,0,1:T(8,128)(2,1)S(1)}, bf16[2,1,6,197,384]{4,3,2,0,1:T(8,128)(2,1)S(1)}) fusion(bf16[2,6,197,384]{3,2,1,0:T(8,128)(2,1)S(1)} %copy-done.1, pred[]{:T(512)S(6)} %eq.3, bf16[2,6,197,384]{3,0,2,1:T(2,128)(2,1)} %collective-permute-done.5), kind=kLoop, calls=%fused_computation.6 | loop fusion | flops 1815552 | bytes 7262209 | tf_op jit(solution)/shard_map/stack | solution.py:740
  124.5 1.2 add_convert_fusion.9
  125.7 0.7 collective-permute-start.13
  126.5 4.5 %collective-permute-done.9 = bf16[4,24,3200]{2,1,0:T(8,128)(2,1)} collective-permute-done((bf16[4,24,3200]{2,1,0:T(8,128)(2,1)}, bf16[4,24,3200]{2,1,0:T(8,128)(2,1)}, u32[]{:S(2)}, u32[]{:S(2)}) %collective-permute-start.9) | collective-permute-done | bytes 614432 | tf_op jit(solution)/shard_map/ppermute | solution.py:676
  130.9 1.2 add_convert_fusion.7
  132.1 2.1 %collective-permute-start.10 = (bf16[2,24,3200]{2,1,0:T(8,128)(2,1)S(1)}, bf16[2,24,3200]{2,1,0:T(8,128)(2,1)S(1)}, u32[]{:S(2)}, u32[]{:S(2)}) collective-permute-start(bf16[2,24,3200]{2,1,0:T(8,128)(2,1)S(1)} %get-tuple-element.109), channel_id=1, source_target_pairs={{0,4},{1,5},{2,6},{3,7},{4,0},{5,1},{6,2},{7,3},{8,12},{9,13},{10,... | collective-permute-start | bytes 921608 | tf_op jit(solution)/shard_map/ppermute | solution.py:676
  134.3 2.7 %collective-permute-start.14 = (bf16[2,96,384]{2,1,0:T(8,128)(2,1)S(1)}, bf16[2,96,384]{2,1,0:T(8,128)(2,1)S(1)}, u32[]{:S(2)}, u32[]{:S(2)}) collective-permute-start(bf16[2,96,384]{2,1,0:T(8,128)(2,1)S(1)} %get-tuple-element.115), channel_id=1, source_target_pairs={{0,8},{1,9},{2,10},{3,11},{4,12},{5,13},{6,14},{7,15},{8,0},{9,1},... | collective-permute-start | bytes 442376 | tf_op jit(solution)/shard_map/ppermute | solution.py:676
  137.4 2.6 %copy.50 = bf16[1,2,6,197,384]{4,1,3,2,0:T(2,128)(2,1)} copy(bf16[1,2,6,197,384]{4,3,2,0,1:T(8,128)(2,1)S(1)} %get-tuple-element.101) | data formatting | bytes 3631104
  140.1 2.6 %copy.51 = bf16[1,2,6,197,384]{4,1,3,2,0:T(2,128)(2,1)} copy(bf16[1,2,6,197,384]{4,3,2,0,1:T(8,128)(2,1)S(1)} %get-tuple-element.100) | data formatting | bytes 3631104
  142.7 1.1 collective-permute-start.15
  143.8 0.7 fusion.3
  144.5 1.6 %collective-permute-start.11 = (bf16[1,24,3200]{2,1,0:T(8,128)(2,1)S(1)}, bf16[1,24,3200]{2,1,0:T(8,128)(2,1)S(1)}, u32[]{:S(2)}, u32[]{:S(2)}) collective-permute-start(bf16[1,24,3200]{2,1,0:T(8,128)(2,1)S(1)} %get-tuple-element.112), channel_id=1, source_target_pairs={{0,8},{1,9},{2,10},{3,11},{4,12},{5,13},{6,14},{7,15},{8,0},{9,1},... | collective-permute-start | bytes 460808 | tf_op jit(solution)/shard_map/ppermute | solution.py:676
  146.1 1.0 collective-permute-done.15
  147.1 0.7 convert_add_fusion.4
  147.8 5.2 %collective-permute-done.11 = bf16[1,24,3200]{2,1,0:T(8,128)(2,1)S(1)} collective-permute-done((bf16[1,24,3200]{2,1,0:T(8,128)(2,1)S(1)}, bf16[1,24,3200]{2,1,0:T(8,128)(2,1)S(1)}, u32[]{:S(2)}, u32[]{:S(2)}) %collective-permute-start.11) | collective-permute-done | bytes 153632 | tf_op jit(solution)/shard_map/ppermute | solution.py:676
  153.0 0.7 copy-done.4
  153.7 1.8 %shard_map.256 = (f32[1,24,1536]{2,1,0:T(8,128)}, f32[1,24,1152]{2,1,0:T(8,128)}, f32[1,24,384]{2,1,0:T(8,128)}, f32[1,48]{1,0:T(1,128)}, f32[1,96]{1,0:T(1,128)...) custom-call(bf16[24,3200]{1,0:T(8,128)(2,1)} %get-tuple-element.113., ...), custom_call_target="tpu_custom_call" | custom-call | tf_op jit(solution)/shard_map/pallas_call | solution.py:710
  (43 shorter events, 3.7 us)
Async XLA Ops:
  0.6 7.7 %collective-permute-start.3 = (bf16[1,384,1536]{2,1,0:T(8,128)(2,1)}, bf16[1,384,1536]{2,1,0:T(8,128)(2,1)S(1)}, u32[]{:S(2)}, u32[]{:S(2)}) collective-permute-start(bf16[1,384,1536]{2,1,0:T(8,128)(2,1)} %refs_8_.1), channel_id=1, source_target_pairs={{0,16},{16,0},{1,17},{17,1},{2,18},{18,2},{3,19},{19,3},{4,20},{20... | collective-permute-start | bytes 3538952 | tf_op jit(solution)/shard_map/ppermute | solution.py:629
  1.2 8.1 %collective-permute-start.4 = (bf16[1,1536,384]{2,1,0:T(8,128)(2,1)}, bf16[1,1536,384]{2,1,0:T(8,128)(2,1)}, u32[]{:S(2)}, u32[]{:S(2)}) collective-permute-start(bf16[1,1536,384]{2,1,0:T(8,128)(2,1)} %refs_9_.1), channel_id=1, source_target_pairs={{0,16},{16,0},{1,17},{17,1},{2,18},{18,2},{3,19},{19,3},{4,20},{20... | collective-permute-start | bytes 3538952 | tf_op jit(solution)/shard_map/ppermute | solution.py:629
  1.2 7.0 %collective-permute-start.1 = (bf16[1,384,1152]{2,1,0:T(8,128)(2,1)}, bf16[1,384,1152]{2,1,0:T(8,128)(2,1)S(1)}, u32[]{:S(2)}, u32[]{:S(2)}) collective-permute-start(bf16[1,384,1152]{2,1,0:T(8,128)(2,1)} %refs_6_.3), channel_id=1, source_target_pairs={{0,16},{16,0},{1,17},{17,1},{2,18},{18,2},{3,19},{19,3},{4,20},{20... | collective-permute-start | bytes 2654216 | tf_op jit(solution)/shard_map/ppermute | solution.py:629
  1.7 6.6 %collective-permute-start.2 = (bf16[1,384,384]{2,1,0:T(8,128)(2,1)}, bf16[1,384,384]{2,1,0:T(8,128)(2,1)S(1)}, u32[]{:S(2)}, u32[]{:S(2)}) collective-permute-start(bf16[1,384,384]{2,1,0:T(8,128)(2,1)} %refs_7_.3), channel_id=1, source_target_pairs={{0,16},{16,0},{1,17},{17,1},{2,18},{18,2},{3,19},{19,3},{4,20},{20... | collective-permute-start | bytes 884744 | tf_op jit(solution)/shard_map/ppermute | solution.py:629
  3.2 5.1 %collective-permute-start = (f32[1,4992]{1,0:T(1,128)}, f32[1,4992]{1,0:T(1,128)S(1)}, u32[]{:S(2)}, u32[]{:S(2)}) collective-permute-start(f32[1,4992]{1,0:T(1,128)} %shard_map.254.refs_4_), channel_id=1, source_target_pairs={{0,16},{16,0},{1,17},{17,1},{2,18},{18,2},{3,19},{19,3},{4,20},{20... | collective-permute-start | bytes 59912 | tf_op jit(solution)/shard_map/ppermute | solution.py:629
  3.6 3.2 %copy-start.2 = (bf16[2,6,197,384]{3,0,2,1:T(2,128)(2,1)S(1)}, bf16[2,6,197,384]{3,0,2,1:T(2,128)(2,1)}, u32[]{:S(2)}) copy-start(bf16[2,6,197,384]{3,0,2,1:T(2,128)(2,1)} %param.17) | copy-start | bytes 5446660
  8.3 1.0 copy-start.9
  8.3 1.0 copy-start.8
  8.3 1.0 copy-start.7
  9.3 1.0 copy-start.6
  70.3 5.0 %collective-permute-start.6 = (bf16[384,3200]{1,0:T(8,128)(2,1)}, bf16[384,3200]{1,0:T(8,128)(2,1)S(1)}, u32[]{:S(2)}, u32[]{:S(2)}) collective-permute-start(bf16[384,3200]{1,0:T(8,128)(2,1)} %get-tuple-element.40), channel_id=1, source_target_pairs={{0,16},{16,0},{1,17},{17,1},{2,18},{18,2},{3,19},{19,3},{4,20},{20... | collective-permute-start | bytes 7372808 | tf_op jit(solution)/shard_map/ppermute | solution.py:629
  70.4 4.9 %copy-start.5 = (bf16[1536,384]{1,0:T(8,128)(2,1)S(1)}, bf16[1536,384]{1,0:T(8,128)(2,1)}, u32[]{:S(2)}) copy-start(bf16[1536,384]{1,0:T(8,128)(2,1)} %get-tuple-element.41) | copy-start | bytes 3538948
  70.5 5.0 %copy-start = (bf16[384,3200]{1,0:T(8,128)(2,1)S(1)}, bf16[384,3200]{1,0:T(8,128)(2,1)}, u32[]{:S(2)}) copy-start(bf16[384,3200]{1,0:T(8,128)(2,1)} %get-tuple-element.45) | copy-start | bytes 7372804
  74.7 47.8 %collective-permute-start.5 = (bf16[2,6,197,384]{3,0,2,1:T(2,128)(2,1)}, bf16[2,6,197,384]{3,0,2,1:T(2,128)(2,1)}, u32[]{:S(2)}, u32[]{:S(2)}) collective-permute-start(bf16[2,6,197,384]{3,0,2,1:T(2,128)(2,1)} %copy.43), channel_id=1, source_target_pairs={{0,16},{16,0},{1,17},{17,1},{2,18},{18,2},{3,19},{19,3},{4,20},{20... | collective-permute-start | bytes 5446664 | tf_op jit(solution)/shard_map/ppermute | solution.py:629
  75.3 5.0 %collective-permute-start.7 = (bf16[1536,384]{1,0:T(8,128)(2,1)S(1)}, bf16[1536,384]{1,0:T(8,128)(2,1)S(1)}, u32[]{:S(2)}, u32[]{:S(2)}) collective-permute-start(bf16[1536,384]{1,0:T(8,128)(2,1)S(1)} %copy-done.5), channel_id=1, source_target_pairs={{0,16},{16,0},{1,17},{17,1},{2,18},{18,2},{3,19},{19,3},{4,20},{20... | collective-permute-start | bytes 3538952 | tf_op jit(solution)/shard_map/ppermute | solution.py:629
  75.7 4.6 %copy-start.3 = (bf16[1536,384]{1,0:T(8,128)(2,1)S(1)}, bf16[1536,384]{1,0:T(8,128)(2,1)}, u32[]{:S(2)}) copy-start(bf16[1536,384]{1,0:T(8,128)(2,1)} %get-tuple-element.38) | copy-start | bytes 3538948
  76.5 34.1 %collective-permute-start.8 = (bf16[8,24,3200]{2,1,0:T(8,128)(2,1)S(1)}, bf16[8,24,3200]{2,1,0:T(8,128)(2,1)S(1)}, u32[]{:S(2)}, u32[]{:S(2)}) collective-permute-start(bf16[8,24,3200]{2,1,0:T(8,128)(2,1)S(1)} %add_convert_fusion), channel_id=1, source_target_pairs={{0,1},{1,0},{2,3},{3,2},{4,5},{5,4},{6,7},{7,6},{8,9},{9,8},{10,11... | collective-permute-start | bytes 3686408 | tf_op jit(solution)/shard_map/ppermute | solution.py:676
  81.5 43.1 %collective-permute-start.12 = (bf16[8,96,384]{2,1,0:T(8,128)(2,1)}, bf16[8,96,384]{2,1,0:T(8,128)(2,1)}, u32[]{:S(2)}, u32[]{:S(2)}) collective-permute-start(bf16[8,96,384]{2,1,0:T(8,128)(2,1)} %bitcast.4), channel_id=1, source_target_pairs={{0,2},{1,3},{2,0},{3,1},{4,6},{5,7},{6,4},{7,5},{8,10},{9,11},{10,... | collective-permute-start | bytes 1769480 | tf_op jit(solution)/shard_map/ppermute | solution.py:676
  110.6 11.8 %copy-start.1 = (bf16[2,6,197,384]{3,2,1,0:T(8,128)(2,1)S(1)}, bf16[2,6,197,384]{3,2,1,0:T(8,128)(2,1)}, u32[]{:S(2)}) copy-start(bf16[2,6,197,384]{3,2,1,0:T(8,128)(2,1)} %get-tuple-element.36) | copy-start | bytes 5446660
  111.8 19.1 %collective-permute-start.9 = (bf16[4,24,3200]{2,1,0:T(8,128)(2,1)}, bf16[4,24,3200]{2,1,0:T(8,128)(2,1)}, u32[]{:S(2)}, u32[]{:S(2)}) collective-permute-start(bf16[4,24,3200]{2,1,0:T(8,128)(2,1)} %get-tuple-element.105), channel_id=1, source_target_pairs={{0,2},{1,3},{2,0},{3,1},{4,6},{5,7},{6,4},{7,5},{8,10},{9,11},{10,... | collective-permute-start | bytes 1843208 | tf_op jit(solution)/shard_map/ppermute | solution.py:676
  125.7 8.5 %collective-permute-start.13 = (bf16[4,96,384]{2,1,0:T(8,128)(2,1)S(1)}, bf16[4,96,384]{2,1,0:T(8,128)(2,1)S(1)}, u32[]{:S(2)}, u32[]{:S(2)}) collective-permute-start(bf16[4,96,384]{2,1,0:T(8,128)(2,1)S(1)} %bitcast.94), channel_id=1, source_target_pairs={{0,4},{1,5},{2,6},{3,7},{4,0},{5,1},{6,2},{7,3},{8,12},{9,13},{10,... | collective-permute-start | bytes 884744 | tf_op jit(solution)/shard_map/ppermute | solution.py:676
  132.1 11.6 %collective-permute-start.10 = (bf16[2,24,3200]{2,1,0:T(8,128)(2,1)S(1)}, bf16[2,24,3200]{2,1,0:T(8,128)(2,1)S(1)}, u32[]{:S(2)}, u32[]{:S(2)}) collective-permute-start(bf16[2,24,3200]{2,1,0:T(8,128)(2,1)S(1)} %get-tuple-element.109), channel_id=1, source_target_pairs={{0,4},{1,5},{2,6},{3,7},{4,0},{5,1},{6,2},{7,3},{8,12},{9,13},{10,... | collective-permute-start | bytes 921608 | tf_op jit(solution)/shard_map/ppermute | solution.py:676
  134.3 8.3 %collective-permute-start.14 = (bf16[2,96,384]{2,1,0:T(8,128)(2,1)S(1)}, bf16[2,96,384]{2,1,0:T(8,128)(2,1)S(1)}, u32[]{:S(2)}, u32[]{:S(2)}) collective-permute-start(bf16[2,96,384]{2,1,0:T(8,128)(2,1)S(1)} %get-tuple-element.115), channel_id=1, source_target_pairs={{0,8},{1,9},{2,10},{3,11},{4,12},{5,13},{6,14},{7,15},{8,0},{9,1},... | collective-permute-start | bytes 442376 | tf_op jit(solution)/shard_map/ppermute | solution.py:676
  142.7 4.4 %collective-permute-start.15 = (bf16[1,96,384]{2,1,0:T(8,128)(2,1)S(1)}, bf16[1,96,384]{2,1,0:T(8,128)(2,1)S(1)}, u32[]{:S(2)}, u32[]{:S(2)}) collective-permute-start(bf16[1,96,384]{2,1,0:T(8,128)(2,1)S(1)} %fusion.7), channel_id=1, source_target_pairs={{0,1},{1,0},{2,3},{3,2},{4,5},{5,4},{6,7},{7,6},{8,9},{9,8},{10,11... | collective-permute-start | bytes 221192 | tf_op jit(solution)/shard_map/ppermute | solution.py:676
  144.5 8.5 %collective-permute-start.11 = (bf16[1,24,3200]{2,1,0:T(8,128)(2,1)S(1)}, bf16[1,24,3200]{2,1,0:T(8,128)(2,1)S(1)}, u32[]{:S(2)}, u32[]{:S(2)}) collective-permute-start(bf16[1,24,3200]{2,1,0:T(8,128)(2,1)S(1)} %get-tuple-element.112), channel_id=1, source_target_pairs={{0,8},{1,9},{2,10},{3,11},{4,12},{5,13},{6,14},{7,15},{8,0},{9,1},... | collective-permute-start | bytes 460808 | tf_op jit(solution)/shard_map/ppermute | solution.py:676
  153.0 0.7 copy-start.4

commit v6 on v5

--- a/solution.py
+++ b/solution.py
@@ -1,6 +1,7 @@
 import jax
 import jax.numpy as jnp
 from jax import lax
+from jax.experimental.layout import Layout, with_layout_constraint
 from jax.experimental import pallas as pl
 from jax.experimental.pallas import tpu as pltpu
 from jax.sharding import PartitionSpec as P
@@ -157,19 +158,20 @@
     def load(source, n, layer):
         return pltpu.make_async_copy(source[n].at[0], held[n].at[layer], load_sem.at[layer, n])
 
+    def fetch(layer):
+        for n in range(4):
+
+            @pl.when(core == layer)
+            def _():
+                load(own, n, layer).start()
+
+            @pl.when(core != layer)
+            def _():
+                load(got, n, layer).start()
+
     @pl.when(step == 0)
     def _():
-        for layer in range(2):
-            for n in range(4):
-
-                @pl.when(core == layer)
-                def _():
-                    load(own, n, layer).start()
-
-                @pl.when(core != layer)
-                def _():
-                    load(got, n, layer).start()
-
+        fetch(0)
         for layer in range(2):
             mine = jnp.full(own_vec.shape, core == layer)
             vecs[layer : layer + 1] = jnp.where(mine, own_vec[...], got_vec[...])
@@ -218,6 +220,10 @@
         def _():
             for n in range(4):
                 load(own, n, layer).wait()
+
+            @pl.when(layer == 0)
+            def _():
+                fetch(1)
 
         for at, size in row_chunks(rows):
             hat, _ = normalized(hidden[layer, at : at + size])
@@ -315,7 +321,7 @@
             leave(layer, 0, j, result[:tokens])
             hidden[layer + 1, image[j]] = result.astype(F32)
 
-    def backward(layer):
+    def backward_mlp(layer):
         for at, size in row_chunks(rows):
             value = grad_out[at : at + size]
             grad_low[at : at + size] = value.astype(BF16)
@@ -365,6 +371,7 @@
             sum_up[layer, :, chunks[c]] += dot_tn(second[layer], grad_before[:, chunks[c]])
             if c < GROUP:
                 norm_two(c)
+    def backward_attention(layer):
         for j in range(GROUP):
             value = dot_nt(out_low[image[j]], w_out[layer]).astype(BF16)
             for n in range(heads // 2):
@@ -434,12 +441,37 @@
         for j in range(GROUP):
             leave(layer, 1, j, grad_out[j * padded : j * padded + tokens].astype(BF16))
 
-    def store(layer, kind, target):
-        stage = (wide, tall)[kind].at[layer]
-        return pltpu.make_async_copy(stage, target, store_sem.at[layer, kind])
-
-    def finish(layer):
+    left_columns, right_columns = pl.ds(0, units), pl.ds(units, 4 * features + 128)
+    parts = (
+        (wide, mine_wide, away_wide, left_columns),
+        (tall, mine_tall, away_tall, pl.ds(0, features)),
+        (wide, mine_wide, away_wide, right_columns),
+    )
+
+    def store(layer, kind, away=False):
+        stage, mine, other, columns = parts[kind]
+        target = (other if away else mine).at[:, columns]
+        return pltpu.make_async_copy(
+            stage.at[layer, :, columns], target, store_sem.at[layer, kind]
+        )
+
+    def send(layer, kind):
+        @pl.when(core == layer)
+        def _():
+            store(layer, kind).start()
+
+        @pl.when(core != layer)
+        def _():
+            store(layer, kind, away=True).start()
+
+    def finish_mlp(layer):
         wide[layer, :, :units] = sum_up[layer].astype(BF16)
+        send(layer, 0)
+        for columns in spans(units, features):
+            tall[layer, columns, :] = sum_down[layer, :, columns].astype(BF16).T
+        send(layer, 1)
+
+    def finish_attention(layer):
         wide[layer, :, units : units + 4 * features] = sum_att[layer].astype(BF16)
         line = lax.broadcasted_iota(jnp.int32, (128, features), 0)
         plain = jnp.zeros((128, features), F32)
@@ -464,19 +496,7 @@
             columns = columns + dot_nt(pick, total.astype(BF16))
         wide[layer, :, units + 4 * features :] = columns.astype(BF16)
 
-        def send(kind, mine, away):
-            @pl.when(core == layer)
-            def _():
-                store(layer, kind, mine).start()
-
-            @pl.when(core != layer)
-            def _():
-                store(layer, kind, away).start()
-
-        send(0, mine_wide, away_wide)
-        for columns in spans(units, features):
-            tall[layer, columns, :] = sum_down[layer, :, columns].astype(BF16).T
-        send(1, mine_tall, away_tall)
+        send(layer, 2)
 
     @pl.when(jnp.logical_not(running))
     def _():
@@ -499,13 +519,18 @@
     def second_half(at, carry):
         layer = 1 - at
 
-        @pl.when(running)
-        def _():
-            backward(layer)
-
-        @pl.when(step == last)
-        def _():
-            finish(layer)
+        for compute, finish in (
+            (backward_mlp, finish_mlp),
+            (backward_attention, finish_attention),
+        ):
+
+            @pl.when(running)
+            def _():
+                compute(layer)
+
+            @pl.when(step == last)
+            def _():
+                finish(layer)
 
         return carry
 
@@ -514,8 +539,8 @@
     @pl.when(step == last)
     def _():
         for layer in range(2):
-            for kind, mine in enumerate((mine_wide, mine_tall)):
-                store(layer, kind, mine).wait()
+            for kind in range(3):
+                store(layer, kind).wait()
 
 
 def run_layers(counts, which, inputs, cotangent, vectors, weights):
@@ -581,7 +606,7 @@
             pltpu.VMEM((2, 2 * padded, keys), BF16),
         ]
         + two(sums)
-        + [pltpu.SemaphoreType.DMA((2, 4)), pltpu.SemaphoreType.DMA((2, 2))]
+        + [pltpu.SemaphoreType.DMA((2, 4)), pltpu.SemaphoreType.DMA((2, 3))]
     )
     return pl.pallas_call(
         lambda *refs: layers_kernel(padded, keys, *refs),
@@ -629,7 +654,7 @@
     return lax.ppermute(block, "segment", [(0, 1), (1, 0)])
 
 
-def reduce_shards(mine, got, orders, first, after=None):
+def reduce_shards(mine, got, orders, first, after=None, beside=()):
     dp = lax.axis_size("dp")
     me = lax.axis_index("dp")
     bits = dp.bit_length() - 1
@@ -674,8 +699,10 @@
             for i in range(dp)
         ]
         arrived = lax.ppermute(send, ("segment", "dp"), route)
+        if n == 0 and beside:
+            arrived, *beside = lax.optimization_barrier((arrived, *beside))
         terms = (keep, arrived)
-    return tuple(t.reshape(rest) for t in terms), first_send
+    return tuple(t.reshape(rest) for t in terms), first_send, beside
 
 
 def split_wide(terms, features, units):
@@ -734,15 +761,22 @@
     bits = list(range(dp.bit_length() - 1))
     near, far = bits[:3], bits[3:]
     plain, turned, crossed = near + far, near[2:] + near[:2] + far, near[1:] + far + near[:1]
-    tall, tall_sent = reduce_shards(mine_tall, got_tall, (crossed, crossed), first)
-    wide, _ = reduce_shards(mine_wide, got_wide, (plain, turned), first, after=tall_sent)
+    tall, tall_sent, _ = reduce_shards(mine_tall, got_tall, (crossed, crossed), first)
     got, _ = lax.optimization_barrier((got, tall_sent))
-    both = jnp.stack([jnp.where(first, mine, got), jnp.where(first, got, mine)], axis=1)
+    both = [
+        jnp.stack([jnp.where(first, a, b), jnp.where(first, b, a)], axis=2)
+        for a, b in zip(mine, got)
+    ]
+    both = [with_layout_constraint(b, Layout(major_to_minor=(0, 1, 2, 3))) for b in both]
+    wide, _, both = reduce_shards(
+        mine_wide, got_wide, (plain, turned), first, after=tall_sent, beside=both
+    )
+    activations, input_grads = (b.transpose(2, 0, 1, 3)[None] for b in both)
     g_up, g_qkv, g_out, g_bqv, g_bup, *vectors = split_wide(wide, features, units)
     ln1_gain, ln1_bias, g_bo, ln2_gain, ln2_bias, g_bd = vectors
     g_down = (tall[0].astype(F32) + tall[1].astype(F32))[None]
     outs = (ln1_gain, ln1_bias, g_qkv, g_bqv, g_out, g_bo, ln2_gain, ln2_bias, g_up, g_bup)
-    return (both[0][None], both[1][None]) + outs + (g_down, g_bd)
+    return (activations, input_grads) + outs + (g_down, g_bd)
 
 
 def solution(mesh):

time: 156 us -> 165 us (1.058)
  starting transfers between devices: 52.1 us -> 42.6 us
  other arithmetic: 10.1 us -> 16.9 us
  local copies, waits for them, and re-layouts: 17.6 us -> 23.4 us
  waiting for transfers between devices: 11.6 us -> 16.4 us
    ppermute x8, starting transfers between devices: 49.9 us -> 15 us  [reduce_shards(): arrived = lax.ppermute(send, ('segment', 'dp'), route)]
    ppermute x8, starting transfers between devices: 2.21 us -> 27.6 us  [swap_cores(): return lax.ppermute(block, 'segment', [(0, 1), (1, 0)])]
    another operation x2 -> x1, other arithmetic: 2.42 us -> 9.34 us  [on_device(): jnp.stack([jnp.where(first, a, b), jnp.where(first, b, a)], axis=2)]
    select_n x0 -> x4, local copies, waits for them, and re-layouts: none -> 5.61 us  [the longest x2 2.81 us: on_device(): jnp.where(first, a, b)]
    ppermute x8, waiting for transfers between devices: 10.7 us -> 16 us  [reduce_shards(): arrived = lax.ppermute(send, ('segment', 'dp'), route)]
    unnamed x24 -> x20, local copies, waits for them, and re-layouts: 12.6 us -> 7.31 us
    dynamic_slice x3, local copies, waits for them, and re-layouts: 0.8 us -> 4.46 us  [slices(): part = lax.dynamic_index_in_dim(view, index, 1, keepdims=False)]
    optimization_barrier x0 -> x1, local copies, waits for them, and re-layouts: none -> 1.73 us  [on_device(): got, _ = lax.optimization_barrier((got, tall_sent))]
  transfers between devices with their start and end apart: 16 -> 16, of which waited for: 5 -> 4; matrix products, arithmetic and copies ran while one was open for 16% -> 23% of each run, Pallas kernels for 1% -> 1%
where the time goes in v6:
time: 165 us; the launch traced here: 164 us
  Pallas kernels  63.6 us (39%)
  starting transfers between devices  42.6 us (26%)
  local copies, waits for them, and re-layouts  23.4 us (14%)
  other arithmetic  16.9 us (10%)
  waiting for transfers between devices  16.4 us (10%)
    pallas_call x1, Pallas kernels, run_layers(): pl.pallas_call(lambda *refs: layers_kernel(padded, keys, *refs), grid_spe...  60.4 us
    ppermute x8, starting transfers between devices, swap_cores(): return lax.ppermute(block, 'segment', [(0, 1), (1, 0)])  27.6 us
    ppermute x8, waiting for transfers between devices, reduce_shards(): arrived = lax.ppermute(send, ('segment', 'dp'), route)  16 us
    ppermute x8, starting transfers between devices, reduce_shards(): arrived = lax.ppermute(send, ('segment', 'dp'), route)  15 us
    another operation x1, other arithmetic, on_device(): jnp.stack([jnp.where(first, a, b), jnp.where(first, b, a)], axis=2)  9.34 us
    unnamed x20, local copies, waits for them, and re-layouts  7.31 us
    convert_element_type x9, other arithmetic, half(): return total.astype(BF16)  6.46 us
    dynamic_slice x3, local copies, waits for them, and re-layouts, slices(): part = lax.dynamic_index_in_dim(view, index, 1, keepdims=False)  4.46 us
  transfers between devices with their start and end apart: 16, of which 4 were waited for; matrix products, arithmetic and copies ran while one was open for 23% of the time, Pallas kernels for 1%

profile of v6, /device:TPU:0, one launch (start us, length us, event | category | flops | bytes accessed | tf_op | source)
XLA Modules:
  0.0 163.9 jit_solution(3355428166676655834)
XLA Ops:
  1.8 1.4 shard_map.254.refs_4_
  3.6 3.1 %copy.69.refs_2_ = bf16[2,6,197,384]{3,2,1,0:T(8,128)(2,1)} copy(bf16[2,6,197,384]{3,0,2,1:T(2,128)(2,1)} %param.15) | data formatting | bytes 3631104 | tf_op args[0]
  6.7 1.6 copy.70.refs_3_
  8.3 1.0 copy-done.6
  9.3 1.0 copy-done.5
  10.3 60.4 %shard_map.255 = (bf16[2,6,197,384]{3,2,1,0:T(8,128)(2,1)}, bf16[2,6,197,384]{3,2,1,0:T(8,128)(2,1)}, bf16[384,3200]{1,0:T(8,128)(2,1)}, bf16[384,3200]{1,0:T(8,...) custom-call(s32[2]{0:T(128)} %bitcast.106, s32[1]{0:T(128)} %bitcast.1.refs_1_, ...), custom_call_target="tpu_custom_call" | custom-call | flops 80000000000 | bytes 30000000 | tf_op jit(solution)/shard_map/pallas_call | solution.py:611
  70.7 25.7 %collective-permute-start.5 = (bf16[384,3200]{1,0:T(8,128)(2,1)}, bf16[384,3200]{1,0:T(8,128)(2,1)}, u32[]{:S(2)}, u32[]{:S(2)}) collective-permute-start(bf16[384,3200]{1,0:T(8,128)(2,1)} %get-tuple-element.41), channel_id=1, source_target_pairs={{0,16},{16,0},{1,17},{17,1},{2,18},{18,2},{3,19},{19,3},{4,20},{20... | collective-permute-start | bytes 7372808 | tf_op jit(solution)/shard_map/ppermute | solution.py:654
  96.4 4.3 %copy.71 = bf16[2,6,197,384]{3,0,2,1:T(2,128)(2,1)} copy(bf16[2,6,197,384]{3,2,1,0:T(8,128)(2,1)} %get-tuple-element.44) | data formatting | bytes 3631104 | tf_op jit(solution)/shard_map/pallas_call | solution.py:611
  101.4 1.5 constant_dynamic-slice_fusion.4
  103.0 2.2 %add_convert_fusion.1 = bf16[8,24,3200]{2,1,0:T(8,128)(2,1)S(1)} fusion(bf16[2,1,4,24,3200]{4,3,2,1,0:T(8,128)(2,1)S(1)} %get-tuple-element.80, bf16[2,1,4,24,3200]{4,3,2,1,0:T(8,128)(2,1)S(1)} %get-tuple-element.81, bf16[8,2,1,24,3200]{4,3,1,0,2:T(8,128)(2,1)} %bitcast.6, s32[]{:T(128)S(6)} %select_n.185, bf16[8,2,1,24,3200]{4,3,1,0,2:T(8,128)(2,1)S(1)} %bitcast.88, ...), kind=kLoop, calls=%fused_computation.1 | loop fusion | flops 3686400 | bytes 6144005 | tf_op jit(solution)/shard_map/convert_element_type | solution.py:688
  105.1 3.0 %collective-permute-start.6 = (bf16[8,24,3200]{2,1,0:T(8,128)(2,1)S(1)}, bf16[8,24,3200]{2,1,0:T(8,128)(2,1)S(1)}, u32[]{:S(2)}, u32[]{:S(2)}) collective-permute-start(bf16[8,24,3200]{2,1,0:T(8,128)(2,1)S(1)} %add_convert_fusion.1), channel_id=1, source_target_pairs={{0,1},{1,0},{2,3},{3,2},{4,5},{5,4},{6,7},{7,6},{8,9},{9,8},{10,11... | collective-permute-start | bytes 3686408 | tf_op jit(solution)/shard_map/ppermute | solution.py:701
  108.1 1.2 add_convert_fusion.4
  109.3 1.2 collective-permute-start.12
  110.4 1.7 %copy.72 = bf16[2,6,197,384]{3,2,1,0:T(8,128)(2,1)S(1)} copy(bf16[2,6,197,384]{3,0,2,1:T(2,128)(2,1)} %collective-permute-done.7) | data formatting | bytes 3631104 | tf_op jit(solution)/shard_map/optimization_barrier | solution.py:765
  112.6 1.4 copy.74
  114.0 1.4 copy.73
  115.4 1.4 copy.77
  116.8 1.4 copy.76
  118.2 1.5 constant_dynamic-slice_fusion
  119.7 9.3 %pad_maximum_fusion = (bf16[6,197,2,384]{3,2,1,0:T(2,128)(2,1)}, bf16[6,197,2,384]{3,2,1,0:T(2,128)(2,1)}) fusion(bf16[6,197,1,384]{3,2,1,0:T(2,128)(2,1)S(1)} %copy.74, bf16[6,197,1,384]{3,2,1,0:T(2,128)(2,1)S(1)} %copy.73, bf16[6,197,1,384]{3,2,1,0:T(2,128)(2,1)S(1)} %copy.77, bf16[6,197,1,384]{3,2,1,0:T(2,128)(2,1)S(1)} %copy.76), kind=kLoop, calls=%fused_computation.2 | loop fusion | flops 7262208 | bytes 7262208 | tf_op jit(solution)/shard_map/stack | solution.py:767
  129.0 1.5 constant_dynamic-slice_fusion.1
  131.4 1.0 collective-permute-start.9
  132.4 1.2 add_convert_fusion.9
  133.6 1.6 collective-permute-start.13
  135.3 6.4 %collective-permute-done.9 = bf16[4,24,3200]{2,1,0:T(8,128)(2,1)S(1)} collective-permute-done((bf16[4,24,3200]{2,1,0:T(8,128)(2,1)S(1)}, bf16[4,24,3200]{2,1,0:T(8,128)(2,1)S(1)}, u32[]{:S(2)}, u32[]{:S(2)}) %collective-permute-start.9) | collective-permute-done | bytes 614432 | tf_op jit(solution)/shard_map/ppermute | solution.py:701
  141.8 1.7 %collective-permute-start.10 = (bf16[2,24,3200]{2,1,0:T(8,128)(2,1)S(1)}, bf16[2,24,3200]{2,1,0:T(8,128)(2,1)S(1)}, u32[]{:S(2)}, u32[]{:S(2)}) collective-permute-start(bf16[2,24,3200]{2,1,0:T(8,128)(2,1)S(1)} %get-tuple-element.73), channel_id=1, source_target_pairs={{0,4},{1,5},{2,6},{3,7},{4,0},{5,1},{6,2},{7,3},{8,12},{9,13},{10,... | collective-permute-start | bytes 921608 | tf_op jit(solution)/shard_map/ppermute | solution.py:701
  143.6 2.0 %collective-permute-start.14 = (bf16[2,96,384]{2,1,0:T(8,128)(2,1)S(1)}, bf16[2,96,384]{2,1,0:T(8,128)(2,1)S(1)}, u32[]{:S(2)}, u32[]{:S(2)}) collective-permute-start(bf16[2,96,384]{2,1,0:T(8,128)(2,1)S(1)} %get-tuple-element.79), channel_id=1, source_target_pairs={{0,8},{1,9},{2,10},{3,11},{4,12},{5,13},{6,14},{7,15},{8,0},{9,1},... | collective-permute-start | bytes 442376 | tf_op jit(solution)/shard_map/ppermute | solution.py:701
  145.6 5.5 %collective-permute-done.14 = bf16[2,96,384]{2,1,0:T(8,128)(2,1)S(1)} collective-permute-done((bf16[2,96,384]{2,1,0:T(8,128)(2,1)S(1)}, bf16[2,96,384]{2,1,0:T(8,128)(2,1)S(1)}, u32[]{:S(2)}, u32[]{:S(2)}) %collective-permute-start.14) | collective-permute-done | bytes 147488 | tf_op jit(solution)/shard_map/ppermute | solution.py:701
  151.1 1.2 collective-permute-start.15
  153.0 3.4 %collective-permute-start.11 = (bf16[1,24,3200]{2,1,0:T(8,128)(2,1)S(1)}, bf16[1,24,3200]{2,1,0:T(8,128)(2,1)S(1)}, u32[]{:S(2)}, u32[]{:S(2)}) collective-permute-start(bf16[1,24,3200]{2,1,0:T(8,128)(2,1)S(1)} %get-tuple-element.76), channel_id=1, source_target_pairs={{0,8},{1,9},{2,10},{3,11},{4,12},{5,13},{6,14},{7,15},{8,0},{9,1},... | collective-permute-start | bytes 460808 | tf_op jit(solution)/shard_map/ppermute | solution.py:701
  157.1 4.1 %collective-permute-done.11 = bf16[1,24,3200]{2,1,0:T(8,128)(2,1)S(1)} collective-permute-done((bf16[1,24,3200]{2,1,0:T(8,128)(2,1)S(1)}, bf16[1,24,3200]{2,1,0:T(8,128)(2,1)S(1)}, u32[]{:S(2)}, u32[]{:S(2)}) %collective-permute-start.11) | collective-permute-done | bytes 153632 | tf_op jit(solution)/shard_map/ppermute | solution.py:701
  161.9 1.8 %shard_map.256 = (f32[1,24,1536]{2,1,0:T(8,128)}, f32[1,24,1152]{2,1,0:T(8,128)}, f32[1,24,384]{2,1,0:T(8,128)}, f32[1,48]{1,0:T(1,128)}, f32[1,96]{1,0:T(1,128)...) custom-call(bf16[24,3200]{1,0:T(8,128)(2,1)} %get-tuple-element.77.o, ...), custom_call_target="tpu_custom_call" | custom-call | tf_op jit(solution)/shard_map/pallas_call | solution.py:737
  (44 shorter events, 6.0 us)
Async XLA Ops:
  0.6 7.7 %collective-permute-start.3 = (bf16[1,384,1536]{2,1,0:T(8,128)(2,1)}, bf16[1,384,1536]{2,1,0:T(8,128)(2,1)S(1)}, u32[]{:S(2)}, u32[]{:S(2)}) collective-permute-start(bf16[1,384,1536]{2,1,0:T(8,128)(2,1)} %refs_8_.1), channel_id=1, source_target_pairs={{0,16},{16,0},{1,17},{17,1},{2,18},{18,2},{3,19},{19,3},{4,20},{20... | collective-permute-start | bytes 3538952 | tf_op jit(solution)/shard_map/ppermute | solution.py:654
  1.2 8.1 %collective-permute-start.4 = (bf16[1,1536,384]{2,1,0:T(8,128)(2,1)}, bf16[1,1536,384]{2,1,0:T(8,128)(2,1)}, u32[]{:S(2)}, u32[]{:S(2)}) collective-permute-start(bf16[1,1536,384]{2,1,0:T(8,128)(2,1)} %refs_9_.1), channel_id=1, source_target_pairs={{0,16},{16,0},{1,17},{17,1},{2,18},{18,2},{3,19},{19,3},{4,20},{20... | collective-permute-start | bytes 3538952 | tf_op jit(solution)/shard_map/ppermute | solution.py:654
  1.2 7.0 %collective-permute-start.1 = (bf16[1,384,1152]{2,1,0:T(8,128)(2,1)}, bf16[1,384,1152]{2,1,0:T(8,128)(2,1)S(1)}, u32[]{:S(2)}, u32[]{:S(2)}) collective-permute-start(bf16[1,384,1152]{2,1,0:T(8,128)(2,1)} %refs_6_.3), channel_id=1, source_target_pairs={{0,16},{16,0},{1,17},{17,1},{2,18},{18,2},{3,19},{19,3},{4,20},{20... | collective-permute-start | bytes 2654216 | tf_op jit(solution)/shard_map/ppermute | solution.py:654
  1.7 6.6 %collective-permute-start.2 = (bf16[1,384,384]{2,1,0:T(8,128)(2,1)}, bf16[1,384,384]{2,1,0:T(8,128)(2,1)S(1)}, u32[]{:S(2)}, u32[]{:S(2)}) collective-permute-start(bf16[1,384,384]{2,1,0:T(8,128)(2,1)} %refs_7_.3), channel_id=1, source_target_pairs={{0,16},{16,0},{1,17},{17,1},{2,18},{18,2},{3,19},{19,3},{4,20},{20... | collective-permute-start | bytes 884744 | tf_op jit(solution)/shard_map/ppermute | solution.py:654
  3.2 5.1 %collective-permute-start = (f32[1,4992]{1,0:T(1,128)}, f32[1,4992]{1,0:T(1,128)S(1)}, u32[]{:S(2)}, u32[]{:S(2)}) collective-permute-start(f32[1,4992]{1,0:T(1,128)} %shard_map.254.refs_4_), channel_id=1, source_target_pairs={{0,16},{16,0},{1,17},{17,1},{2,18},{18,2},{3,19},{19,3},{4,20},{20... | collective-permute-start | bytes 59912 | tf_op jit(solution)/shard_map/ppermute | solution.py:654
  3.6 3.1 %copy-start.2 = (bf16[2,6,197,384]{3,0,2,1:T(2,128)(2,1)S(1)}, bf16[2,6,197,384]{3,0,2,1:T(2,128)(2,1)}, u32[]{:S(2)}) copy-start(bf16[2,6,197,384]{3,0,2,1:T(2,128)(2,1)} %param.17) | copy-start | bytes 5446660
  8.3 1.0 copy-start.8
  8.3 1.0 copy-start.7
  8.3 1.0 copy-start.6
  9.3 1.0 copy-start.5
  70.7 30.3 %collective-permute-start.5 = (bf16[384,3200]{1,0:T(8,128)(2,1)}, bf16[384,3200]{1,0:T(8,128)(2,1)}, u32[]{:S(2)}, u32[]{:S(2)}) collective-permute-start(bf16[384,3200]{1,0:T(8,128)(2,1)} %get-tuple-element.41), channel_id=1, source_target_pairs={{0,16},{16,0},{1,17},{17,1},{2,18},{18,2},{3,19},{19,3},{4,20},{20... | collective-permute-start | bytes 7372808 | tf_op jit(solution)/shard_map/ppermute | solution.py:654
  96.4 5.0 %copy-start = (bf16[384,3200]{1,0:T(8,128)(2,1)S(1)}, bf16[384,3200]{1,0:T(8,128)(2,1)}, u32[]{:S(2)}) copy-start(bf16[384,3200]{1,0:T(8,128)(2,1)} %get-tuple-element.50) | copy-start | bytes 7372804
  100.7 9.8 %collective-permute-start.7 = (bf16[2,6,197,384]{3,0,2,1:T(2,128)(2,1)}, bf16[2,6,197,384]{3,0,2,1:T(2,128)(2,1)}, u32[]{:S(2)}, u32[]{:S(2)}) collective-permute-start(bf16[2,6,197,384]{3,0,2,1:T(2,128)(2,1)} %copy.71), channel_id=1, source_target_pairs={{0,16},{16,0},{1,17},{17,1},{2,18},{18,2},{3,19},{19,3},{4,20},{20... | collective-permute-start | bytes 5446664 | tf_op jit(solution)/shard_map/ppermute | solution.py:654
  101.0 7.1 %collective-permute-start.8 = (bf16[1536,384]{1,0:T(8,128)(2,1)}, bf16[1536,384]{1,0:T(8,128)(2,1)S(1)}, u32[]{:S(2)}, u32[]{:S(2)}) collective-permute-start(bf16[1536,384]{1,0:T(8,128)(2,1)} %get-tuple-element.46), channel_id=1, source_target_pairs={{0,16},{16,0},{1,17},{17,1},{2,18},{18,2},{3,19},{19,3},{4,20},{20... | collective-permute-start | bytes 3538952 | tf_op jit(solution)/shard_map/ppermute | solution.py:654
  102.9 5.2 %copy-start.3 = (bf16[1536,384]{1,0:T(8,128)(2,1)S(1)}, bf16[1536,384]{1,0:T(8,128)(2,1)}, u32[]{:S(2)}) copy-start(bf16[1536,384]{1,0:T(8,128)(2,1)} %get-tuple-element.45) | copy-start | bytes 3538948
  105.1 26.0 %collective-permute-start.6 = (bf16[8,24,3200]{2,1,0:T(8,128)(2,1)S(1)}, bf16[8,24,3200]{2,1,0:T(8,128)(2,1)S(1)}, u32[]{:S(2)}, u32[]{:S(2)}) collective-permute-start(bf16[8,24,3200]{2,1,0:T(8,128)(2,1)S(1)} %add_convert_fusion.1), channel_id=1, source_target_pairs={{0,1},{1,0},{2,3},{3,2},{4,5},{5,4},{6,7},{7,6},{8,9},{9,8},{10,11... | collective-permute-start | bytes 3686408 | tf_op jit(solution)/shard_map/ppermute | solution.py:701
  109.3 2.9 %copy-start.1 = (bf16[2,6,197,384]{3,2,1,0:T(8,128)(2,1)S(1)}, bf16[2,6,197,384]{3,2,1,0:T(8,128)(2,1)}, u32[]{:S(2)}) copy-start(bf16[2,6,197,384]{3,2,1,0:T(8,128)(2,1)} %get-tuple-element.43) | copy-start | bytes 5446660
  109.3 23.1 %collective-permute-start.12 = (bf16[8,96,384]{2,1,0:T(8,128)(2,1)}, bf16[8,96,384]{2,1,0:T(8,128)(2,1)}, u32[]{:S(2)}, u32[]{:S(2)}) collective-permute-start(bf16[8,96,384]{2,1,0:T(8,128)(2,1)} %bitcast.12), channel_id=1, source_target_pairs={{0,2},{1,3},{2,0},{3,1},{4,6},{5,7},{6,4},{7,5},{8,10},{9,11},{10,... | collective-permute-start | bytes 1769480 | tf_op jit(solution)/shard_map/ppermute | solution.py:701
  131.4 10.2 %collective-permute-start.9 = (bf16[4,24,3200]{2,1,0:T(8,128)(2,1)S(1)}, bf16[4,24,3200]{2,1,0:T(8,128)(2,1)S(1)}, u32[]{:S(2)}, u32[]{:S(2)}) collective-permute-start(bf16[4,24,3200]{2,1,0:T(8,128)(2,1)S(1)} %get-tuple-element.69), channel_id=1, source_target_pairs={{0,2},{1,3},{2,0},{3,1},{4,6},{5,7},{6,4},{7,5},{8,10},{9,11},{10,... | collective-permute-start | bytes 1843208 | tf_op jit(solution)/shard_map/ppermute | solution.py:701
  133.6 9.9 %collective-permute-start.13 = (bf16[4,96,384]{2,1,0:T(8,128)(2,1)S(1)}, bf16[4,96,384]{2,1,0:T(8,128)(2,1)S(1)}, u32[]{:S(2)}, u32[]{:S(2)}) collective-permute-start(bf16[4,96,384]{2,1,0:T(8,128)(2,1)S(1)} %bitcast.103), channel_id=1, source_target_pairs={{0,4},{1,5},{2,6},{3,7},{4,0},{5,1},{6,2},{7,3},{8,12},{9,13},{10,... | collective-permute-start | bytes 884744 | tf_op jit(solution)/shard_map/ppermute | solution.py:701
  141.8 10.5 %collective-permute-start.10 = (bf16[2,24,3200]{2,1,0:T(8,128)(2,1)S(1)}, bf16[2,24,3200]{2,1,0:T(8,128)(2,1)S(1)}, u32[]{:S(2)}, u32[]{:S(2)}) collective-permute-start(bf16[2,24,3200]{2,1,0:T(8,128)(2,1)S(1)} %get-tuple-element.73), channel_id=1, source_target_pairs={{0,4},{1,5},{2,6},{3,7},{4,0},{5,1},{6,2},{7,3},{8,12},{9,13},{10,... | collective-permute-start | bytes 921608 | tf_op jit(solution)/shard_map/ppermute | solution.py:701
  143.6 7.5 %collective-permute-start.14 = (bf16[2,96,384]{2,1,0:T(8,128)(2,1)S(1)}, bf16[2,96,384]{2,1,0:T(8,128)(2,1)S(1)}, u32[]{:S(2)}, u32[]{:S(2)}) collective-permute-start(bf16[2,96,384]{2,1,0:T(8,128)(2,1)S(1)} %get-tuple-element.79), channel_id=1, source_target_pairs={{0,8},{1,9},{2,10},{3,11},{4,12},{5,13},{6,14},{7,15},{8,0},{9,1},... | collective-permute-start | bytes 442376 | tf_op jit(solution)/shard_map/ppermute | solution.py:701
  151.1 5.3 %collective-permute-start.15 = (bf16[1,96,384]{2,1,0:T(8,128)(2,1)S(1)}, bf16[1,96,384]{2,1,0:T(8,128)(2,1)S(1)}, u32[]{:S(2)}, u32[]{:S(2)}) collective-permute-start(bf16[1,96,384]{2,1,0:T(8,128)(2,1)S(1)} %fusion.6), channel_id=1, source_target_pairs={{0,1},{1,0},{2,3},{3,2},{4,5},{5,4},{6,7},{7,6},{8,9},{9,8},{10,11... | collective-permute-start | bytes 221192 | tf_op jit(solution)/shard_map/ppermute | solution.py:701
  153.0 8.2 %collective-permute-start.11 = (bf16[1,24,3200]{2,1,0:T(8,128)(2,1)S(1)}, bf16[1,24,3200]{2,1,0:T(8,128)(2,1)S(1)}, u32[]{:S(2)}, u32[]{:S(2)}) collective-permute-start(bf16[1,24,3200]{2,1,0:T(8,128)(2,1)S(1)} %get-tuple-element.76), channel_id=1, source_target_pairs={{0,8},{1,9},{2,10},{3,11},{4,12},{5,13},{6,14},{7,15},{8,0},{9,1},... | collective-permute-start | bytes 460808 | tf_op jit(solution)/shard_map/ppermute | solution.py:701
  161.3 0.7 copy-start.4

commit v7 on v5

--- a/solution.py
+++ b/solution.py
@@ -216,7 +216,7 @@
     def forward(layer):
         @pl.when(step == 0)
         def _():
-            for n in range(4):
+            for n in range(2):
                 load(own, n, layer).wait()
 
         for at, size in row_chunks(rows):
@@ -280,6 +280,11 @@
         attend(len(tasks) - 1)
         project(GROUP - 1)
         norm_two(GROUP - 1)
+
+        @pl.when(step == 0)
+        def _():
+            for n in range(2, 4):
+                load(own, n, layer).wait()
 
         def up(c):
             before[:, chunks[c]] = dot(second[layer], w_up[layer, :, chunks[c]])
@@ -629,53 +634,54 @@
     return lax.ppermute(block, "segment", [(0, 1), (1, 0)])
 
 
-def reduce_shards(mine, got, orders, first, after=None):
-    dp = lax.axis_size("dp")
-    me = lax.axis_index("dp")
-    bits = dp.bit_length() - 1
-    rest = (mine.shape[0] // dp, mine.shape[1])
-    terms = (mine, got)
-    held = [list(range(bits)) for _ in orders]
-    first_send = None
-    for n in range(bits):
-        below = [left.index(order[n]) for order, left in zip(orders, held)]
-        bit = [(me >> order[n]) & 1 for order in orders]
-        for order, left in zip(orders, held):
+class Shards:
+    def __init__(self, mine, got, orders, first):
+        self.dp = lax.axis_size("dp")
+        self.bits = self.dp.bit_length() - 1
+        self.rest = (mine.shape[0] // self.dp, mine.shape[1])
+        self.terms = (mine, got)
+        self.orders, self.first = orders, first
+        self.held = [list(range(self.bits)) for _ in orders]
+
+    def wait_for(self, *others):
+        self.terms = lax.optimization_barrier(self.terms + others)[:2]
+
+    def begin(self, n):
+        me = lax.axis_index("dp")
+        self.below = [left.index(order[n]) for order, left in zip(self.orders, self.held)]
+        self.bit = [(me >> order[n]) & 1 for order in self.orders]
+        for order, left in zip(self.orders, self.held):
             left.remove(order[n])
 
-        def slices(terms, at, index):
-            taken = []
-            for term in terms:
-                view = term.reshape((-1, 2, 1 << at) + rest)
-                part = lax.dynamic_index_in_dim(view, index, 1, keepdims=False)
-                taken.append(part.reshape((-1,) + rest))
-            return taken
-
-        def half(terms, other):
-            if below[0] == below[1]:
-                index = jnp.where(first, bit[0], bit[1])
-                taken = slices(terms, below[0], 1 - index if other else index)
-            else:
-                index = [1 - b if other else b for b in bit]
-                sides = zip(slices(terms, below[0], index[0]), slices(terms, below[1], index[1]))
-                taken = [jnp.where(first, a, b) for a, b in sides]
-            total = sum(part.astype(F32) for part in taken)
-            return total.astype(BF16)
-
-        send = half(terms, True)
-        if n == 0:
-            first_send = send
-            if after is not None:
-                terms = lax.optimization_barrier(terms + (after,))[:2]
-        keep = half(terms, False)
+    def slices(self, at, index):
+        taken = []
+        for term in self.terms:
+            view = term.reshape((-1, 2, 1 << at) + self.rest)
+            part = lax.dynamic_index_in_dim(view, index, 1, keepdims=False)
+            taken.append(part.reshape((-1,) + self.rest))
+        return taken
+
+    def half(self, other):
+        index = [1 - b if other else b for b in self.bit]
+        below, first = self.below, self.first
+        if below[0] == below[1]:
+            taken = self.slices(below[0], jnp.where(first, index[0], index[1]))
+        else:
+            sides = zip(self.slices(below[0], index[0]), self.slices(below[1], index[1]))
+            taken = [jnp.where(first, a, b) for a, b in sides]
+        return sum(part.astype(F32) for part in taken).astype(BF16)
+
+    def exchange(self, n, send):
+        keep = self.half(False)
         route = [
-            (core * dp + i, core * dp + (i ^ (1 << order[n])))
-            for core, order in enumerate(orders)
-            for i in range(dp)
+            (core * self.dp + i, core * self.dp + (i ^ (1 << order[n])))
+            for core, order in enumerate(self.orders)
+            for i in range(self.dp)
         ]
-        arrived = lax.ppermute(send, ("segment", "dp"), route)
-        terms = (keep, arrived)
-    return tuple(t.reshape(rest) for t in terms), first_send
+        self.terms = (keep, lax.ppermute(send, ("segment", "dp"), route))
+
+    def result(self):
+        return tuple(t.reshape(self.rest) for t in self.terms)
 
 
 def split_wide(terms, features, units):
@@ -730,14 +736,33 @@
     got_wide = swap_cores(away_wide)
     away_tall, got_wide = lax.optimization_barrier((away_tall, got_wide))
     got_tall = swap_cores(away_tall)
-    got = swap_cores(away)
     bits = list(range(dp.bit_length() - 1))
     near, far = bits[:3], bits[3:]
     plain, turned, crossed = near + far, near[2:] + near[:2] + far, near[1:] + far + near[:1]
-    tall, tall_sent = reduce_shards(mine_tall, got_tall, (crossed, crossed), first)
-    wide, _ = reduce_shards(mine_wide, got_wide, (plain, turned), first, after=tall_sent)
-    got, _ = lax.optimization_barrier((got, tall_sent))
-    both = jnp.stack([jnp.where(first, mine, got), jnp.where(first, got, mine)], axis=1)
+    wide = Shards(mine_wide, got_wide, (plain, turned), first)
+    tall = Shards(mine_tall, got_tall, (crossed, crossed), first)
+    for n in bits:
+        wide.begin(n)
+        tall.begin(n)
+        wide_send = wide.half(True)
+        if n in (0, bits[-1]):
+            tall.wait_for(wide_send)
+        tall_send = tall.half(True)
+        if n == 0:
+            wide.wait_for(tall_send)
+            away, _ = lax.optimization_barrier((away, tall_send))
+            got = swap_cores(away)
+            both = [
+                jnp.stack([jnp.where(first, a, b), jnp.where(first, b, a)])
+                for a, b in zip(mine, got)
+            ]
+        wide.exchange(n, wide_send)
+        tall.exchange(n, tall_send)
+        if n == 0:
+            keep, arrived, *both = lax.optimization_barrier(wide.terms + tuple(both))
+            wide.terms = (keep, arrived)
+    *both, _ = lax.optimization_barrier((*both, tall_send))
+    wide, tall = wide.result(), tall.result()
     g_up, g_qkv, g_out, g_bqv, g_bup, *vectors = split_wide(wide, features, units)
     ln1_gain, ln1_bias, g_bo, ln2_gain, ln2_bias, g_bd = vectors
     g_down = (tall[0].astype(F32) + tall[1].astype(F32))[None]

time: 156 us -> 158 us (1.013)
  Pallas kernels: 63.2 us -> 38.6 us
  starting transfers between devices: 52.1 us -> 69.6 us
  waiting for transfers between devices: 11.6 us -> 17.5 us
  other arithmetic: 10.1 us -> 12.4 us
    pallas_call x1, Pallas kernels: 60 us -> 35.4 us  [run_layers(): pl.pallas_call(lambda *refs: layers_kernel(padded, keys, *refs), grid_spe...]
    ppermute x8, starting transfers between devices: 2.21 us -> 26.1 us  [swap_cores(): return lax.ppermute(block, 'segment', [(0, 1), (1, 0)])]
    ppermute x8, waiting for transfers between devices: 0.88 us -> 7.25 us  [swap_cores(): return lax.ppermute(block, 'segment', [(0, 1), (1, 0)])]
    ppermute x8, starting transfers between devices: 49.9 us -> 43.5 us  [exchange(): self.terms = (keep, lax.ppermute(send, ('segment', 'dp'), route))]
    pallas_call x1 -> x0, local copies, waits for them, and re-layouts: 4.28 us -> none  [run_layers(): pl.pallas_call(lambda *refs: layers_kernel(padded, keys, *refs), grid_spe...]
    another operation x0 -> x1, local copies, waits for them, and re-layouts: none -> 2.51 us  [on_device(): zip(mine, got)]
    convert_element_type x9 -> x8, other arithmetic: 7 us -> 8.82 us  [half(): return sum((part.astype(F32) for part in taken)).astype(BF16)]
    unnamed x24 -> x26, local copies, waits for them, and re-layouts: 12.6 us -> 12.9 us
  transfers between devices with their start and end apart: 16 -> 16, of which waited for: 5 -> 5; matrix products, arithmetic and copies ran while one was open for 16% -> 18% of each run, Pallas kernels for 1% -> 1%
where the time goes in v7:
time: 158 us
  starting transfers between devices  69.6 us (44%)
  Pallas kernels  38.6 us (24%)
  local copies, waits for them, and re-layouts  18.7 us (12%)
  waiting for transfers between devices  17.5 us (11%)
  other arithmetic  12.4 us (8%)
    ppermute x8, starting transfers between devices, exchange(): self.terms = (keep, lax.ppermute(send, ('segment', 'dp'), route))  43.5 us
    pallas_call x1, Pallas kernels, run_layers(): pl.pallas_call(lambda *refs: layers_kernel(padded, keys, *refs), grid_spe...  35.4 us
    ppermute x8, starting transfers between devices, swap_cores(): return lax.ppermute(block, 'segment', [(0, 1), (1, 0)])  26.1 us
    unnamed x26, local copies, waits for them, and re-layouts  12.9 us
    ppermute x8, waiting for transfers between devices, exchange(): self.terms = (keep, lax.ppermute(send, ('segment', 'dp'), route))  10.2 us
    convert_element_type x8, other arithmetic, half(): return sum((part.astype(F32) for part in taken)).astype(BF16)  8.82 us
    ppermute x8, waiting for transfers between devices, swap_cores(): return lax.ppermute(block, 'segment', [(0, 1), (1, 0)])  7.25 us
  transfers between devices with their start and end apart: 16, of which 5 were waited for; matrix products, arithmetic and copies ran while one was open for 18% of the time, Pallas kernels for 1%

profile of v7, /device:TPU:0, one launch (start us, length us, event | category | flops | bytes accessed | tf_op | source)
XLA Modules:
  0.0 157.7 jit_solution(1626243217011052173)
XLA Ops:
  1.8 1.4 shard_map.254.refs_4_
  3.6 3.1 %copy.37.refs_2_ = bf16[2,6,197,384]{3,2,1,0:T(8,128)(2,1)} copy(bf16[2,6,197,384]{3,0,2,1:T(2,128)(2,1)} %param.15) | data formatting | bytes 3631104 | tf_op args[0]
  6.7 1.5 copy.38.refs_3_
  8.3 1.0 copy-done.8
  9.3 1.0 copy-done.7
  10.2 35.4 %shard_map.255 = (bf16[2,6,197,384]{3,2,1,0:T(8,128)(2,1)}, bf16[2,6,197,384]{3,2,1,0:T(8,128)(2,1)}, bf16[384,3200]{1,0:T(8,128)(2,1)}, bf16[384,3200]{1,0:T(8,...) custom-call(s32[2]{0:T(128)} %bitcast.81, s32[1]{0:T(128)} %bitcast.1.refs_1_, ...), custom_call_target="tpu_custom_call" | custom-call | flops 80000000000 | bytes 30000000 | tf_op jit(solution)/shard_map/pallas_call | solution.py:591
  45.7 24.1 %collective-permute-start.5 = (bf16[384,3200]{1,0:T(8,128)(2,1)}, bf16[384,3200]{1,0:T(8,128)(2,1)S(1)}, u32[]{:S(2)}, u32[]{:S(2)}) collective-permute-start(bf16[384,3200]{1,0:T(8,128)(2,1)} %get-tuple-element.48), channel_id=1, source_target_pairs={{0,16},{16,0},{1,17},{17,1},{2,18},{18,2},{3,19},{19,3},{4,20},{20... | collective-permute-start | bytes 7372808 | tf_op jit(solution)/shard_map/ppermute | solution.py:634
  69.8 4.5 %collective-permute-done.5 = bf16[384,3200]{1,0:T(8,128)(2,1)S(1)} collective-permute-done((bf16[384,3200]{1,0:T(8,128)(2,1)}, bf16[384,3200]{1,0:T(8,128)(2,1)S(1)}, u32[]{:S(2)}, u32[]{:S(2)}) %collective-permute-start.5) | collective-permute-done | bytes 2457632 | tf_op jit(solution)/shard_map/ppermute | solution.py:634
  74.6 1.6 %constant_dynamic-slice_fusion.2 = (bf16[2,1,4,24,3200]{4,3,2,1,0:T(8,128)(2,1)S(1)}, bf16[2,1,4,24,3200]{4,3,2,1,0:T(8,128)(2,1)S(1)}) fusion(bf16[2,2,4,24,3200]{4,3,2,1,0:T(8,128)(2,1)S(1)} %bitcast.68, s32[]{:T(128)S(6)} %select_n.138, bf16[2,2,4,24,3200]{4,3,2,1,0:T(8,128)(2,1)} %bitcast.64), kind=kLoop, calls=%fused_computation.36 | loop fusion | bytes 4915204 | tf_op jit(solution)/shard_map/jit(dynamic_index_in_dim)/dynamic_slice | solution.py:660
  77.5 3.0 %collective-permute-start.7 = (bf16[8,24,3200]{2,1,0:T(8,128)(2,1)S(1)}, bf16[8,24,3200]{2,1,0:T(8,128)(2,1)S(1)}, u32[]{:S(2)}, u32[]{:S(2)}) collective-permute-start(bf16[8,24,3200]{2,1,0:T(8,128)(2,1)S(1)} %add_convert_fusion.1), channel_id=1, source_target_pairs={{0,1},{1,0},{2,3},{3,2},{4,5},{5,4},{6,7},{7,6},{8,9},{9,8},{10,11... | collective-permute-start | bytes 3686408 | tf_op jit(solution)/shard_map/ppermute | solution.py:681
  80.5 1.1 add_convert_fusion.4
  81.7 26.8 %collective-permute-start.9 = (bf16[8,96,384]{2,1,0:T(8,128)(2,1)}, bf16[8,96,384]{2,1,0:T(8,128)(2,1)}, u32[]{:S(2)}, u32[]{:S(2)}) collective-permute-start(bf16[8,96,384]{2,1,0:T(8,128)(2,1)} %bitcast.12), channel_id=1, source_target_pairs={{0,2},{1,3},{2,0},{3,1},{4,6},{5,7},{6,4},{7,5},{8,10},{9,11},{10,... | collective-permute-start | bytes 1769480 | tf_op jit(solution)/shard_map/ppermute | solution.py:681
  108.4 1.4 copy.39
  110.1 0.8 add_convert_fusion
  110.9 2.7 %collective-permute-done.8 = bf16[2,6,197,384]{3,0,2,1:T(2,128)(2,1)S(1)} collective-permute-done((bf16[2,6,197,384]{3,0,2,1:T(2,128)(2,1)S(1)}, bf16[2,6,197,384]{3,0,2,1:T(2,128)(2,1)S(1)}, u32[]{:S(2)}, u32[]{:S(2)}) %collective-permute-start.8) | collective-permute-done | bytes 1815584 | tf_op jit(solution)/shard_map/ppermute | solution.py:634
  113.7 2.5 %fusion.7 = (bf16[1,6,197,384]{3,0,2,1:T(2,128)(2,1)S(1)}, bf16[1,6,197,384]{3,0,2,1:T(2,128)(2,1)S(1)}) fusion(bf16[2,6,197,384]{3,0,2,1:T(2,128)(2,1)S(1)} %collective-permute-done.8), kind=kLoop, calls=%fused_computation.38 | loop fusion | bytes 3631104 | tf_op jit(solution)/shard_map/unstack | solution.py:757
  116.9 1.5 pad_maximum_fusion.1
  118.4 1.1 add_convert_fusion.3
  119.5 4.2 %collective-permute-start.12 = (bf16[4,24,3200]{2,1,0:T(8,128)(2,1)}, bf16[4,24,3200]{2,1,0:T(8,128)(2,1)}, u32[]{:S(2)}, u32[]{:S(2)}) collective-permute-start(bf16[4,24,3200]{2,1,0:T(8,128)(2,1)} %get-tuple-element.125), channel_id=1, source_target_pairs={{0,2},{1,3},{2,0},{3,1},{4,6},{5,7},{6,4},{7,5},{8,10},{9,11},{10,... | collective-permute-start | bytes 1843208 | tf_op jit(solution)/shard_map/ppermute | solution.py:681
  123.7 1.9 %add_convert_fusion.9 = (bf16[2,1,2,96,384]{4,3,2,1,0:T(8,128)(2,1)S(1)}, bf16[2,1,2,96,384]{4,3,2,1,0:T(8,128)(2,1)}) fusion(bf16[2,2,2,96,384]{4,3,2,1,0:T(8,128)(2,1)} %bitcast.22, s32[]{:T(128)S(6)} %select_n.143, bf16[2,2,2,96,384]{4,3,2,1,0:T(8,128)(2,1)S(1)} %bitcast.76, s32[]{:T(128)S(6)} %select_n.138), kind=kLoop, calls=%fused_computation.20 | loop fusion | flops 1179648 | bytes 1769480 | tf_op jit(solution)/shard_map/convert_element_type | solution.py:672
  125.6 1.6 collective-permute-start.10
  127.1 5.0 %collective-permute-done.12 = bf16[4,24,3200]{2,1,0:T(8,128)(2,1)} collective-permute-done((bf16[4,24,3200]{2,1,0:T(8,128)(2,1)}, bf16[4,24,3200]{2,1,0:T(8,128)(2,1)}, u32[]{:S(2)}, u32[]{:S(2)}) %collective-permute-start.12) | collective-permute-done | bytes 614432 | tf_op jit(solution)/shard_map/ppermute | solution.py:681
  132.1 1.9 %add_convert_fusion.7 = (bf16[2,1,1,24,3200]{4,3,2,1,0:T(8,128)(2,1)S(1)}, bf16[2,24,3200]{2,1,0:T(8,128)(2,1)}) fusion(bf16[2,2,1,24,3200]{4,3,2,1,0:T(8,128)(2,1)} %bitcast.31, s32[]{:T(128)S(6)} %select_n.157, bf16[2,2,1,24,3200]{4,3,2,1,0:T(8,128)(2,1)S(1)} %bitcast.75, s32[]{:T(128)S(6)} %select_n.161), kind=kLoop, calls=%fused_computation.18 | loop fusion | flops 1228800 | bytes 1843208 | tf_op jit(solution)/shard_map/convert_element_type | solution.py:672
  134.0 1.6 collective-permute-start.13
  135.6 1.1 fusion.6
  136.7 3.1 %collective-permute-start.11 = (bf16[2,96,384]{2,1,0:T(8,128)(2,1)S(1)}, bf16[2,96,384]{2,1,0:T(8,128)(2,1)S(1)}, u32[]{:S(2)}, u32[]{:S(2)}) collective-permute-start(bf16[2,96,384]{2,1,0:T(8,128)(2,1)S(1)} %get-tuple-element.138), channel_id=1, source_target_pairs={{0,8},{1,9},{2,10},{3,11},{4,12},{5,13},{6,14},{7,15},{8,0},{9,1},... | collective-permute-start | bytes 442376 | tf_op jit(solution)/shard_map/ppermute | solution.py:681
  139.8 4.5 %collective-permute-done.13 = bf16[2,24,3200]{2,1,0:T(8,128)(2,1)S(1)} collective-permute-done((bf16[2,24,3200]{2,1,0:T(8,128)(2,1)}, bf16[2,24,3200]{2,1,0:T(8,128)(2,1)S(1)}, u32[]{:S(2)}, u32[]{:S(2)}) %collective-permute-start.13) | collective-permute-done | bytes 307232 | tf_op jit(solution)/shard_map/ppermute | solution.py:681
  145.0 1.6 collective-permute-start.15
  146.6 1.8 %collective-permute-start.14 = (bf16[1,24,3200]{2,1,0:T(8,128)(2,1)S(1)}, bf16[1,24,3200]{2,1,0:T(8,128)(2,1)S(1)}, u32[]{:S(2)}, u32[]{:S(2)}) collective-permute-start(bf16[1,24,3200]{2,1,0:T(8,128)(2,1)S(1)} %get-tuple-element.137), channel_id=1, source_target_pairs={{0,8},{1,9},{2,10},{3,11},{4,12},{5,13},{6,14},{7,15},{8,0},{9,1},... | collective-permute-start | bytes 460808 | tf_op jit(solution)/shard_map/ppermute | solution.py:681
  148.4 2.6 %copy.42 = bf16[1,2,6,197,384]{4,1,3,2,0:T(2,128)(2,1)} copy(bf16[1,2,6,197,384]{4,3,2,1,0:T(8,128)(2,1)S(1)} %bitcast.72) | data formatting | bytes 3631104
  151.0 2.6 %copy.43 = bf16[1,2,6,197,384]{4,1,3,2,0:T(2,128)(2,1)} copy(bf16[1,2,6,197,384]{4,3,2,1,0:T(8,128)(2,1)S(1)} %bitcast.73) | data formatting | bytes 3631104
  155.8 1.8 %shard_map.256 = (f32[1,24,1536]{2,1,0:T(8,128)}, f32[1,24,1152]{2,1,0:T(8,128)}, f32[1,24,384]{2,1,0:T(8,128)}, f32[1,48]{1,0:T(1,128)}, f32[1,96]{1,0:T(1,128)...) custom-call(bf16[24,3200]{1,0:T(8,128)(2,1)} %get-tuple-element.136., ...), custom_call_target="tpu_custom_call" | custom-call | tf_op jit(solution)/shard_map/pallas_call | solution.py:716
  (47 shorter events, 7.1 us)
Async XLA Ops:
  0.6 7.6 %collective-permute-start.3 = (bf16[1,384,1536]{2,1,0:T(8,128)(2,1)}, bf16[1,384,1536]{2,1,0:T(8,128)(2,1)S(1)}, u32[]{:S(2)}, u32[]{:S(2)}) collective-permute-start(bf16[1,384,1536]{2,1,0:T(8,128)(2,1)} %refs_8_.1), channel_id=1, source_target_pairs={{0,16},{16,0},{1,17},{17,1},{2,18},{18,2},{3,19},{19,3},{4,20},{20... | collective-permute-start | bytes 3538952 | tf_op jit(solution)/shard_map/ppermute | solution.py:634
  1.2 8.1 %collective-permute-start.4 = (bf16[1,1536,384]{2,1,0:T(8,128)(2,1)}, bf16[1,1536,384]{2,1,0:T(8,128)(2,1)}, u32[]{:S(2)}, u32[]{:S(2)}) collective-permute-start(bf16[1,1536,384]{2,1,0:T(8,128)(2,1)} %refs_9_.1), channel_id=1, source_target_pairs={{0,16},{16,0},{1,17},{17,1},{2,18},{18,2},{3,19},{19,3},{4,20},{20... | collective-permute-start | bytes 3538952 | tf_op jit(solution)/shard_map/ppermute | solution.py:634
  1.2 7.0 %collective-permute-start.1 = (bf16[1,384,1152]{2,1,0:T(8,128)(2,1)}, bf16[1,384,1152]{2,1,0:T(8,128)(2,1)S(1)}, u32[]{:S(2)}, u32[]{:S(2)}) collective-permute-start(bf16[1,384,1152]{2,1,0:T(8,128)(2,1)} %refs_6_.3), channel_id=1, source_target_pairs={{0,16},{16,0},{1,17},{17,1},{2,18},{18,2},{3,19},{19,3},{4,20},{20... | collective-permute-start | bytes 2654216 | tf_op jit(solution)/shard_map/ppermute | solution.py:634
  1.7 6.5 %collective-permute-start.2 = (bf16[1,384,384]{2,1,0:T(8,128)(2,1)}, bf16[1,384,384]{2,1,0:T(8,128)(2,1)S(1)}, u32[]{:S(2)}, u32[]{:S(2)}) collective-permute-start(bf16[1,384,384]{2,1,0:T(8,128)(2,1)} %refs_7_.3), channel_id=1, source_target_pairs={{0,16},{16,0},{1,17},{17,1},{2,18},{18,2},{3,19},{19,3},{4,20},{20... | collective-permute-start | bytes 884744 | tf_op jit(solution)/shard_map/ppermute | solution.py:634
  3.2 5.0 %collective-permute-start = (f32[1,4992]{1,0:T(1,128)}, f32[1,4992]{1,0:T(1,128)S(1)}, u32[]{:S(2)}, u32[]{:S(2)}) collective-permute-start(f32[1,4992]{1,0:T(1,128)} %shard_map.254.refs_4_), channel_id=1, source_target_pairs={{0,16},{16,0},{1,17},{17,1},{2,18},{18,2},{3,19},{19,3},{4,20},{20... | collective-permute-start | bytes 59912 | tf_op jit(solution)/shard_map/ppermute | solution.py:634
  3.6 3.1 %copy-start.4 = (bf16[2,6,197,384]{3,0,2,1:T(2,128)(2,1)S(1)}, bf16[2,6,197,384]{3,0,2,1:T(2,128)(2,1)}, u32[]{:S(2)}) copy-start(bf16[2,6,197,384]{3,0,2,1:T(2,128)(2,1)} %param.17) | copy-start | bytes 5446660
  8.2 1.0 copy-start.10
  8.2 1.0 copy-start.9
  8.2 1.0 copy-start.8
  9.2 1.0 copy-start.7
  45.7 28.6 %collective-permute-start.5 = (bf16[384,3200]{1,0:T(8,128)(2,1)}, bf16[384,3200]{1,0:T(8,128)(2,1)S(1)}, u32[]{:S(2)}, u32[]{:S(2)}) collective-permute-start(bf16[384,3200]{1,0:T(8,128)(2,1)} %get-tuple-element.48), channel_id=1, source_target_pairs={{0,16},{16,0},{1,17},{17,1},{2,18},{18,2},{3,19},{19,3},{4,20},{20... | collective-permute-start | bytes 7372808 | tf_op jit(solution)/shard_map/ppermute | solution.py:634
  74.3 6.2 %collective-permute-start.6 = (bf16[1536,384]{1,0:T(8,128)(2,1)}, bf16[1536,384]{1,0:T(8,128)(2,1)S(1)}, u32[]{:S(2)}, u32[]{:S(2)}) collective-permute-start(bf16[1536,384]{1,0:T(8,128)(2,1)} %get-tuple-element.51), channel_id=1, source_target_pairs={{0,16},{16,0},{1,17},{17,1},{2,18},{18,2},{3,19},{19,3},{4,20},{20... | collective-permute-start | bytes 3538952 | tf_op jit(solution)/shard_map/ppermute | solution.py:634
  74.6 2.1 %copy-start = (bf16[384,3200]{1,0:T(8,128)(2,1)S(1)}, bf16[384,3200]{1,0:T(8,128)(2,1)}, u32[]{:S(2)}) copy-start(bf16[384,3200]{1,0:T(8,128)(2,1)} %get-tuple-element.54) | copy-start | bytes 7372804
  76.7 3.8 %copy-start.5 = (bf16[1536,384]{1,0:T(8,128)(2,1)S(1)}, bf16[1536,384]{1,0:T(8,128)(2,1)}, u32[]{:S(2)}) copy-start(bf16[1536,384]{1,0:T(8,128)(2,1)} %get-tuple-element.52) | copy-start | bytes 3538948
  77.5 40.9 %collective-permute-start.7 = (bf16[8,24,3200]{2,1,0:T(8,128)(2,1)S(1)}, bf16[8,24,3200]{2,1,0:T(8,128)(2,1)S(1)}, u32[]{:S(2)}, u32[]{:S(2)}) collective-permute-start(bf16[8,24,3200]{2,1,0:T(8,128)(2,1)S(1)} %add_convert_fusion.1), channel_id=1, source_target_pairs={{0,1},{1,0},{2,3},{3,2},{4,5},{5,4},{6,7},{7,6},{8,9},{9,8},{10,11... | collective-permute-start | bytes 3686408 | tf_op jit(solution)/shard_map/ppermute | solution.py:681
  80.5 27.9 %copy-start.3 = (bf16[2,6,197,384]{3,2,1,0:T(8,128)(2,1)S(1)}, bf16[2,6,197,384]{3,2,1,0:T(8,128)(2,1)}, u32[]{:S(2)}) copy-start(bf16[2,6,197,384]{3,2,1,0:T(8,128)(2,1)} %get-tuple-element.58) | copy-start | bytes 5446660
  81.7 42.0 %collective-permute-start.9 = (bf16[8,96,384]{2,1,0:T(8,128)(2,1)}, bf16[8,96,384]{2,1,0:T(8,128)(2,1)}, u32[]{:S(2)}, u32[]{:S(2)}) collective-permute-start(bf16[8,96,384]{2,1,0:T(8,128)(2,1)} %bitcast.12), channel_id=1, source_target_pairs={{0,2},{1,3},{2,0},{3,1},{4,6},{5,7},{6,4},{7,5},{8,10},{9,11},{10,... | collective-permute-start | bytes 1769480 | tf_op jit(solution)/shard_map/ppermute | solution.py:681
  109.8 3.8 %collective-permute-start.8 = (bf16[2,6,197,384]{3,0,2,1:T(2,128)(2,1)S(1)}, bf16[2,6,197,384]{3,0,2,1:T(2,128)(2,1)S(1)}, u32[]{:S(2)}, u32[]{:S(2)}) collective-permute-start(bf16[2,6,197,384]{3,0,2,1:T(2,128)(2,1)S(1)} %copy.39), channel_id=1, source_target_pairs={{0,16},{16,0},{1,17},{17,1},{2,18},{18,2},{3,19},{19,3},{4,20},{20... | collective-permute-start | bytes 5446664 | tf_op jit(solution)/shard_map/ppermute | solution.py:634
  113.7 2.5 %copy-start.2 = (bf16[2,6,197,384]{3,2,1,0:T(8,128)(2,1)S(1)}, bf16[2,6,197,384]{3,2,1,0:T(8,128)(2,1)}, u32[]{:S(2)}) copy-start(bf16[2,6,197,384]{3,2,1,0:T(8,128)(2,1)} %get-tuple-element.56) | copy-start | bytes 5446660
  119.5 12.6 %collective-permute-start.12 = (bf16[4,24,3200]{2,1,0:T(8,128)(2,1)}, bf16[4,24,3200]{2,1,0:T(8,128)(2,1)}, u32[]{:S(2)}, u32[]{:S(2)}) collective-permute-start(bf16[4,24,3200]{2,1,0:T(8,128)(2,1)} %get-tuple-element.125), channel_id=1, source_target_pairs={{0,2},{1,3},{2,0},{3,1},{4,6},{5,7},{6,4},{7,5},{8,10},{9,11},{10,... | collective-permute-start | bytes 1843208 | tf_op jit(solution)/shard_map/ppermute | solution.py:681
  125.6 10.0 %collective-permute-start.10 = (bf16[4,96,384]{2,1,0:T(8,128)(2,1)}, bf16[4,96,384]{2,1,0:T(8,128)(2,1)}, u32[]{:S(2)}, u32[]{:S(2)}) collective-permute-start(bf16[4,96,384]{2,1,0:T(8,128)(2,1)} %bitcast.23), channel_id=1, source_target_pairs={{0,4},{1,5},{2,6},{3,7},{4,0},{5,1},{6,2},{7,3},{8,12},{9,13},{10,... | collective-permute-start | bytes 884744 | tf_op jit(solution)/shard_map/ppermute | solution.py:681
  134.0 10.2 %collective-permute-start.13 = (bf16[2,24,3200]{2,1,0:T(8,128)(2,1)}, bf16[2,24,3200]{2,1,0:T(8,128)(2,1)S(1)}, u32[]{:S(2)}, u32[]{:S(2)}) collective-permute-start(bf16[2,24,3200]{2,1,0:T(8,128)(2,1)} %get-tuple-element.133), channel_id=1, source_target_pairs={{0,4},{1,5},{2,6},{3,7},{4,0},{5,1},{6,2},{7,3},{8,12},{9,13},{10,... | collective-permute-start | bytes 921608 | tf_op jit(solution)/shard_map/ppermute | solution.py:681
  136.7 8.3 %collective-permute-start.11 = (bf16[2,96,384]{2,1,0:T(8,128)(2,1)S(1)}, bf16[2,96,384]{2,1,0:T(8,128)(2,1)S(1)}, u32[]{:S(2)}, u32[]{:S(2)}) collective-permute-start(bf16[2,96,384]{2,1,0:T(8,128)(2,1)S(1)} %get-tuple-element.138), channel_id=1, source_target_pairs={{0,8},{1,9},{2,10},{3,11},{4,12},{5,13},{6,14},{7,15},{8,0},{9,1},... | collective-permute-start | bytes 442376 | tf_op jit(solution)/shard_map/ppermute | solution.py:681
  145.0 8.6 %collective-permute-start.15 = (bf16[1,96,384]{2,1,0:T(8,128)(2,1)S(1)}, bf16[1,96,384]{2,1,0:T(8,128)(2,1)S(1)}, u32[]{:S(2)}, u32[]{:S(2)}) collective-permute-start(bf16[1,96,384]{2,1,0:T(8,128)(2,1)S(1)} %add_convert_fusion.13), channel_id=1, source_target_pairs={{0,1},{1,0},{2,3},{3,2},{4,5},{5,4},{6,7},{7,6},{8,9},{9,8},{10,11... | collective-permute-start | bytes 221192 | tf_op jit(solution)/shard_map/ppermute | solution.py:681
  146.6 8.5 %collective-permute-start.14 = (bf16[1,24,3200]{2,1,0:T(8,128)(2,1)S(1)}, bf16[1,24,3200]{2,1,0:T(8,128)(2,1)S(1)}, u32[]{:S(2)}, u32[]{:S(2)}) collective-permute-start(bf16[1,24,3200]{2,1,0:T(8,128)(2,1)S(1)} %get-tuple-element.137), channel_id=1, source_target_pairs={{0,8},{1,9},{2,10},{3,11},{4,12},{5,13},{6,14},{7,15},{8,0},{9,1},... | collective-permute-start | bytes 460808 | tf_op jit(solution)/shard_map/ppermute | solution.py:681
  148.4 2.6 %copy-start.1 = (bf16[2,6,197,384]{3,2,1,0:T(8,128)(2,1)S(1)}, bf16[2,6,197,384]{3,2,1,0:T(8,128)(2,1)}, u32[]{:S(2)}) copy-start(bf16[2,6,197,384]{3,2,1,0:T(8,128)(2,1)} %pad_maximum_fusion.1) | copy-start | bytes 5446660
  155.1 0.7 copy-start.6

commit v8 on v7

--- a/solution.py
+++ b/solution.py
@@ -1,6 +1,7 @@
 import jax
 import jax.numpy as jnp
 from jax import lax
+from jax.experimental.layout import Layout, with_layout_constraint
 from jax.experimental import pallas as pl
 from jax.experimental.pallas import tpu as pltpu
 from jax.sharding import PartitionSpec as P
@@ -134,6 +135,7 @@
     tall,
     load_sem,
     store_sem,
+    clear_sem,
 ):
     step = pl.program_id(0)
     last = pl.num_programs(0) - 1
@@ -157,6 +159,11 @@
     def load(source, n, layer):
         return pltpu.make_async_copy(source[n].at[0], held[n].at[layer], load_sem.at[layer, n])
 
+    blank = [sum_up.at[1]] + [ref.at[layer] for ref in (sum_down, sum_att) for layer in range(2)]
+
+    def clear(n):
+        return pltpu.make_async_copy(sum_up.at[0], blank[n], clear_sem.at[n])
+
     @pl.when(step == 0)
     def _():
         for layer in range(2):
@@ -173,7 +180,10 @@
         for layer in range(2):
             mine = jnp.full(own_vec.shape, core == layer)
             vecs[layer : layer + 1] = jnp.where(mine, own_vec[...], got_vec[...])
-        for ref in (sum_up, sum_down, sum_att, vec_one, vec_up, vec_qkv):
+        sum_up[0] = jnp.zeros(sum_up.shape[1:], F32)
+        for n in range(len(blank)):
+            clear(n).start()
+        for ref in (vec_one, vec_up, vec_qkv):
             for layer in range(2):
                 ref[layer] = jnp.zeros(ref.shape[1:], F32)
         for layer in range(2):
@@ -500,6 +510,11 @@
             tail = slice(j * padded + padded - 16, (j + 1) * padded)
             grad_out[tail] = jnp.zeros((16, features), F32)
             grad_out[j * padded : j * padded + tokens] = cot_ref[0, j].astype(F32) * keep
+
+    @pl.when(step == 0)
+    def _():
+        for n in range(len(blank)):
+            clear(n).wait()
 
     def second_half(at, carry):
         layer = 1 - at
@@ -587,6 +602,7 @@
         ]
         + two(sums)
         + [pltpu.SemaphoreType.DMA((2, 4)), pltpu.SemaphoreType.DMA((2, 2))]
+        + [pltpu.SemaphoreType.DMA((5,))]
     )
     return pl.pallas_call(
         lambda *refs: layers_kernel(padded, keys, *refs),
@@ -752,16 +768,22 @@
             wide.wait_for(tall_send)
             away, _ = lax.optimization_barrier((away, tall_send))
             got = swap_cores(away)
+            here = (lax.iota(jnp.int32, 2) == core)[:, None, None, None]
+            straight = Layout(major_to_minor=(0, 1, 2, 3))
             both = [
-                jnp.stack([jnp.where(first, a, b), jnp.where(first, b, a)])
+                with_layout_constraint(jnp.where(here, a[None], b[None]), straight)
                 for a, b in zip(mine, got)
             ]
         wide.exchange(n, wide_send)
         tall.exchange(n, tall_send)
-        if n == 0:
+        if n == 1:
+            both = [
+                with_layout_constraint(b.transpose(1, 2, 0, 3), straight) for b in both
+            ]
+        if n < 2:
             keep, arrived, *both = lax.optimization_barrier(wide.terms + tuple(both))
             wide.terms = (keep, arrived)
-    *both, _ = lax.optimization_barrier((*both, tall_send))
+    both = [b.transpose(2, 0, 1, 3) for b in both]
     wide, tall = wide.result(), tall.result()
     g_up, g_qkv, g_out, g_bqv, g_bup, *vectors = split_wide(wide, features, units)
     ln1_gain, ln1_bias, g_bo, ln2_gain, ln2_bias, g_bd = vectors

time: 158 us -> 156 us (0.987)
  starting transfers between devices: 69.6 us -> 15.3 us
  Pallas kernels: 38.6 us -> 88.1 us
  waiting for transfers between devices: 17.5 us -> 20 us
  local copies, waits for them, and re-layouts: 18.7 us -> 20.5 us
    pallas_call x1, Pallas kernels: 35.4 us -> 84.9 us  [run_layers(): pl.pallas_call(lambda *refs: layers_kernel(padded, keys, *refs), grid_spe...]
    ppermute x8, starting transfers between devices: 43.5 us -> 13.4 us  [exchange(): self.terms = (keep, lax.ppermute(send, ('segment', 'dp'), route))]
    ppermute x8, starting transfers between devices: 26.1 us -> 1.95 us  [swap_cores(): return lax.ppermute(block, 'segment', [(0, 1), (1, 0)])]
    optimization_barrier x0 -> x2, local copies, waits for them, and re-layouts: none -> 6.75 us  [on_device(): keep, arrived, *both = lax.optimization_barrier(wide.terms + tuple(both))]
    unnamed x26 -> x24, local copies, waits for them, and re-layouts: 12.9 us -> 7.63 us
    ppermute x8, waiting for transfers between devices: 10.2 us -> 14.3 us  [exchange(): self.terms = (keep, lax.ppermute(send, ('segment', 'dp'), route))]
    broadcast_in_dim x0 -> x1, local copies, waits for them, and re-layouts: none -> 1.8 us  [on_device(): jnp.where(here, a[None], b[None])]
    another operation x2 -> x0, other arithmetic: 1.67 us -> none  [on_device(): jnp.stack([jnp.where(first, a, b), jnp.where(first, b, a)])]
  transfers between devices with their start and end apart: 16 -> 16, of which waited for: 5 -> 6; matrix products, arithmetic and copies ran while one was open for 18% -> 19% of each run, Pallas kernels for 1% -> 1%
where the time goes in v8:
time: 156 us
  Pallas kernels  88.1 us (56%)
  local copies, waits for them, and re-layouts  20.5 us (13%)
  waiting for transfers between devices  20 us (13%)
  starting transfers between devices  15.3 us (10%)
  other arithmetic  11.4 us (7%)
    pallas_call x1, Pallas kernels, run_layers(): pl.pallas_call(lambda *refs: layers_kernel(padded, keys, *refs), grid_spe...  84.9 us
    ppermute x8, waiting for transfers between devices, exchange(): self.terms = (keep, lax.ppermute(send, ('segment', 'dp'), route))  14.3 us
    ppermute x8, starting transfers between devices, exchange(): self.terms = (keep, lax.ppermute(send, ('segment', 'dp'), route))  13.4 us
    convert_element_type x9, other arithmetic, half(): return sum((part.astype(F32) for part in taken)).astype(BF16)  8.89 us
    unnamed x24, local copies, waits for them, and re-layouts  7.63 us
    optimization_barrier x2, local copies, waits for them, and re-layouts, on_device(): keep, arrived, *both = lax.optimization_barrier(wide.terms + tuple(both))  6.75 us
    ppermute x8, waiting for transfers between devices, swap_cores(): return lax.ppermute(block, 'segment', [(0, 1), (1, 0)])  5.67 us
  transfers between devices with their start and end apart: 16, of which 6 were waited for; matrix products, arithmetic and copies ran while one was open for 19% of the time, Pallas kernels for 1%

profile of v8, /device:TPU:0, one launch (start us, length us, event | category | flops | bytes accessed | tf_op | source)
XLA Modules:
  0.0 156.2 jit_solution(13491319008067667645)
XLA Ops:
  1.8 1.4 shard_map.254.refs_4_
  3.6 3.2 %copy.42.refs_2_ = bf16[2,6,197,384]{3,2,1,0:T(8,128)(2,1)} copy(bf16[2,6,197,384]{3,0,2,1:T(2,128)(2,1)} %param.15) | data formatting | bytes 3631104 | tf_op args[0]
  6.8 1.5 copy.43.refs_3_
  8.3 1.0 copy-done.7
  9.3 1.0 copy-done.6
  10.3 84.9 %shard_map.255 = (bf16[2,6,197,384]{3,2,1,0:T(8,128)(2,1)}, bf16[2,6,197,384]{3,2,1,0:T(8,128)(2,1)}, bf16[384,3200]{1,0:T(8,128)(2,1)}, bf16[384,3200]{1,0:T(8,...) custom-call(s32[2]{0:T(128)} %bitcast.105, s32[1]{0:T(128)} %bitcast.1.refs_1_, ...), custom_call_target="tpu_custom_call" | custom-call | flops 80000000000 | bytes 30000000 | tf_op jit(solution)/shard_map/pallas_call | solution.py:607
  95.4 1.8 %slice_bitcast_fusion = (bf16[6,197,384]{2,1,0:T(8,128)(2,1)S(1)}, bf16[6,197,384]{2,1,0:T(8,128)(2,1)S(1)}) fusion(bf16[2,6,197,384]{3,2,1,0:T(8,128)(2,1)} %get-tuple-element.58), kind=kLoop, calls=%fused_computation.16 | loop fusion | bytes 3631104 | tf_op jit(solution)/shard_map/jit(_where)/broadcast_in_dim | solution.py:774
  97.2 2.9 %collective-permute-done.5 = bf16[384,3200]{1,0:T(8,128)(2,1)S(1)} collective-permute-done((bf16[384,3200]{1,0:T(8,128)(2,1)}, bf16[384,3200]{1,0:T(8,128)(2,1)S(1)}, u32[]{:S(2)}, u32[]{:S(2)}) %collective-permute-start.5) | collective-permute-done | bytes 2457632 | tf_op jit(solution)/shard_map/ppermute | solution.py:650
  100.5 0.8 add_convert_fusion.1
  101.3 3.0 %collective-permute-start.7 = (bf16[8,24,3200]{2,1,0:T(8,128)(2,1)S(1)}, bf16[8,24,3200]{2,1,0:T(8,128)(2,1)S(1)}, u32[]{:S(2)}, u32[]{:S(2)}) collective-permute-start(bf16[8,24,3200]{2,1,0:T(8,128)(2,1)S(1)} %add_convert_fusion.1), channel_id=1, source_target_pairs={{0,1},{1,0},{2,3},{3,2},{4,5},{5,4},{6,7},{7,6},{8,9},{9,8},{10,11... | collective-permute-start | bytes 3686408 | tf_op jit(solution)/shard_map/ppermute | solution.py:697
  104.3 1.1 add_convert_fusion.4
  105.5 1.5 collective-permute-start.12
  107.0 1.4 copy.44
  108.7 0.8 add_convert_fusion
  109.5 2.7 %collective-permute-done.8 = bf16[2,6,197,384]{3,0,2,1:T(2,128)(2,1)S(1)} collective-permute-done((bf16[2,6,197,384]{3,0,2,1:T(2,128)(2,1)S(1)}, bf16[2,6,197,384]{3,0,2,1:T(2,128)(2,1)S(1)}, u32[]{:S(2)}, u32[]{:S(2)}) %collective-permute-start.8) | collective-permute-done | bytes 1815584 | tf_op jit(solution)/shard_map/ppermute | solution.py:650
  112.2 2.5 %fusion.8 = (bf16[1,6,197,384]{3,0,2,1:T(2,128)(2,1)S(1)}, bf16[1,6,197,384]{3,0,2,1:T(2,128)(2,1)S(1)}) fusion(bf16[2,6,197,384]{3,0,2,1:T(2,128)(2,1)S(1)} %collective-permute-done.8), kind=kLoop, calls=%fused_computation.42 | loop fusion | bytes 3631104 | tf_op jit(solution)/shard_map/unstack | solution.py:775
  115.1 1.9 %broadcast_select_fusion = (bf16[2,6,197,384]{3,2,1,0:T(8,128)(2,1)S(1)}, bf16[2,6,197,384]{3,2,1,0:T(8,128)(2,1)}) fusion(pred[2]{0:T(512)(128)(4,1)S(1)} %iota_compare_fusion, bf16[6,197,384]{2,1,0:T(8,128)(2,1)S(1)} %bitcast.95, bf16[6,197,384]{2,1,0:T(8,128)(2,1)S(1)} %get-tuple-element.86, bf16[6,197,384]{2,1,0:T(8,128)(2,1)S(1)} %bitcast.96, ...), kind=kLoop, calls=%fused_computation.2 | loop fusion | flops 1815552 | bytes 7262210 | tf_op jit(solution)/shard_map/jit(_where)/select_n | solution.py:774
  116.9 2.1 %collective-permute-done.7 = bf16[8,24,3200]{2,1,0:T(8,128)(2,1)S(1)} collective-permute-done((bf16[8,24,3200]{2,1,0:T(8,128)(2,1)S(1)}, bf16[8,24,3200]{2,1,0:T(8,128)(2,1)S(1)}, u32[]{:S(2)}, u32[]{:S(2)}) %collective-permute-start.7) | collective-permute-done | bytes 1228832 | tf_op jit(solution)/shard_map/ppermute | solution.py:697
  119.0 1.2 fusion.1
  120.2 1.5 collective-permute-start.9
  121.7 1.9 %add_convert_fusion.9 = (bf16[2,1,2,96,384]{4,3,2,1,0:T(8,128)(2,1)S(1)}, bf16[2,1,2,96,384]{4,3,2,1,0:T(8,128)(2,1)}) fusion(bf16[2,2,2,96,384]{4,3,2,1,0:T(8,128)(2,1)} %bitcast.43, s32[]{:T(128)S(6)} %select_n.126, bf16[2,2,2,96,384]{4,3,2,1,0:T(8,128)(2,1)S(1)} %bitcast.98, s32[]{:T(128)S(6)} %select_n.121), kind=kLoop, calls=%fused_computation.23 | loop fusion | flops 1179648 | bytes 1769480 | tf_op jit(solution)/shard_map/convert_element_type | solution.py:688
  123.6 2.1 %collective-permute-start.13 = (bf16[4,96,384]{2,1,0:T(8,128)(2,1)}, bf16[4,96,384]{2,1,0:T(8,128)(2,1)}, u32[]{:S(2)}, u32[]{:S(2)}) collective-permute-start(bf16[4,96,384]{2,1,0:T(8,128)(2,1)} %bitcast.44), channel_id=1, source_target_pairs={{0,4},{1,5},{2,6},{3,7},{4,0},{5,1},{6,2},{7,3},{8,12},{9,13},{10,... | collective-permute-start | bytes 884744 | tf_op jit(solution)/shard_map/ppermute | solution.py:697
  125.7 4.1 %copy.56 = bf16[2,6,197,384]{3,0,2,1:T(2,128)(2,1)} copy(bf16[2,6,197,384]{3,2,1,0:T(8,128)(2,1)} %get-tuple-element.63) | data formatting | bytes 3631104 | tf_op jit(solution)/shard_map/optimization_barrier | solution.py:784
  129.8 2.6 %copy.55 = bf16[2,6,197,384]{3,0,2,1:T(2,128)(2,1)} copy(bf16[2,6,197,384]{3,2,1,0:T(8,128)(2,1)S(1)} %get-tuple-element.64) | data formatting | bytes 3631104 | tf_op jit(solution)/shard_map/optimization_barrier | solution.py:784
  132.5 1.2 add_convert_fusion.7
  133.8 1.1 fusion.7
  134.8 2.9 %collective-permute-start.14 = (bf16[2,96,384]{2,1,0:T(8,128)(2,1)S(1)}, bf16[2,96,384]{2,1,0:T(8,128)(2,1)S(1)}, u32[]{:S(2)}, u32[]{:S(2)}) collective-permute-start(bf16[2,96,384]{2,1,0:T(8,128)(2,1)S(1)} %get-tuple-element.96), channel_id=1, source_target_pairs={{0,8},{1,9},{2,10},{3,11},{4,12},{5,13},{6,14},{7,15},{8,0},{9,1},... | collective-permute-start | bytes 442376 | tf_op jit(solution)/shard_map/ppermute | solution.py:697
  137.8 6.0 %collective-permute-done.10 = bf16[2,24,3200]{2,1,0:T(8,128)(2,1)S(1)} collective-permute-done((bf16[2,24,3200]{2,1,0:T(8,128)(2,1)S(1)}, bf16[2,24,3200]{2,1,0:T(8,128)(2,1)S(1)}, u32[]{:S(2)}, u32[]{:S(2)}) %collective-permute-start.10) | collective-permute-done | bytes 307232 | tf_op jit(solution)/shard_map/ppermute | solution.py:697
  144.5 1.6 collective-permute-start.15
  146.8 2.1 %collective-permute-done.15 = bf16[1,96,384]{2,1,0:T(8,128)(2,1)S(1)} collective-permute-done((bf16[1,96,384]{2,1,0:T(8,128)(2,1)S(1)}, bf16[1,96,384]{2,1,0:T(8,128)(2,1)S(1)}, u32[]{:S(2)}, u32[]{:S(2)}) %collective-permute-start.15) | collective-permute-done | bytes 73760 | tf_op jit(solution)/shard_map/ppermute | solution.py:697
  149.6 4.0 %collective-permute-done.11 = bf16[1,24,3200]{2,1,0:T(8,128)(2,1)S(1)} collective-permute-done((bf16[1,24,3200]{2,1,0:T(8,128)(2,1)S(1)}, bf16[1,24,3200]{2,1,0:T(8,128)(2,1)S(1)}, u32[]{:S(2)}, u32[]{:S(2)}) %collective-permute-start.11) | collective-permute-done | bytes 153632 | tf_op jit(solution)/shard_map/ppermute | solution.py:697
  154.3 1.8 %shard_map.256 = (f32[1,24,1536]{2,1,0:T(8,128)}, f32[1,24,1152]{2,1,0:T(8,128)}, f32[1,24,384]{2,1,0:T(8,128)}, f32[1,48]{1,0:T(1,128)}, f32[1,96]{1,0:T(1,128)...) custom-call(bf16[24,3200]{1,0:T(8,128)(2,1)} %get-tuple-element.95.o, ...), custom_call_target="tpu_custom_call" | custom-call | tf_op jit(solution)/shard_map/pallas_call | solution.py:732
  (47 shorter events, 5.7 us)
Async XLA Ops:
  0.6 7.7 %collective-permute-start.3 = (bf16[1,384,1536]{2,1,0:T(8,128)(2,1)}, bf16[1,384,1536]{2,1,0:T(8,128)(2,1)S(1)}, u32[]{:S(2)}, u32[]{:S(2)}) collective-permute-start(bf16[1,384,1536]{2,1,0:T(8,128)(2,1)} %refs_8_.1), channel_id=1, source_target_pairs={{0,16},{16,0},{1,17},{17,1},{2,18},{18,2},{3,19},{19,3},{4,20},{20... | collective-permute-start | bytes 3538952 | tf_op jit(solution)/shard_map/ppermute | solution.py:650
  1.2 8.1 %collective-permute-start.4 = (bf16[1,1536,384]{2,1,0:T(8,128)(2,1)}, bf16[1,1536,384]{2,1,0:T(8,128)(2,1)}, u32[]{:S(2)}, u32[]{:S(2)}) collective-permute-start(bf16[1,1536,384]{2,1,0:T(8,128)(2,1)} %refs_9_.1), channel_id=1, source_target_pairs={{0,16},{16,0},{1,17},{17,1},{2,18},{18,2},{3,19},{19,3},{4,20},{20... | collective-permute-start | bytes 3538952 | tf_op jit(solution)/shard_map/ppermute | solution.py:650
  1.2 7.0 %collective-permute-start.1 = (bf16[1,384,1152]{2,1,0:T(8,128)(2,1)}, bf16[1,384,1152]{2,1,0:T(8,128)(2,1)S(1)}, u32[]{:S(2)}, u32[]{:S(2)}) collective-permute-start(bf16[1,384,1152]{2,1,0:T(8,128)(2,1)} %refs_6_.3), channel_id=1, source_target_pairs={{0,16},{16,0},{1,17},{17,1},{2,18},{18,2},{3,19},{19,3},{4,20},{20... | collective-permute-start | bytes 2654216 | tf_op jit(solution)/shard_map/ppermute | solution.py:650
  1.7 6.6 %collective-permute-start.2 = (bf16[1,384,384]{2,1,0:T(8,128)(2,1)}, bf16[1,384,384]{2,1,0:T(8,128)(2,1)S(1)}, u32[]{:S(2)}, u32[]{:S(2)}) collective-permute-start(bf16[1,384,384]{2,1,0:T(8,128)(2,1)} %refs_7_.3), channel_id=1, source_target_pairs={{0,16},{16,0},{1,17},{17,1},{2,18},{18,2},{3,19},{19,3},{4,20},{20... | collective-permute-start | bytes 884744 | tf_op jit(solution)/shard_map/ppermute | solution.py:650
  3.2 5.1 %collective-permute-start = (f32[1,4992]{1,0:T(1,128)}, f32[1,4992]{1,0:T(1,128)S(1)}, u32[]{:S(2)}, u32[]{:S(2)}) collective-permute-start(f32[1,4992]{1,0:T(1,128)} %shard_map.254.refs_4_), channel_id=1, source_target_pairs={{0,16},{16,0},{1,17},{17,1},{2,18},{18,2},{3,19},{19,3},{4,20},{20... | collective-permute-start | bytes 59912 | tf_op jit(solution)/shard_map/ppermute | solution.py:650
  3.6 3.2 %copy-start.2 = (bf16[2,6,197,384]{3,0,2,1:T(2,128)(2,1)S(1)}, bf16[2,6,197,384]{3,0,2,1:T(2,128)(2,1)}, u32[]{:S(2)}) copy-start(bf16[2,6,197,384]{3,0,2,1:T(2,128)(2,1)} %param.17) | copy-start | bytes 5446660
  8.3 1.0 copy-start.9
  8.3 1.0 copy-start.8
  8.3 1.0 copy-start.7
  9.3 1.0 copy-start.6
  95.2 5.0 %collective-permute-start.5 = (bf16[384,3200]{1,0:T(8,128)(2,1)}, bf16[384,3200]{1,0:T(8,128)(2,1)S(1)}, u32[]{:S(2)}, u32[]{:S(2)}) collective-permute-start(bf16[384,3200]{1,0:T(8,128)(2,1)} %get-tuple-element.50), channel_id=1, source_target_pairs={{0,16},{16,0},{1,17},{17,1},{2,18},{18,2},{3,19},{19,3},{4,20},{20... | collective-permute-start | bytes 7372808 | tf_op jit(solution)/shard_map/ppermute | solution.py:650
  95.4 4.7 %copy-start.5 = (bf16[1536,384]{1,0:T(8,128)(2,1)S(1)}, bf16[1536,384]{1,0:T(8,128)(2,1)}, u32[]{:S(2)}) copy-start(bf16[1536,384]{1,0:T(8,128)(2,1)} %get-tuple-element.53) | copy-start | bytes 3538948
  95.4 4.9 %copy-start = (bf16[384,3200]{1,0:T(8,128)(2,1)S(1)}, bf16[384,3200]{1,0:T(8,128)(2,1)}, u32[]{:S(2)}) copy-start(bf16[384,3200]{1,0:T(8,128)(2,1)} %get-tuple-element.56) | copy-start | bytes 7372804
  100.1 4.2 %collective-permute-start.6 = (bf16[1536,384]{1,0:T(8,128)(2,1)S(1)}, bf16[1536,384]{1,0:T(8,128)(2,1)S(1)}, u32[]{:S(2)}, u32[]{:S(2)}) collective-permute-start(bf16[1536,384]{1,0:T(8,128)(2,1)S(1)} %copy-done.5), channel_id=1, source_target_pairs={{0,16},{16,0},{1,17},{17,1},{2,18},{18,2},{3,19},{19,3},{4,20},{20... | collective-permute-start | bytes 3538952 | tf_op jit(solution)/shard_map/ppermute | solution.py:650
  100.5 3.8 %copy-start.3 = (bf16[1536,384]{1,0:T(8,128)(2,1)S(1)}, bf16[1536,384]{1,0:T(8,128)(2,1)}, u32[]{:S(2)}) copy-start(bf16[1536,384]{1,0:T(8,128)(2,1)} %get-tuple-element.54) | copy-start | bytes 3538948
  101.3 17.7 %collective-permute-start.7 = (bf16[8,24,3200]{2,1,0:T(8,128)(2,1)S(1)}, bf16[8,24,3200]{2,1,0:T(8,128)(2,1)S(1)}, u32[]{:S(2)}, u32[]{:S(2)}) collective-permute-start(bf16[8,24,3200]{2,1,0:T(8,128)(2,1)S(1)} %add_convert_fusion.1), channel_id=1, source_target_pairs={{0,1},{1,0},{2,3},{3,2},{4,5},{5,4},{6,7},{7,6},{8,9},{9,8},{10,11... | collective-permute-start | bytes 3686408 | tf_op jit(solution)/shard_map/ppermute | solution.py:697
  104.3 2.7 %copy-start.1 = (bf16[2,6,197,384]{3,2,1,0:T(8,128)(2,1)S(1)}, bf16[2,6,197,384]{3,2,1,0:T(8,128)(2,1)}, u32[]{:S(2)}) copy-start(bf16[2,6,197,384]{3,2,1,0:T(8,128)(2,1)} %get-tuple-element.60) | copy-start | bytes 5446660
  105.5 16.2 %collective-permute-start.12 = (bf16[8,96,384]{2,1,0:T(8,128)(2,1)}, bf16[8,96,384]{2,1,0:T(8,128)(2,1)}, u32[]{:S(2)}, u32[]{:S(2)}) collective-permute-start(bf16[8,96,384]{2,1,0:T(8,128)(2,1)} %bitcast.12), channel_id=1, source_target_pairs={{0,2},{1,3},{2,0},{3,1},{4,6},{5,7},{6,4},{7,5},{8,10},{9,11},{10,... | collective-permute-start | bytes 1769480 | tf_op jit(solution)/shard_map/ppermute | solution.py:697
  108.4 3.8 %collective-permute-start.8 = (bf16[2,6,197,384]{3,0,2,1:T(2,128)(2,1)S(1)}, bf16[2,6,197,384]{3,0,2,1:T(2,128)(2,1)S(1)}, u32[]{:S(2)}, u32[]{:S(2)}) collective-permute-start(bf16[2,6,197,384]{3,0,2,1:T(2,128)(2,1)S(1)} %copy.44), channel_id=1, source_target_pairs={{0,16},{16,0},{1,17},{17,1},{2,18},{18,2},{3,19},{19,3},{4,20},{20... | collective-permute-start | bytes 5446664 | tf_op jit(solution)/shard_map/ppermute | solution.py:650
  120.2 12.3 %collective-permute-start.9 = (bf16[4,24,3200]{2,1,0:T(8,128)(2,1)}, bf16[4,24,3200]{2,1,0:T(8,128)(2,1)}, u32[]{:S(2)}, u32[]{:S(2)}) collective-permute-start(bf16[4,24,3200]{2,1,0:T(8,128)(2,1)} %get-tuple-element.82), channel_id=1, source_target_pairs={{0,2},{1,3},{2,0},{3,1},{4,6},{5,7},{6,4},{7,5},{8,10},{9,11},{10,... | collective-permute-start | bytes 1843208 | tf_op jit(solution)/shard_map/ppermute | solution.py:697
  123.6 10.2 %collective-permute-start.13 = (bf16[4,96,384]{2,1,0:T(8,128)(2,1)}, bf16[4,96,384]{2,1,0:T(8,128)(2,1)}, u32[]{:S(2)}, u32[]{:S(2)}) collective-permute-start(bf16[4,96,384]{2,1,0:T(8,128)(2,1)} %bitcast.44), channel_id=1, source_target_pairs={{0,4},{1,5},{2,6},{3,7},{4,0},{5,1},{6,2},{7,3},{8,12},{9,13},{10,... | collective-permute-start | bytes 884744 | tf_op jit(solution)/shard_map/ppermute | solution.py:697
  133.7 10.1 %collective-permute-start.10 = (bf16[2,24,3200]{2,1,0:T(8,128)(2,1)S(1)}, bf16[2,24,3200]{2,1,0:T(8,128)(2,1)S(1)}, u32[]{:S(2)}, u32[]{:S(2)}) collective-permute-start(bf16[2,24,3200]{2,1,0:T(8,128)(2,1)S(1)} %get-tuple-element.91), channel_id=1, source_target_pairs={{0,4},{1,5},{2,6},{3,7},{4,0},{5,1},{6,2},{7,3},{8,12},{9,13},{10,... | collective-permute-start | bytes 921608 | tf_op jit(solution)/shard_map/ppermute | solution.py:697
  134.8 9.7 %collective-permute-start.14 = (bf16[2,96,384]{2,1,0:T(8,128)(2,1)S(1)}, bf16[2,96,384]{2,1,0:T(8,128)(2,1)S(1)}, u32[]{:S(2)}, u32[]{:S(2)}) collective-permute-start(bf16[2,96,384]{2,1,0:T(8,128)(2,1)S(1)} %get-tuple-element.96), channel_id=1, source_target_pairs={{0,8},{1,9},{2,10},{3,11},{4,12},{5,13},{6,14},{7,15},{8,0},{9,1},... | collective-permute-start | bytes 442376 | tf_op jit(solution)/shard_map/ppermute | solution.py:697
  144.5 4.4 %collective-permute-start.15 = (bf16[1,96,384]{2,1,0:T(8,128)(2,1)S(1)}, bf16[1,96,384]{2,1,0:T(8,128)(2,1)S(1)}, u32[]{:S(2)}, u32[]{:S(2)}) collective-permute-start(bf16[1,96,384]{2,1,0:T(8,128)(2,1)S(1)} %add_convert_fusion.12), channel_id=1, source_target_pairs={{0,1},{1,0},{2,3},{3,2},{4,5},{5,4},{6,7},{7,6},{8,9},{9,8},{10,11... | collective-permute-start | bytes 221192 | tf_op jit(solution)/shard_map/ppermute | solution.py:697
  146.1 7.6 %collective-permute-start.11 = (bf16[1,24,3200]{2,1,0:T(8,128)(2,1)S(1)}, bf16[1,24,3200]{2,1,0:T(8,128)(2,1)S(1)}, u32[]{:S(2)}, u32[]{:S(2)}) collective-permute-start(bf16[1,24,3200]{2,1,0:T(8,128)(2,1)S(1)} %get-tuple-element.94), channel_id=1, source_target_pairs={{0,8},{1,9},{2,10},{3,11},{4,12},{5,13},{6,14},{7,15},{8,0},{9,1},... | collective-permute-start | bytes 460808 | tf_op jit(solution)/shard_map/ppermute | solution.py:697
  153.6 0.7 copy-start.4

commit v9 on v7

--- a/solution.py
+++ b/solution.py
@@ -1,6 +1,7 @@
 import jax
 import jax.numpy as jnp
 from jax import lax
+from jax.experimental.layout import Layout, with_layout_constraint
 from jax.experimental import pallas as pl
 from jax.experimental.pallas import tpu as pltpu
 from jax.sharding import PartitionSpec as P
@@ -738,7 +739,9 @@
     got_tall = swap_cores(away_tall)
     bits = list(range(dp.bit_length() - 1))
     near, far = bits[:3], bits[3:]
-    plain, turned, crossed = near + far, near[2:] + near[:2] + far, near[1:] + far + near[:1]
+    plain = near[:1] + near[2:] + near[1:2] + far
+    turned = near[2:] + near[1:2] + near[:1] + far
+    crossed = near[1:2] + near[:1] + far + near[2:]
     wide = Shards(mine_wide, got_wide, (plain, turned), first)
     tall = Shards(mine_tall, got_tall, (crossed, crossed), first)
     for n in bits:
@@ -752,16 +755,22 @@
             wide.wait_for(tall_send)
             away, _ = lax.optimization_barrier((away, tall_send))
             got = swap_cores(away)
+            here = (lax.iota(jnp.int32, 2) == core)[:, None, None, None]
+            straight = Layout(major_to_minor=(0, 1, 2, 3))
             both = [
-                jnp.stack([jnp.where(first, a, b), jnp.where(first, b, a)])
+                with_layout_constraint(jnp.where(here, a[None], b[None]), straight)
                 for a, b in zip(mine, got)
             ]
         wide.exchange(n, wide_send)
         tall.exchange(n, tall_send)
-        if n == 0:
+        if n == 1:
+            both = [
+                with_layout_constraint(b.transpose(1, 2, 0, 3), straight) for b in both
+            ]
+        if n < 2:
             keep, arrived, *both = lax.optimization_barrier(wide.terms + tuple(both))
             wide.terms = (keep, arrived)
-    *both, _ = lax.optimization_barrier((*both, tall_send))
+    both = [b.transpose(2, 0, 1, 3) for b in both]
     wide, tall = wide.result(), tall.result()
     g_up, g_qkv, g_out, g_bqv, g_bup, *vectors = split_wide(wide, features, units)
     ln1_gain, ln1_bias, g_bo, ln2_gain, ln2_bias, g_bd = vectors

time: 158 us -> 157 us (level)
  starting transfers between devices: 69.6 us -> 18 us
  Pallas kernels: 38.6 us -> 87.8 us
  local copies, waits for them, and re-layouts: 18.7 us -> 20.5 us
    pallas_call x1, Pallas kernels: 35.4 us -> 84.6 us  [run_layers(): pl.pallas_call(lambda *refs: layers_kernel(padded, keys, *refs), grid_spe...]
    ppermute x8, starting transfers between devices: 43.5 us -> 16.2 us  [exchange(): self.terms = (keep, lax.ppermute(send, ('segment', 'dp'), route))]
    ppermute x8, starting transfers between devices: 26.1 us -> 1.82 us  [swap_cores(): return lax.ppermute(block, 'segment', [(0, 1), (1, 0)])]
    optimization_barrier x0 -> x2, local copies, waits for them, and re-layouts: none -> 6.75 us  [on_device(): keep, arrived, *both = lax.optimization_barrier(wide.terms + tuple(both))]
    unnamed x26 -> x24, local copies, waits for them, and re-layouts: 12.9 us -> 7.63 us
    broadcast_in_dim x0 -> x1, local copies, waits for them, and re-layouts: none -> 1.8 us  [on_device(): jnp.where(here, a[None], b[None])]
    another operation x2 -> x0, other arithmetic: 1.67 us -> none  [on_device(): jnp.stack([jnp.where(first, a, b), jnp.where(first, b, a)])]
    ppermute x8, waiting for transfers between devices: 10.2 us -> 11.9 us  [exchange(): self.terms = (keep, lax.ppermute(send, ('segment', 'dp'), route))]
  transfers between devices with their start and end apart: 16 -> 16, of which waited for: 5 -> 7; matrix products, arithmetic and copies ran while one was open for 18% -> 19% of each run, Pallas kernels for 1% -> 1%
where the time goes in v9:
time: 157 us; the launch traced here: 156 us
  Pallas kernels  87.8 us (56%)
  local copies, waits for them, and re-layouts  20.5 us (13%)
  starting transfers between devices  18 us (11%)
  waiting for transfers between devices  17.7 us (11%)
  other arithmetic  11.4 us (7%)
    pallas_call x1, Pallas kernels, run_layers(): pl.pallas_call(lambda *refs: layers_kernel(padded, keys, *refs), grid_spe...  84.6 us
    ppermute x8, starting transfers between devices, exchange(): self.terms = (keep, lax.ppermute(send, ('segment', 'dp'), route))  16.2 us
    ppermute x8, waiting for transfers between devices, exchange(): self.terms = (keep, lax.ppermute(send, ('segment', 'dp'), route))  11.9 us
    convert_element_type x9, other arithmetic, half(): return sum((part.astype(F32) for part in taken)).astype(BF16)  8.87 us
    unnamed x24, local copies, waits for them, and re-layouts  7.63 us
    optimization_barrier x2, local copies, waits for them, and re-layouts, on_device(): keep, arrived, *both = lax.optimization_barrier(wide.terms + tuple(both))  6.75 us
    ppermute x8, waiting for transfers between devices, swap_cores(): return lax.ppermute(block, 'segment', [(0, 1), (1, 0)])  5.75 us
  transfers between devices with their start and end apart: 16, of which 7 were waited for; matrix products, arithmetic and copies ran while one was open for 19% of the time, Pallas kernels for 1%

profile of v9, /device:TPU:0, one launch (start us, length us, event | category | flops | bytes accessed | tf_op | source)
XLA Modules:
  0.0 156.3 jit_solution(16258135083843785016)
XLA Ops:
  1.8 1.4 shard_map.254.refs_4_
  3.6 3.2 %copy.42.refs_2_ = bf16[2,6,197,384]{3,2,1,0:T(8,128)(2,1)} copy(bf16[2,6,197,384]{3,0,2,1:T(2,128)(2,1)} %param.15) | data formatting | bytes 3631104 | tf_op args[0]
  6.8 1.5 copy.43.refs_3_
  8.3 1.0 copy-done.7
  9.3 1.0 copy-done.6
  10.3 84.6 %shard_map.255 = (bf16[2,6,197,384]{3,2,1,0:T(8,128)(2,1)}, bf16[2,6,197,384]{3,2,1,0:T(8,128)(2,1)}, bf16[384,3200]{1,0:T(8,128)(2,1)}, bf16[384,3200]{1,0:T(8,...) custom-call(s32[2]{0:T(128)} %bitcast.104, s32[1]{0:T(128)} %bitcast.1.refs_1_, ...), custom_call_target="tpu_custom_call" | custom-call | flops 80000000000 | bytes 30000000 | tf_op jit(solution)/shard_map/pallas_call | solution.py:592
  95.0 1.8 %slice_bitcast_fusion = (bf16[6,197,384]{2,1,0:T(8,128)(2,1)S(1)}, bf16[6,197,384]{2,1,0:T(8,128)(2,1)S(1)}) fusion(bf16[2,6,197,384]{3,2,1,0:T(8,128)(2,1)} %get-tuple-element.58), kind=kLoop, calls=%fused_computation.16 | loop fusion | bytes 3631104 | tf_op jit(solution)/shard_map/jit(_where)/broadcast_in_dim | solution.py:761
  96.8 3.0 %collective-permute-done.5 = bf16[384,3200]{1,0:T(8,128)(2,1)S(1)} collective-permute-done((bf16[384,3200]{1,0:T(8,128)(2,1)}, bf16[384,3200]{1,0:T(8,128)(2,1)S(1)}, u32[]{:S(2)}, u32[]{:S(2)}) %collective-permute-start.5) | collective-permute-done | bytes 2457632 | tf_op jit(solution)/shard_map/ppermute | solution.py:635
  100.2 0.8 add_convert_fusion.1
  101.0 3.0 %collective-permute-start.7 = (bf16[8,24,3200]{2,1,0:T(8,128)(2,1)S(1)}, bf16[8,24,3200]{2,1,0:T(8,128)(2,1)S(1)}, u32[]{:S(2)}, u32[]{:S(2)}) collective-permute-start(bf16[8,24,3200]{2,1,0:T(8,128)(2,1)S(1)} %add_convert_fusion.1), channel_id=1, source_target_pairs={{0,1},{1,0},{2,3},{3,2},{4,5},{5,4},{6,7},{7,6},{8,9},{9,8},{10,11... | collective-permute-start | bytes 3686408 | tf_op jit(solution)/shard_map/ppermute | solution.py:682
  104.1 1.1 add_convert_fusion.4
  105.2 1.5 collective-permute-start.12
  106.7 1.4 copy.44
  109.2 2.7 %collective-permute-done.8 = bf16[2,6,197,384]{3,0,2,1:T(2,128)(2,1)S(1)} collective-permute-done((bf16[2,6,197,384]{3,0,2,1:T(2,128)(2,1)S(1)}, bf16[2,6,197,384]{3,0,2,1:T(2,128)(2,1)S(1)}, u32[]{:S(2)}, u32[]{:S(2)}) %collective-permute-start.8) | collective-permute-done | bytes 1815584 | tf_op jit(solution)/shard_map/ppermute | solution.py:635
  112.0 2.5 %fusion.7 = (bf16[1,6,197,384]{3,0,2,1:T(2,128)(2,1)S(1)}, bf16[1,6,197,384]{3,0,2,1:T(2,128)(2,1)S(1)}) fusion(bf16[2,6,197,384]{3,0,2,1:T(2,128)(2,1)S(1)} %collective-permute-done.8), kind=kLoop, calls=%fused_computation.41 | loop fusion | bytes 3631104 | tf_op jit(solution)/shard_map/unstack | solution.py:762
  114.8 1.9 %broadcast_select_fusion = (bf16[2,6,197,384]{3,2,1,0:T(8,128)(2,1)S(1)}, bf16[2,6,197,384]{3,2,1,0:T(8,128)(2,1)}) fusion(pred[2]{0:T(512)(128)(4,1)S(1)} %iota_compare_fusion, bf16[6,197,384]{2,1,0:T(8,128)(2,1)S(1)} %bitcast.94, bf16[6,197,384]{2,1,0:T(8,128)(2,1)S(1)} %get-tuple-element.86, bf16[6,197,384]{2,1,0:T(8,128)(2,1)S(1)} %bitcast.95, ...), kind=kLoop, calls=%fused_computation.2 | loop fusion | flops 1815552 | bytes 7262210 | tf_op jit(solution)/shard_map/jit(_where)/select_n | solution.py:761
  116.7 2.1 %collective-permute-done.7 = bf16[8,24,3200]{2,1,0:T(8,128)(2,1)S(1)} collective-permute-done((bf16[8,24,3200]{2,1,0:T(8,128)(2,1)S(1)}, bf16[8,24,3200]{2,1,0:T(8,128)(2,1)S(1)}, u32[]{:S(2)}, u32[]{:S(2)}) %collective-permute-start.7) | collective-permute-done | bytes 1228832 | tf_op jit(solution)/shard_map/ppermute | solution.py:682
  118.8 1.2 add_convert_fusion.2
  119.9 1.6 %collective-permute-start.9 = (bf16[4,24,3200]{2,1,0:T(8,128)(2,1)}, bf16[4,24,3200]{2,1,0:T(8,128)(2,1)}, u32[]{:S(2)}, u32[]{:S(2)}) collective-permute-start(bf16[4,24,3200]{2,1,0:T(8,128)(2,1)} %bitcast.28), channel_id=1, source_target_pairs={{0,4},{1,5},{2,6},{3,7},{4,0},{5,1},{6,2},{7,3},{8,12},{9,13},{10,... | collective-permute-start | bytes 1843208 | tf_op jit(solution)/shard_map/ppermute | solution.py:682
  121.5 1.9 %add_convert_fusion.9 = (bf16[4,1,1,96,384]{4,3,2,1,0:T(8,128)(2,1)S(1)}, bf16[4,96,384]{2,1,0:T(8,128)(2,1)}) fusion(bf16[4,2,1,96,384]{4,3,2,1,0:T(8,128)(2,1)} %bitcast.42, s32[]{:T(128)S(6)} %select_n.125, bf16[4,1,2,96,384]{4,3,2,1,0:T(8,128)(2,1)S(1)} %get-tuple-element.84, s32[]{:T(128)S(6)} %select_n.120), kind=kLoop, calls=%fused_computation.21 | loop fusion | flops 1179648 | bytes 1769480 | tf_op jit(solution)/shard_map/convert_element_type | solution.py:673
  123.4 2.0 %collective-permute-start.13 = (bf16[4,96,384]{2,1,0:T(8,128)(2,1)}, bf16[4,96,384]{2,1,0:T(8,128)(2,1)}, u32[]{:S(2)}, u32[]{:S(2)}) collective-permute-start(bf16[4,96,384]{2,1,0:T(8,128)(2,1)} %get-tuple-element.93), channel_id=1, source_target_pairs={{0,1},{1,0},{2,3},{3,2},{4,5},{5,4},{6,7},{7,6},{8,9},{9,8},{10,11... | collective-permute-start | bytes 884744 | tf_op jit(solution)/shard_map/ppermute | solution.py:682
  125.4 4.1 %copy.56 = bf16[2,6,197,384]{3,0,2,1:T(2,128)(2,1)} copy(bf16[2,6,197,384]{3,2,1,0:T(8,128)(2,1)} %get-tuple-element.63) | data formatting | bytes 3631104 | tf_op jit(solution)/shard_map/optimization_barrier | solution.py:771
  129.6 2.6 %copy.55 = bf16[2,6,197,384]{3,0,2,1:T(2,128)(2,1)} copy(bf16[2,6,197,384]{3,2,1,0:T(8,128)(2,1)S(1)} %get-tuple-element.64) | data formatting | bytes 3631104 | tf_op jit(solution)/shard_map/optimization_barrier | solution.py:771
  132.2 1.2 add_convert_fusion.7
  133.9 1.1 fusion.6
  135.0 3.4 %collective-permute-start.14 = (bf16[2,96,384]{2,1,0:T(8,128)(2,1)S(1)}, bf16[2,96,384]{2,1,0:T(8,128)(2,1)S(1)}, u32[]{:S(2)}, u32[]{:S(2)}) collective-permute-start(bf16[2,96,384]{2,1,0:T(8,128)(2,1)S(1)} %get-tuple-element.96), channel_id=1, source_target_pairs={{0,8},{1,9},{2,10},{3,11},{4,12},{5,13},{6,14},{7,15},{8,0},{9,1},... | collective-permute-start | bytes 442376 | tf_op jit(solution)/shard_map/ppermute | solution.py:682
  138.3 2.0 %collective-permute-done.10 = bf16[2,24,3200]{2,1,0:T(8,128)(2,1)S(1)} collective-permute-done((bf16[2,24,3200]{2,1,0:T(8,128)(2,1)S(1)}, bf16[2,24,3200]{2,1,0:T(8,128)(2,1)S(1)}, u32[]{:S(2)}, u32[]{:S(2)}) %collective-permute-start.10) | collective-permute-done | bytes 307232 | tf_op jit(solution)/shard_map/ppermute | solution.py:682
  141.1 2.2 %collective-permute-done.14 = bf16[2,96,384]{2,1,0:T(8,128)(2,1)S(1)} collective-permute-done((bf16[2,96,384]{2,1,0:T(8,128)(2,1)S(1)}, bf16[2,96,384]{2,1,0:T(8,128)(2,1)S(1)}, u32[]{:S(2)}, u32[]{:S(2)}) %collective-permute-start.14) | collective-permute-done | bytes 147488 | tf_op jit(solution)/shard_map/ppermute | solution.py:682
  144.0 3.4 %collective-permute-start.11 = (bf16[1,24,3200]{2,1,0:T(8,128)(2,1)S(1)}, bf16[1,24,3200]{2,1,0:T(8,128)(2,1)S(1)}, u32[]{:S(2)}, u32[]{:S(2)}) collective-permute-start(bf16[1,24,3200]{2,1,0:T(8,128)(2,1)S(1)} %get-tuple-element.94), channel_id=1, source_target_pairs={{0,8},{1,9},{2,10},{3,11},{4,12},{5,13},{6,14},{7,15},{8,0},{9,1},... | collective-permute-start | bytes 460808 | tf_op jit(solution)/shard_map/ppermute | solution.py:682
  147.4 0.9 collective-permute-done.15
  149.0 4.8 %collective-permute-done.11 = bf16[1,24,3200]{2,1,0:T(8,128)(2,1)S(1)} collective-permute-done((bf16[1,24,3200]{2,1,0:T(8,128)(2,1)S(1)}, bf16[1,24,3200]{2,1,0:T(8,128)(2,1)S(1)}, u32[]{:S(2)}, u32[]{:S(2)}) %collective-permute-start.11) | collective-permute-done | bytes 153632 | tf_op jit(solution)/shard_map/ppermute | solution.py:682
  154.4 1.8 %shard_map.256 = (f32[1,24,1536]{2,1,0:T(8,128)}, f32[1,24,1152]{2,1,0:T(8,128)}, f32[1,24,384]{2,1,0:T(8,128)}, f32[1,48]{1,0:T(1,128)}, f32[1,96]{1,0:T(1,128)...) custom-call(bf16[24,3200]{1,0:T(8,128)(2,1)} %get-tuple-element.95.o, ...), custom_call_target="tpu_custom_call" | custom-call | tf_op jit(solution)/shard_map/pallas_call | solution.py:717
  (47 shorter events, 6.9 us)
Async XLA Ops:
  0.6 7.7 %collective-permute-start.3 = (bf16[1,384,1536]{2,1,0:T(8,128)(2,1)}, bf16[1,384,1536]{2,1,0:T(8,128)(2,1)S(1)}, u32[]{:S(2)}, u32[]{:S(2)}) collective-permute-start(bf16[1,384,1536]{2,1,0:T(8,128)(2,1)} %refs_8_.1), channel_id=1, source_target_pairs={{0,16},{16,0},{1,17},{17,1},{2,18},{18,2},{3,19},{19,3},{4,20},{20... | collective-permute-start | bytes 3538952 | tf_op jit(solution)/shard_map/ppermute | solution.py:635
  1.2 8.1 %collective-permute-start.4 = (bf16[1,1536,384]{2,1,0:T(8,128)(2,1)}, bf16[1,1536,384]{2,1,0:T(8,128)(2,1)}, u32[]{:S(2)}, u32[]{:S(2)}) collective-permute-start(bf16[1,1536,384]{2,1,0:T(8,128)(2,1)} %refs_9_.1), channel_id=1, source_target_pairs={{0,16},{16,0},{1,17},{17,1},{2,18},{18,2},{3,19},{19,3},{4,20},{20... | collective-permute-start | bytes 3538952 | tf_op jit(solution)/shard_map/ppermute | solution.py:635
  1.2 7.0 %collective-permute-start.1 = (bf16[1,384,1152]{2,1,0:T(8,128)(2,1)}, bf16[1,384,1152]{2,1,0:T(8,128)(2,1)S(1)}, u32[]{:S(2)}, u32[]{:S(2)}) collective-permute-start(bf16[1,384,1152]{2,1,0:T(8,128)(2,1)} %refs_6_.3), channel_id=1, source_target_pairs={{0,16},{16,0},{1,17},{17,1},{2,18},{18,2},{3,19},{19,3},{4,20},{20... | collective-permute-start | bytes 2654216 | tf_op jit(solution)/shard_map/ppermute | solution.py:635
  1.7 6.6 %collective-permute-start.2 = (bf16[1,384,384]{2,1,0:T(8,128)(2,1)}, bf16[1,384,384]{2,1,0:T(8,128)(2,1)S(1)}, u32[]{:S(2)}, u32[]{:S(2)}) collective-permute-start(bf16[1,384,384]{2,1,0:T(8,128)(2,1)} %refs_7_.3), channel_id=1, source_target_pairs={{0,16},{16,0},{1,17},{17,1},{2,18},{18,2},{3,19},{19,3},{4,20},{20... | collective-permute-start | bytes 884744 | tf_op jit(solution)/shard_map/ppermute | solution.py:635
  3.2 5.1 %collective-permute-start = (f32[1,4992]{1,0:T(1,128)}, f32[1,4992]{1,0:T(1,128)S(1)}, u32[]{:S(2)}, u32[]{:S(2)}) collective-permute-start(f32[1,4992]{1,0:T(1,128)} %shard_map.254.refs_4_), channel_id=1, source_target_pairs={{0,16},{16,0},{1,17},{17,1},{2,18},{18,2},{3,19},{19,3},{4,20},{20... | collective-permute-start | bytes 59912 | tf_op jit(solution)/shard_map/ppermute | solution.py:635
  3.6 3.2 %copy-start.2 = (bf16[2,6,197,384]{3,0,2,1:T(2,128)(2,1)S(1)}, bf16[2,6,197,384]{3,0,2,1:T(2,128)(2,1)}, u32[]{:S(2)}) copy-start(bf16[2,6,197,384]{3,0,2,1:T(2,128)(2,1)} %param.17) | copy-start | bytes 5446660
  8.3 1.0 copy-start.9
  8.3 1.0 copy-start.8
  8.3 1.0 copy-start.7
  9.3 1.0 copy-start.6
  94.9 5.0 %collective-permute-start.5 = (bf16[384,3200]{1,0:T(8,128)(2,1)}, bf16[384,3200]{1,0:T(8,128)(2,1)S(1)}, u32[]{:S(2)}, u32[]{:S(2)}) collective-permute-start(bf16[384,3200]{1,0:T(8,128)(2,1)} %get-tuple-element.50), channel_id=1, source_target_pairs={{0,16},{16,0},{1,17},{17,1},{2,18},{18,2},{3,19},{19,3},{4,20},{20... | collective-permute-start | bytes 7372808 | tf_op jit(solution)/shard_map/ppermute | solution.py:635
  95.0 4.8 %copy-start.5 = (bf16[1536,384]{1,0:T(8,128)(2,1)S(1)}, bf16[1536,384]{1,0:T(8,128)(2,1)}, u32[]{:S(2)}) copy-start(bf16[1536,384]{1,0:T(8,128)(2,1)} %get-tuple-element.53) | copy-start | bytes 3538948
  95.0 5.0 %copy-start = (bf16[384,3200]{1,0:T(8,128)(2,1)S(1)}, bf16[384,3200]{1,0:T(8,128)(2,1)}, u32[]{:S(2)}) copy-start(bf16[384,3200]{1,0:T(8,128)(2,1)} %get-tuple-element.56) | copy-start | bytes 7372804
  99.8 4.2 %collective-permute-start.6 = (bf16[1536,384]{1,0:T(8,128)(2,1)S(1)}, bf16[1536,384]{1,0:T(8,128)(2,1)S(1)}, u32[]{:S(2)}, u32[]{:S(2)}) collective-permute-start(bf16[1536,384]{1,0:T(8,128)(2,1)S(1)} %copy-done.5), channel_id=1, source_target_pairs={{0,16},{16,0},{1,17},{17,1},{2,18},{18,2},{3,19},{19,3},{4,20},{20... | collective-permute-start | bytes 3538952 | tf_op jit(solution)/shard_map/ppermute | solution.py:635
  100.2 3.8 %copy-start.3 = (bf16[1536,384]{1,0:T(8,128)(2,1)S(1)}, bf16[1536,384]{1,0:T(8,128)(2,1)}, u32[]{:S(2)}) copy-start(bf16[1536,384]{1,0:T(8,128)(2,1)} %get-tuple-element.54) | copy-start | bytes 3538948
  101.0 17.7 %collective-permute-start.7 = (bf16[8,24,3200]{2,1,0:T(8,128)(2,1)S(1)}, bf16[8,24,3200]{2,1,0:T(8,128)(2,1)S(1)}, u32[]{:S(2)}, u32[]{:S(2)}) collective-permute-start(bf16[8,24,3200]{2,1,0:T(8,128)(2,1)S(1)} %add_convert_fusion.1), channel_id=1, source_target_pairs={{0,1},{1,0},{2,3},{3,2},{4,5},{5,4},{6,7},{7,6},{8,9},{9,8},{10,11... | collective-permute-start | bytes 3686408 | tf_op jit(solution)/shard_map/ppermute | solution.py:682
  104.1 2.7 %copy-start.1 = (bf16[2,6,197,384]{3,2,1,0:T(8,128)(2,1)S(1)}, bf16[2,6,197,384]{3,2,1,0:T(8,128)(2,1)}, u32[]{:S(2)}) copy-start(bf16[2,6,197,384]{3,2,1,0:T(8,128)(2,1)} %get-tuple-element.60) | copy-start | bytes 5446660
  105.2 16.3 %collective-permute-start.12 = (bf16[8,96,384]{2,1,0:T(8,128)(2,1)}, bf16[8,96,384]{2,1,0:T(8,128)(2,1)}, u32[]{:S(2)}, u32[]{:S(2)}) collective-permute-start(bf16[8,96,384]{2,1,0:T(8,128)(2,1)} %bitcast.12), channel_id=1, source_target_pairs={{0,2},{1,3},{2,0},{3,1},{4,6},{5,7},{6,4},{7,5},{8,10},{9,11},{10,... | collective-permute-start | bytes 1769480 | tf_op jit(solution)/shard_map/ppermute | solution.py:682
  108.1 3.8 %collective-permute-start.8 = (bf16[2,6,197,384]{3,0,2,1:T(2,128)(2,1)S(1)}, bf16[2,6,197,384]{3,0,2,1:T(2,128)(2,1)S(1)}, u32[]{:S(2)}, u32[]{:S(2)}) collective-permute-start(bf16[2,6,197,384]{3,0,2,1:T(2,128)(2,1)S(1)} %copy.44), channel_id=1, source_target_pairs={{0,16},{16,0},{1,17},{17,1},{2,18},{18,2},{3,19},{19,3},{4,20},{20... | collective-permute-start | bytes 5446664 | tf_op jit(solution)/shard_map/ppermute | solution.py:635
  119.9 12.3 %collective-permute-start.9 = (bf16[4,24,3200]{2,1,0:T(8,128)(2,1)}, bf16[4,24,3200]{2,1,0:T(8,128)(2,1)}, u32[]{:S(2)}, u32[]{:S(2)}) collective-permute-start(bf16[4,24,3200]{2,1,0:T(8,128)(2,1)} %bitcast.28), channel_id=1, source_target_pairs={{0,4},{1,5},{2,6},{3,7},{4,0},{5,1},{6,2},{7,3},{8,12},{9,13},{10,... | collective-permute-start | bytes 1843208 | tf_op jit(solution)/shard_map/ppermute | solution.py:682
  123.4 10.5 %collective-permute-start.13 = (bf16[4,96,384]{2,1,0:T(8,128)(2,1)}, bf16[4,96,384]{2,1,0:T(8,128)(2,1)}, u32[]{:S(2)}, u32[]{:S(2)}) collective-permute-start(bf16[4,96,384]{2,1,0:T(8,128)(2,1)} %get-tuple-element.93), channel_id=1, source_target_pairs={{0,1},{1,0},{2,3},{3,2},{4,5},{5,4},{6,7},{7,6},{8,9},{9,8},{10,11... | collective-permute-start | bytes 884744 | tf_op jit(solution)/shard_map/ppermute | solution.py:682
  133.4 6.9 %collective-permute-start.10 = (bf16[2,24,3200]{2,1,0:T(8,128)(2,1)S(1)}, bf16[2,24,3200]{2,1,0:T(8,128)(2,1)S(1)}, u32[]{:S(2)}, u32[]{:S(2)}) collective-permute-start(bf16[2,24,3200]{2,1,0:T(8,128)(2,1)S(1)} %get-tuple-element.91), channel_id=1, source_target_pairs={{0,2},{1,3},{2,0},{3,1},{4,6},{5,7},{6,4},{7,5},{8,10},{9,11},{10,... | collective-permute-start | bytes 921608 | tf_op jit(solution)/shard_map/ppermute | solution.py:682
  135.0 8.2 %collective-permute-start.14 = (bf16[2,96,384]{2,1,0:T(8,128)(2,1)S(1)}, bf16[2,96,384]{2,1,0:T(8,128)(2,1)S(1)}, u32[]{:S(2)}, u32[]{:S(2)}) collective-permute-start(bf16[2,96,384]{2,1,0:T(8,128)(2,1)S(1)} %get-tuple-element.96), channel_id=1, source_target_pairs={{0,8},{1,9},{2,10},{3,11},{4,12},{5,13},{6,14},{7,15},{8,0},{9,1},... | collective-permute-start | bytes 442376 | tf_op jit(solution)/shard_map/ppermute | solution.py:682
  143.2 5.0 %collective-permute-start.15 = (bf16[1,96,384]{2,1,0:T(8,128)(2,1)S(1)}, bf16[1,96,384]{2,1,0:T(8,128)(2,1)S(1)}, u32[]{:S(2)}, u32[]{:S(2)}) collective-permute-start(bf16[1,96,384]{2,1,0:T(8,128)(2,1)S(1)} %add_convert_fusion.12), channel_id=1, source_target_pairs={{0,4},{1,5},{2,6},{3,7},{4,0},{5,1},{6,2},{7,3},{8,12},{9,13},{10,... | collective-permute-start | bytes 221192 | tf_op jit(solution)/shard_map/ppermute | solution.py:682
  144.0 9.7 %collective-permute-start.11 = (bf16[1,24,3200]{2,1,0:T(8,128)(2,1)S(1)}, bf16[1,24,3200]{2,1,0:T(8,128)(2,1)S(1)}, u32[]{:S(2)}, u32[]{:S(2)}) collective-permute-start(bf16[1,24,3200]{2,1,0:T(8,128)(2,1)S(1)} %get-tuple-element.94), channel_id=1, source_target_pairs={{0,8},{1,9},{2,10},{3,11},{4,12},{5,13},{6,14},{7,15},{8,0},{9,1},... | collective-permute-start | bytes 460808 | tf_op jit(solution)/shard_map/ppermute | solution.py:682
  153.7 0.7 copy-start.4
